TPU v7x, 128 devices: a whole 4x4x4 slice. The times are simulated.
128 devices in a mesh: shot: 4 (over y_lo, core), sub: 32 (over x, y_hi, z).
Axes of the slice: x: 4, y: 4 (y_hi: 2, y_lo: 2; y = y_hi * 2 + y_lo), z: 4, core: 2. Of those that a mesh axis runs over, the one named last changes fastest.
Arguments:
- velocity: float32 [512, 256, 256], P('sub'), may hold values from 1.5 to 4.5
- adjoint_now: float32 [4, 512, 256, 256], P('shot', 'sub'), may hold values from -1.5 to 1.5
- adjoint_prev: float32 [4, 512, 256, 256], P('shot', 'sub'), may hold values from -1.5 to 1.5
- forward_accel: bfloat16 [4, 4, 512, 256, 256], P('shot', None, 'sub'), may hold values from -6 to 6
- traces: float32 [4, 4, 32768], P('shot', None, 'sub'), may hold values from -120 to 120
- receiver_sub: int32 [4, 32768, 1], P('shot', 'sub'), may hold values from 0 to 31; in each aligned block of 1024 rows (0 to 1023, 1024 to 2047, ..., all dimensions but the last counted through in order) at most 64 rows name the same one
- receiver_cell: int32 [4, 32768], P('shot', 'sub'), may hold values from 0 to 1048575
Outputs:
- adjoint_out: float32 [4, 512, 256, 256], P('shot', 'sub')
- gradient: float32 [512, 256, 256], P('sub', 'shot')
Inputs may be any that keep to these rules, and one draw needn't show every extreme that they name: `receiver_sub`: among the 1024 receivers of one device's aligned block of a shot, at most 64 lie in one slab, and exactly 64 in some slab.
All inputs are finite; a program needn't handle non-finite values.
Results may differ from a plain program's by a relative error of at most 0.0003.
Values sent between devices are 32-bit elements; how exact they have to be, the bound alone decides.
No kernel may reach another device: no remote copies, remote signals or barrier semaphores. Data moves between devices by JAX's collectives and lax.ppermute only.
A program may use at most 128 MiB of HBM per device.

v0:
```python
import jax
import jax.numpy as jnp
from jax import lax
from jax.sharding import PartitionSpec as P

PML = 16
STEPS = 4


COEFFS = (-205.0 / 72.0, 8.0 / 5.0, -1.0 / 5.0, 8.0 / 315.0, -1.0 / 560.0)
COURANT = 0.09
DAMP_MAX = 0.3


def with_halo(cells, sides, width):
    for axis, dim in sides:
        count = lax.axis_size(axis)
        ends = count - 1
        head = lax.slice_in_dim(cells, 0, width, axis=dim)
        tail = lax.slice_in_dim(cells, cells.shape[dim] - width, cells.shape[dim], axis=dim)
        cells = jnp.concatenate(
            [
                lax.ppermute(tail, axis, [(i, (i + 1) % count) for i in range(ends)]),
                cells,
                lax.ppermute(head, axis, [((i + 1) % count, i) for i in range(ends)]),
            ],
            axis=dim,
        )
    return cells


def profile(index, count):
    depth = jnp.maximum(jnp.maximum(PML - index, index - (count - 1 - PML)), 0.0) / PML
    return depth * depth


def laplace(padded, field):
    size_x, size_y, size_z = field.shape
    total = 3.0 * COEFFS[0] * field
    for k in range(1, 5):
        total = total + COEFFS[k] * (
            padded[4 + k : 4 + k + size_x, 4 : 4 + size_y, 4 : 4 + size_z]
            + padded[4 - k : 4 - k + size_x, 4 : 4 + size_y, 4 : 4 + size_z]
            + padded[4 : 4 + size_x, 4 + k : 4 + k + size_y, 4 : 4 + size_z]
            + padded[4 : 4 + size_x, 4 - k : 4 - k + size_y, 4 : 4 + size_z]
            + padded[4 : 4 + size_x, 4 : 4 + size_y, 4 + k : 4 + k + size_z]
            + padded[4 : 4 + size_x, 4 : 4 + size_y, 4 - k : 4 - k + size_z]
        )
    return total


def shards(velocity, adjoint_now, adjoint_prev, forward_accel, traces, receiver_sub, receiver_cell):
    slab_x, size_y, size_z = velocity.shape
    slabs = lax.axis_size("sub")
    listed = receiver_sub.shape[1]
    slot_count = 2 * listed // slabs
    total_x = slab_x * slabs
    slab_cells = slab_x * size_y * size_z
    start_x = (lax.axis_index("sub") * slab_x).astype(jnp.float32)
    coord_x = profile(start_x + jnp.arange(slab_x, dtype=jnp.float32), total_x)
    coord_y = profile(jnp.arange(size_y, dtype=jnp.float32), size_y)
    coord_z = profile(jnp.arange(size_z, dtype=jnp.float32), size_z)
    damp = DAMP_MAX * (coord_x[:, None, None] + coord_y[None, :, None] + coord_z[None, None, :])
    speed_sq = (COURANT * velocity) ** 2
    weight = 2.0 / (velocity * velocity * velocity)
    target = receiver_sub[0, :, 0]
    onehot = (target[:, None] == jnp.arange(slabs, dtype=jnp.int32)[None, :]).astype(jnp.int32)
    before = jnp.cumsum(onehot, axis=0) - onehot
    place = target * slot_count + jnp.sum(before * onehot, axis=1)
    value_buffer = (
        jnp.zeros((STEPS, slabs * slot_count), jnp.float32)
        .at[:, place]
        .set(traces[0])
        .reshape(STEPS, slabs, slot_count)
    )
    cell_buffer = (
        jnp.full((slabs * slot_count,), slab_cells, jnp.int32)
        .at[place]
        .set(receiver_cell[0])
        .reshape(1, slabs, slot_count)
    )
    arrived_cells = lax.all_to_all(cell_buffer, "sub", split_axis=1, concat_axis=1, tiled=True)
    arrived_cells = arrived_cells.reshape(slabs * slot_count)
    current = adjoint_now[0]
    previous = adjoint_prev[0]
    partial_value = jnp.zeros_like(velocity)
    for step in range(STEPS):
        step_values = lax.all_to_all(
            value_buffer[step : step + 1], "sub", split_axis=1, concat_axis=1, tiled=True
        ).reshape(slabs * slot_count)
        source = (
            jnp.zeros((slab_cells,), jnp.float32)
            .at[arrived_cells]
            .add(step_values, mode="drop")
            .reshape(slab_x, size_y, size_z)
        )
        extended = with_halo(current, (("sub", 0),), 4)
        padded = jnp.pad(extended, ((0, 0), (4, 4), (4, 4)))
        after = (
            2.0 * current - (1.0 - damp) * previous + speed_sq * (laplace(padded, current) + source)
        ) / (1.0 + damp)
        term = weight * after * forward_accel[0, step].astype(jnp.float32)
        partial_value = partial_value + term
        previous = current
        current = after
    share = lax.psum_scatter(partial_value, "shot", scatter_dimension=1, tiled=True)
    return (current[None], share)


def solution(mesh):
    in_specs = (
        P("sub", None, None),
        P("shot", "sub", None, None),
        P("shot", "sub", None, None),
        P("shot", None, "sub", None, None),
        P("shot", None, "sub"),
        P("shot", "sub", None),
        P("shot", "sub"),
    )
    out_specs = (P("shot", "sub", None, None), P("sub", "shot", None))
    return jax.shard_map(shards, mesh=mesh, in_specs=in_specs, out_specs=out_specs, check_vma=False)
```

profile of v0, /device:TPU:2, one launch (start us, length us, event | category | flops | bytes accessed | tf_op | source)
XLA Modules:
  0.0 485.2 jit_solution(7967749211216374963)
XLA Ops:
  7.9 9.0 %reduce-window.6 = s32[32,8,128]{2,1,0:T(8,128)S(1)} reduce-window(s32[32,8,128]{2,1,0:T(8,128)S(1)} %fusion.159, s32[]{:T(128)} %constant.54.clone.1), window={size=1x1x128 pad=0_0x0_0x127_0}, to_apply=%region_0.0 | reduce-window | flops 4161536 | bytes 262148 | tf_op jit(solution)/shard_map/reduce-window
  23.9 11.1 %all-to-all-start = ((s32[1,32,64]{2,0,1:T(1,128)}), s32[1,32,64]{2,0,1:T(1,128)S(1)}, u32[]{:S(2)}, u32[]{:S(2)}) async-start(s32[1,32,64]{2,0,1:T(1,128)} %reshape.185), calls=%async_computation | async-start | bytes 32768 | tf_op jit(solution)/shard_map/all_to_all | solution.py:82
  38.1 7.0 %collective-permute-start = (f32[4,256,256]{2,1,0:T(8,128)}, f32[4,256,256]{2,1,0:T(8,128)S(1)}, u32[]{:S(2)}, u32[]{:S(2)}) collective-permute-start(f32[4,256,256]{2,1,0:T(8,128)} %get-tuple-element.14), channel_id=1, source_target_pairs={{1,0},{2,1},{3,2},{4,3},{5,4},{6,5},{7,6},{8,7},{9,8},{10,9},{11,1... | collective-permute-start | bytes 3145736 | tf_op jit(solution)/shard_map/ppermute | solution.py:25
  54.5 11.0 %all-to-all-start.1 = ((f32[1,32,64]{2,0,1:T(1,128)}), f32[1,32,64]{2,0,1:T(1,128)S(1)}, u32[]{:S(2)}, u32[]{:S(2)}) async-start(f32[1,32,64]{2,0,1:T(1,128)} %bitcast.15), calls=%async_computation.1 | async-start | bytes 32768 | tf_op jit(solution)/shard_map/all_to_all | solution.py:88
  67.0 9.0 %all-to-all-done.1 = f32[1,32,64]{2,0,1:T(1,128)S(1)} async-done(((f32[1,32,64]{2,0,1:T(1,128)}), f32[1,32,64]{2,0,1:T(1,128)S(1)}, u32[]{:S(2)}, u32[]{:S(2)}) %all-to-all-start.1) | async-done | bytes 8224 | tf_op jit(solution)/shard_map/all_to_all | solution.py:88
  77.4 13.9 %scatter_custom_fusion.2 = f32[1048576]{0:T(1024)} fusion(s32[2048]{0:T(1024)S(1)} %bitcast.79, f32[2048]{0:T(1024)S(1)} %reshape.219, f32[]{:T(128)} %constant.26.clone.1), kind=kCustom, calls=%fused_computation.250 | custom fusion | flops 2048 | bytes 4194308 | tf_op jit(solution)/shard_map/scatter-add | solution.py:94
  98.4 6.5 %select_maximum_fusion.6 = f32[24,264,264]{2,1,0:T(8,128)S(1)} fusion(f32[4,256,256]{2,1,0:T(8,128)} %copy-done.1, f32[16,256,256]{2,1,0:T(8,128)} %bitcast.67, f32[4,256,256]{2,1,0:T(8,128)} %copy-done.2), kind=kLoop, calls=%fused_computation.16 | loop fusion | flops 25090560 | bytes 12982272 | tf_op jit(solution)/shard_map/concatenate | solution.py:21
  105.0 25.4 %fusion.111 = f32[16,256,256]{2,1,0:T(8,128)} fusion(f32[16,256,256]{2,1,0:T(8,128)} %reshape.188, f32[16,256,256]{2,1,0:T(8,128)} %bitcast.68, f32[4,256,256]{2,1,0:T(8,128)} %copy-done.2, f32[4,256,256]{2,1,0:T(8,128)} %copy-done.1, f32[24,264,264]{2,1,0:T(8,128)S(1)} %select_maximum_fusion.6, f32[1,16,256,256]{3,2,1,0:T(8,128)} %param.9, ...), kind=kLoop, calls=%fused_computation.178 | loop fusion | flops 52428800 | bytes 90194944 | tf_op jit(solution)/shard_map/div | solution.py:99
  139.0 27.2 %all_to_all.25 = f32[1,32,64]{2,0,1:T(1,128)S(1)} all-to-all(f32[1,32,64]{2,0,1:T(1,128)S(1)} %bitcast.71), channel_id=1, replica_groups=mesh['shot'=4,'sub'=32] {'sub'}, dimensions={1} | all-to-all | bytes 16384 | tf_op jit(solution)/shard_map/all_to_all | solution.py:88
  167.1 13.5 %scatter_custom_fusion.3 = f32[1048576]{0:T(1024)} fusion(s32[2048]{0:T(1024)S(1)} %bitcast.80, f32[2048]{0:T(1024)S(1)} %reshape.227, f32[]{:T(128)} %constant.26.clone.1), kind=kCustom, calls=%fused_computation.248 | custom fusion | flops 2048 | bytes 4194308 | tf_op jit(solution)/shard_map/scatter-add | solution.py:94
  180.6 5.3 %reshape.190 = f32[16,256,256]{2,1,0:T(8,128)} reshape(f32[1048576]{0:T(1024)} %scatter_custom_fusion.3) | data formatting | bytes 8388608 | tf_op jit(solution)/shard_map/reshape | solution.py:95
  186.8 6.5 %select_maximum_fusion.4 = f32[24,264,264]{2,1,0:T(8,128)S(1)} fusion(f32[4,256,256]{2,1,0:T(8,128)} %copy-done.3, f32[16,256,256]{2,1,0:T(8,128)} %fusion.111, f32[4,256,256]{2,1,0:T(8,128)} %collective-permute-done.3), kind=kLoop, calls=%fused_computation.14 | loop fusion | flops 25090560 | bytes 12982272 | tf_op jit(solution)/shard_map/concatenate | solution.py:21
  193.4 25.8 %fusion.79 = f32[16,256,256]{2,1,0:T(8,128)} fusion(f32[16,256,256]{2,1,0:T(8,128)} %reshape.190, f32[16,256,256]{2,1,0:T(8,128)} %fusion.111, f32[4,256,256]{2,1,0:T(8,128)} %collective-permute-done.3, f32[4,256,256]{2,1,0:T(8,128)} %copy-done.3, f32[24,264,264]{2,1,0:T(8,128)S(1)} %select_maximum_fusion.4, f32[16,256,256]{2,1,0:T(8,128)} %param.7, ...), kind=kLoop, calls=%fused_computation.146 | loop fusion | flops 52428800 | bytes 90194944 | tf_op jit(solution)/shard_map/div | solution.py:99
  227.0 25.8 %all_to_all.26 = f32[1,32,64]{2,0,1:T(1,128)S(1)} all-to-all(f32[1,32,64]{2,0,1:T(1,128)S(1)} %bitcast.72), channel_id=1, replica_groups=mesh['shot'=4,'sub'=32] {'sub'}, dimensions={1} | all-to-all | bytes 16384 | tf_op jit(solution)/shard_map/all_to_all | solution.py:88
  253.6 13.5 %scatter_custom_fusion.4 = f32[1048576]{0:T(1024)} fusion(s32[2048]{0:T(1024)S(1)} %bitcast.81, f32[2048]{0:T(1024)S(1)} %reshape.235, f32[]{:T(128)} %constant.26.clone.1), kind=kCustom, calls=%fused_computation.246 | custom fusion | flops 2048 | bytes 4194308 | tf_op jit(solution)/shard_map/scatter-add | solution.py:94
  273.3 6.5 %select_maximum_fusion.2 = f32[24,264,264]{2,1,0:T(8,128)S(1)} fusion(f32[4,256,256]{2,1,0:T(8,128)} %copy-done.4, f32[16,256,256]{2,1,0:T(8,128)} %fusion.79, f32[4,256,256]{2,1,0:T(8,128)} %collective-permute-done.5), kind=kLoop, calls=%fused_computation.12 | loop fusion | flops 25090560 | bytes 12982272 | tf_op jit(solution)/shard_map/concatenate | solution.py:21
  279.8 26.6 %fusion.47 = f32[16,256,256]{2,1,0:T(8,128)} fusion(f32[16,256,256]{2,1,0:T(8,128)} %reshape.192, f32[16,256,256]{2,1,0:T(8,128)} %fusion.79, f32[4,256,256]{2,1,0:T(8,128)} %collective-permute-done.5, f32[4,256,256]{2,1,0:T(8,128)} %copy-done.4, f32[24,264,264]{2,1,0:T(8,128)S(1)} %select_maximum_fusion.2, f32[16,256,256]{2,1,0:T(8,128)} %fusion.111, ...), kind=kLoop, calls=%fused_computation.114 | loop fusion | flops 52428800 | bytes 90194944 | tf_op jit(solution)/shard_map/div | solution.py:99
  312.1 7.7 %collective-permute-start.6 = (f32[4,256,256]{2,1,0:T(8,128)}, f32[4,256,256]{2,1,0:T(8,128)}, u32[]{:S(2)}, u32[]{:S(2)}) collective-permute-start(f32[4,256,256]{2,1,0:T(8,128)} %get-tuple-element.9), channel_id=1, source_target_pairs={{1,0},{2,1},{3,2},{4,3},{5,4},{6,5},{7,6},{8,7},{9,8},{10,9},{11,1... | collective-permute-start | bytes 3145736 | tf_op jit(solution)/shard_map/ppermute | solution.py:25
  319.8 19.4 %all_to_all.27 = f32[1,32,64]{2,0,1:T(1,128)S(1)} all-to-all(f32[1,32,64]{2,0,1:T(1,128)S(1)} %bitcast.73), channel_id=1, replica_groups=mesh['shot'=4,'sub'=32] {'sub'}, dimensions={1} | all-to-all | bytes 16384 | tf_op jit(solution)/shard_map/all_to_all | solution.py:88
  340.0 13.7 %scatter_custom_fusion.5 = f32[1048576]{0:T(1024)} fusion(s32[2048]{0:T(1024)S(1)} %bitcast.82, f32[2048]{0:T(1024)S(1)} %reshape.243, f32[]{:T(128)} %constant.26.clone.1), kind=kCustom, calls=%fused_computation.244 | custom fusion | flops 2048 | bytes 4194308 | tf_op jit(solution)/shard_map/scatter-add | solution.py:94
  353.7 5.3 %reshape.194 = f32[16,256,256]{2,1,0:T(8,128)} reshape(f32[1048576]{0:T(1024)} %scatter_custom_fusion.5) | data formatting | bytes 8388608 | tf_op jit(solution)/shard_map/reshape | solution.py:95
  359.0 9.9 %select_maximum_fusion = f32[24,264,264]{2,1,0:T(8,128)} fusion(f32[4,256,256]{2,1,0:T(8,128)} %collective-permute-done.6, f32[16,256,256]{2,1,0:T(8,128)} %fusion.47, f32[4,256,256]{2,1,0:T(8,128)} %collective-permute-done.7), kind=kLoop, calls=%fused_computation.10 | loop fusion | flops 25090560 | bytes 12982272 | tf_op jit(solution)/shard_map/concatenate | solution.py:21
  368.9 62.7 %fusion.140 = (f32[16,256,256]{2,1,0:T(8,128)}, f32[16,256,256]{2,1,0:T(8,128)}) fusion(f32[16,256,256]{2,1,0:T(8,128)} %fusion.47, f32[16,256,256]{2,1,0:T(8,128)} %fusion.79, f32[16,256,256]{2,1,0:T(8,128)S(1)} %copy-done, f32[16,256,256]{2,1,0:T(8,128)} %param.7, bf16[1,4,16,256,256]{4,3,2,1,0:T(8,128)(2,1)} %param.10, f32[16,256,256]{2,1,0:T(8,128)} %reshape.194, ...), kind=kLoop, calls=%fused_computation.232 | loop fusion | flops 71303168 | bytes 106972160 | tf_op jit(solution)/shard_map/add | solution.py:103
  431.6 46.5 %reduce-scatter.2.cloned.1.call-done = f32[16,64,256]{2,1,0:T(8,128)} async-done(((f32[16,256,256]{2,1,0:T(8,128)}), f32[16,64,256]{2,1,0:T(8,128)}) %reduce-scatter.2.cloned.1.call-update) | async-done | bytes 1048592 | tf_op jit(solution)/shard_map/reduce_scatter | solution.py:106
  (69 shorter events, 62.0 us)
Async XLA Ops:
  7.2 39.8 %copy-start.5 = (f32[1,4,1024]{2,1,0:T(4,128)S(1)}, f32[1,4,1024]{2,1,0:T(4,128)}, u32[]{:S(2)}) copy-start(f32[1,4,1024]{2,1,0:T(4,128)} %param.11) | copy-start | bytes 49156
  23.9 30.5 %all-to-all-start = ((s32[1,32,64]{2,0,1:T(1,128)}), s32[1,32,64]{2,0,1:T(1,128)S(1)}, u32[]{:S(2)}, u32[]{:S(2)}) async-start(s32[1,32,64]{2,0,1:T(1,128)} %reshape.185), calls=%async_computation | async-start | bytes 32768 | tf_op jit(solution)/shard_map/all_to_all | solution.py:82
  38.1 58.4 %collective-permute-start = (f32[4,256,256]{2,1,0:T(8,128)}, f32[4,256,256]{2,1,0:T(8,128)S(1)}, u32[]{:S(2)}, u32[]{:S(2)}) collective-permute-start(f32[4,256,256]{2,1,0:T(8,128)} %get-tuple-element.14), channel_id=1, source_target_pairs={{1,0},{2,1},{3,2},{4,3},{5,4},{6,5},{7,6},{8,7},{9,8},{10,9},{11,1... | collective-permute-start | bytes 3145736 | tf_op jit(solution)/shard_map/ppermute | solution.py:25
  45.0 51.5 %collective-permute-start.1 = (f32[4,256,256]{2,1,0:T(8,128)}, f32[4,256,256]{2,1,0:T(8,128)S(1)}, u32[]{:S(2)}, u32[]{:S(2)}) collective-permute-start(f32[4,256,256]{2,1,0:T(8,128)} %get-tuple-element.15), channel_id=1, source_target_pairs={{0,1},{1,2},{2,3},{3,4},{4,5},{5,6},{6,7},{7,8},{8,9},{9,10},{10,1... | collective-permute-start | bytes 3145736 | tf_op jit(solution)/shard_map/ppermute | solution.py:23
  54.5 21.5 %all-to-all-start.1 = ((f32[1,32,64]{2,0,1:T(1,128)}), f32[1,32,64]{2,0,1:T(1,128)S(1)}, u32[]{:S(2)}, u32[]{:S(2)}) async-start(f32[1,32,64]{2,0,1:T(1,128)} %bitcast.15), calls=%async_computation.1 | async-start | bytes 32768 | tf_op jit(solution)/shard_map/all_to_all | solution.py:88
  65.4 412.7 %reduce-scatter.2.cloned.1.call-start = ((), (), s32[]{:S(2)}) async-start(), calls=%async_computation.6 | async-start | bytes 5242880 | tf_op jit(solution)/shard_map/reduce_scatter | solution.py:106
  96.5 1.0 copy-start.1
  97.5 1.0 copy-start.2
  132.1 53.7 %collective-permute-start.2 = (f32[4,256,256]{2,1,0:T(8,128)S(1)}, f32[4,256,256]{2,1,0:T(8,128)S(1)}, u32[]{:S(2)}, u32[]{:S(2)}) collective-permute-start(f32[4,256,256]{2,1,0:T(8,128)S(1)} %get-tuple-element.12), channel_id=1, source_target_pairs={{1,0},{2,1},{3,2},{4,3},{5,4},{6,5},{7,6},{8,7},{9,8},{10,9},{11,1... | collective-permute-start | bytes 3145736 | tf_op jit(solution)/shard_map/ppermute | solution.py:25
  137.0 49.8 %collective-permute-start.3 = (f32[4,256,256]{2,1,0:T(8,128)S(1)}, f32[4,256,256]{2,1,0:T(8,128)}, u32[]{:S(2)}, u32[]{:S(2)}) collective-permute-start(f32[4,256,256]{2,1,0:T(8,128)S(1)} %get-tuple-element.13), channel_id=1, source_target_pairs={{0,1},{1,2},{2,3},{3,4},{4,5},{5,6},{6,7},{7,8},{8,9},{9,10},{10,1... | collective-permute-start | bytes 3145736 | tf_op jit(solution)/shard_map/ppermute | solution.py:23
  185.9 1.0 copy-start.3
  220.9 51.4 %collective-permute-start.4 = (f32[4,256,256]{2,1,0:T(8,128)S(1)}, f32[4,256,256]{2,1,0:T(8,128)S(1)}, u32[]{:S(2)}, u32[]{:S(2)}) collective-permute-start(f32[4,256,256]{2,1,0:T(8,128)S(1)} %get-tuple-element.10), channel_id=1, source_target_pairs={{1,0},{2,1},{3,2},{4,3},{5,4},{6,5},{7,6},{8,7},{9,8},{10,9},{11,1... | collective-permute-start | bytes 3145736 | tf_op jit(solution)/shard_map/ppermute | solution.py:25
  224.8 48.5 %collective-permute-start.5 = (f32[4,256,256]{2,1,0:T(8,128)S(1)}, f32[4,256,256]{2,1,0:T(8,128)}, u32[]{:S(2)}, u32[]{:S(2)}) collective-permute-start(f32[4,256,256]{2,1,0:T(8,128)S(1)} %get-tuple-element.11), channel_id=1, source_target_pairs={{0,1},{1,2},{2,3},{3,4},{4,5},{5,6},{6,7},{7,8},{8,9},{9,10},{10,1... | collective-permute-start | bytes 3145736 | tf_op jit(solution)/shard_map/ppermute | solution.py:23
  272.3 1.0 copy-start.4
  309.4 49.6 %collective-permute-start.7 = (f32[4,256,256]{2,1,0:T(8,128)}, f32[4,256,256]{2,1,0:T(8,128)}, u32[]{:S(2)}, u32[]{:S(2)}) collective-permute-start(f32[4,256,256]{2,1,0:T(8,128)} %get-tuple-element.8), channel_id=1, source_target_pairs={{0,1},{1,2},{2,3},{3,4},{4,5},{5,6},{6,7},{7,8},{8,9},{9,10},{10,1... | collective-permute-start | bytes 3145736 | tf_op jit(solution)/shard_map/ppermute | solution.py:23
  312.1 46.9 %collective-permute-start.6 = (f32[4,256,256]{2,1,0:T(8,128)}, f32[4,256,256]{2,1,0:T(8,128)}, u32[]{:S(2)}, u32[]{:S(2)}) collective-permute-start(f32[4,256,256]{2,1,0:T(8,128)} %get-tuple-element.9), channel_id=1, source_target_pairs={{1,0},{2,1},{3,2},{4,3},{5,4},{6,5},{7,6},{8,7},{9,8},{10,9},{11,1... | collective-permute-start | bytes 3145736 | tf_op jit(solution)/shard_map/ppermute | solution.py:25
  359.0 9.9 %copy-start = (f32[16,256,256]{2,1,0:T(8,128)S(1)}, f32[16,256,256]{2,1,0:T(8,128)}, u32[]{:S(2)}) copy-start(f32[16,256,256]{2,1,0:T(8,128)} %fusion.111) | copy-start | bytes 12582916
Sparse Core Ops, SparseCore 0:
  431.8 46.3 reduce-scatter.1
where the time goes:
time: 494 us; the launch traced here: 485 us
  other arithmetic  239 us (48%)
  blocking collectives  72.4 us (15%)
  waiting for transfers between devices  55.6 us (11%)
  starting transfers between devices  54.2 us (11%)
  local copies, waits for them, and re-layouts  49 us (10%)
  between operations  14.6 us (3%)
    div x3, other arithmetic, shards(): (2.0 * current - (1.0 - damp) * previous + speed_sq * (laplace(padded, cu...  77.7 us
    all_to_all x3, blocking collectives, shards(): lax.all_to_all(value_buffer[step:step + 1], 'sub', split_axis=1, concat_a...  72.4 us
    add x1, other arithmetic, shards(): partial_value = partial_value + term  62.7 us
    scatter-add x4, other arithmetic, shards(): source = jnp.zeros((slab_cells,), jnp.float32).at[arrived_cells].add(step...  54.6 us
    reduce_scatter x1, waiting for transfers between devices, shards(): lax.psum_scatter(partial_value, 'shot', scatter_dimension=1, tiled=True)  46.5 us
    concatenate x4, other arithmetic, with_halo(): jnp.concatenate([lax.ppermute(tail, axis, [(i, (i + 1) % count) for i in...  29.5 us
    ppermute x4, starting transfers between devices, with_halo(): lax.ppermute(head, axis, [((i + 1) % count, i) for i in range(ends)])  23.5 us
    reshape x4, local copies, waits for them, and re-layouts, shards(): source = jnp.zeros((slab_cells,), jnp.float32).at[arrived_cells].add(step...  21 us
  transfers between devices with their start and end apart: 11, of which 2 were waited for; matrix products, arithmetic and copies ran while one was open for 19% of the time, Pallas kernels for 0%

commit v1 on v0

v1 whole, which is shorter than its diff:
```python
import functools

import jax
import jax.numpy as jnp
import ml_dtypes
import numpy as np
from jax import lax
from jax.experimental import pallas as pl
from jax.experimental.pallas import tpu as pltpu
from jax.sharding import PartitionSpec as P

PML = 16
STEPS = 4
COEFFS = (-205.0 / 72.0, 8.0 / 5.0, -1.0 / 5.0, 8.0 / 315.0, -1.0 / 560.0)
COURANT = 0.09
DAMP_MAX = 0.3
RATIO = tuple(c / COEFFS[1] for c in COEFFS)
SLAB = 16
SIZE = 256
HALF = 128
CAP = 64
MIB = 1 << 20

bf16 = jnp.bfloat16
f32 = jnp.float32


def params(mib, dims=1):
    return pltpu.CompilerParams(
        vmem_limit_bytes=mib * MIB, dimension_semantics=("arbitrary",) * dims if dims else None
    )


def cost(flops, mib):
    return pl.CostEstimate(flops=int(flops), bytes_accessed=int(mib * MIB), transcendentals=0)


def profile(index, count):
    depth = jnp.maximum(jnp.maximum(PML - index, index - (count - 1 - PML)), 0.0) / PML
    return depth * depth


def band():
    m = np.zeros((SIZE, SIZE), np.float32)
    for k in range(1, 5):
        m += RATIO[k] * (np.eye(SIZE, k=k, dtype=np.float32) + np.eye(SIZE, k=-k, dtype=np.float32))
    return m.astype(ml_dtypes.bfloat16)


def route_body(slabs, target_ref, cell_ref, trace_ref, out_ref, pick):
    listed = target_ref.shape[1]
    slots = slabs * CAP
    target = target_ref[...]
    hot = (lax.broadcasted_iota(jnp.int32, (slabs, listed), 0) == target).astype(bf16)
    earlier = (
        lax.broadcasted_iota(jnp.int32, (listed, listed), 0)
        < lax.broadcasted_iota(jnp.int32, (listed, listed), 1)
    ).astype(bf16)
    before = jnp.dot(hot, earlier, preferred_element_type=f32)
    rank = jnp.sum(before * hot.astype(f32), axis=0, keepdims=True)
    place = target * CAP + rank.astype(jnp.int32)
    value = trace_ref[...]
    top = value.astype(bf16)
    rest = value - top.astype(f32)
    middle = rest.astype(bf16)
    last = (rest - middle.astype(f32)).astype(bf16)
    cell = cell_ref[...]
    pieces = jnp.concatenate(
        [(cell >> 12).astype(f32), ((cell >> 4) & 255).astype(f32), (cell & 15).astype(f32), jnp.zeros((1, listed), f32)],
        axis=0,
    ).astype(bf16)
    table = jnp.concatenate([top, middle, last, pieces], axis=0)
    chunk = pick.shape[0]
    for start in range(0, slots, chunk):
        pick[...] = (
            lax.broadcasted_iota(jnp.int32, (chunk, listed), 0) + start == place
        ).astype(f32).astype(bf16)
        got = lax.dot_general(
            table, pick[...], (((1,), (1,)), ((), ())), preferred_element_type=f32
        )
        values = got[0:4] + got[4:8] + got[8:12]
        cells = got[12:13] * 4096.0 + got[13:14] * 16.0 + got[14:15]
        block = jnp.concatenate([values, jnp.broadcast_to(cells, (4, chunk))], axis=0)
        for j in range(chunk // CAP):
            out_ref[start // CAP + j] = block[:, j * CAP : (j + 1) * CAP]


def route(target, cell, trace, slabs):
    return pl.pallas_call(
        functools.partial(route_body, slabs),
        out_shape=jax.ShapeDtypeStruct((slabs, 8, CAP), f32),
        scratch_shapes=[pltpu.VMEM((256, target.shape[1]), bf16)],
        compiler_params=params(32, 0),
        cost_estimate=cost(2e8, 4),
        name="route",
    )(target, cell, trace)


def inject_body(cell_ref, value_ref, out_ref, dense):
    plane = pl.program_id(0)

    @pl.when(plane == 0)
    def _():
        zero = jnp.zeros((256, 128), f32)

        @pl.loop(0, dense.shape[0] // 256)
        def _(i):
            dense[pl.ds(pl.multiple_of(i * 256, 256), 256), :] = zero

        position = lax.broadcasted_iota(jnp.int32, (8, 128), 1) + 128 * (
            lax.broadcasted_iota(jnp.int32, (8, 128), 0) >> 2
        )
        batch = 4

        @pl.loop(0, value_ref.shape[0])
        def _(source):
            tile = value_ref[source]
            eight = jnp.concatenate([tile[0:4], tile[0:4]], axis=0)
            for first in range(0, CAP, batch):
                cells = [cell_ref[source * CAP + first + j] for j in range(batch)]
                rows = [c >> 8 for c in cells]
                add = [
                    jnp.where(position == (cells[j] & 255), eight[:, first + j : first + j + 1], 0.0)
                    for j in range(batch)
                ]
                at = [pl.ds(pl.multiple_of(r * 8, 8), 8) for r in rows]
                total = [dense[a, :] + u for a, u in zip(at, add)]
                for j in range(batch):
                    for i in range(j):
                        same = (rows[i] == rows[j]).astype(f32)
                        total[j] = total[j] + same * add[i]
                for j in range(batch):
                    dense[at[j], :] = total[j]

    @pl.loop(0, SIZE // 8)
    def _(group):
        base = (plane * SIZE + group * 8) * 8
        row = pl.ds(pl.multiple_of(group * 8, 8), 8)
        for step in range(STEPS):
            for half in range(2):
                out_ref[step, 0, row, half * HALF : (half + 1) * HALF] = dense[
                    pl.ds(base + half * 4 + step, 8, stride=8), :
                ]


def inject(cells, values):
    return pl.pallas_call(
        inject_body,
        out_shape=jax.ShapeDtypeStruct((STEPS, SLAB, SIZE, SIZE), f32),
        grid=(SLAB,),
        in_specs=[
            pl.BlockSpec(memory_space=pltpu.SMEM),
            pl.BlockSpec(values.shape, lambda i: (0, 0, 0)),
        ],
        out_specs=pl.BlockSpec((STEPS, 1, SIZE, SIZE), lambda i: (0, i, 0, 0)),
        scratch_shapes=[pltpu.VMEM((SLAB * SIZE * 8, 128), f32)],
        compiler_params=params(30),
        cost_estimate=cost(1e7, 32),
        name="inject",
    )(cells, values)


def side_of(group, parity):
    return (group + parity + 1) % 2


def first_edges_body(scalar_ref, *refs):
    for source, target in zip(refs[:4], refs[4:]):
        target[...] = source[...]


def first_edges(current, scalars):
    def source(group, half):
        return pl.BlockSpec((1, SIZE, HALF), lambda i, s: (side_of(group, s[0]) * 12 + i, 0, half))

    out = pl.BlockSpec((1, SIZE, HALF), lambda i, s: (i, 0, 0))
    order = [(group, half) for half in range(2) for group in range(2)]
    return pl.pallas_call(
        first_edges_body,
        out_shape=[jax.ShapeDtypeStruct((4, SIZE, HALF), f32)] * 4,
        grid_spec=pltpu.PrefetchScalarGridSpec(
            num_scalar_prefetch=1,
            grid=(4,),
            in_specs=[source(g, h) for g, h in order],
            out_specs=[out] * 4,
        ),
        compiler_params=params(8),
        cost_estimate=cost(1e5, 4),
        name="first_edges",
    )(scalars, current, current, current, current)


def factor(speed, damp):
    inverse = 1.0 / (1.0 + damp)
    return inverse, (COURANT * COURANT) * (speed * speed) * inverse


def local_body(step, scalar_ref, damp_x_ref, q_ref, p_ref, v_ref, s_ref, damp_ref, band_ref, *rest):
    if step < 2:
        n_ref, high, low, mixed = rest
    elif step == 2:
        a0_ref, a1_ref, n_ref, g_ref, high, low, mixed = rest
    else:
        a0_ref, a1_ref, part_ref, n_ref, loc_ref, send_ref, keep_ref, high, low, mixed, grad = rest
    plane = pl.program_id(0)
    here = q_ref[plane]
    top = here.astype(bf16)
    high[...] = top
    low[...] = (here - top.astype(f32)).astype(bf16)
    matrix = band_ref[...]
    mixed[...] = (
        jnp.dot(matrix, high[...], preferred_element_type=f32)
        + jnp.dot(matrix, low[...], preferred_element_type=f32)
        + jnp.dot(high[...], matrix, preferred_element_type=f32)
        + jnp.dot(low[...], matrix, preferred_element_type=f32)
    )
    damp_x = damp_x_ref[plane]
    rows = 16

    def update(row, across):
        now = q_ref[plane, row, :]
        before = p_ref[0, row, :]
        speed = v_ref[0, row, :]
        inverse, gain = factor(speed, damp_ref[row, :] + damp_x)
        around = mixed[row, :] + across(row)
        laplace = (3.0 * COEFFS[0]) * now + COEFFS[1] * around
        after = before + (2.0 * inverse) * (now - before) + gain * (laplace + s_ref[0, 0, row, :])
        n_ref[0, row, :] = after
        if step == 2:
            g_ref[0, row, :] = before * a0_ref[0, 0, 0, row, :].astype(f32) + now * a1_ref[0, 0, 0, row, :].astype(f32)
        if step == 3:
            total = (
                part_ref[0, row, :]
                + now * a0_ref[0, 0, 0, row, :].astype(f32)
                + after * a1_ref[0, 0, 0, row, :].astype(f32)
            )
            grad[row, :] = total * (2.0 / (speed * speed * speed))

    inside = jnp.logical_and(plane >= 4, plane < SLAB - 4)

    @pl.when(inside)
    def _():
        def across(row):
            total = q_ref[plane - 1, row, :] + q_ref[plane + 1, row, :]
            for k in range(2, 5):
                total = total + RATIO[k] * (q_ref[plane - k, row, :] + q_ref[plane + k, row, :])
            return total

        @pl.loop(0, SIZE // rows)
        def _(i):
            update(pl.ds(pl.multiple_of(i * rows, rows), rows), across)

    @pl.when(jnp.logical_not(inside))
    def _():
        terms = []
        for k in range(1, 5):
            for offset in (-k, k):
                at = plane + offset
                fits = jnp.logical_and(at >= 0, at < SLAB)
                terms.append((jnp.clip(at, 0, SLAB - 1), jnp.where(fits, RATIO[k], 0.0).astype(f32)))

        def across(row):
            total = terms[0][1] * q_ref[terms[0][0], row, :]
            for at, weight in terms[1:]:
                total = total + weight * q_ref[at, row, :]
            return total

        @pl.loop(0, SIZE // rows)
        def _(i):
            update(pl.ds(pl.multiple_of(i * rows, rows), rows), across)

    if step == 3:
        core = scalar_ref[1]

        @pl.when(inside)
        def _():
            for y in range(2):
                send_ref[0, y] = grad[pl.ds(pl.multiple_of(y * 128 + 64 * (1 - core), 64), 64), :]
                keep_ref[0, y] = grad[pl.ds(pl.multiple_of(y * 128 + 64 * core, 64), 64), :]

        @pl.when(jnp.logical_not(inside))
        def _():
            loc_ref[0] = grad[...]


def local_step(step, scalars, damp_x, q, p, v, s, damp, accel, part):
    plane = (1, SIZE, SIZE)
    plane_spec = pl.BlockSpec(plane, lambda i, *_: (i, 0, 0))
    whole_spec = pl.BlockSpec((SLAB, SIZE, SIZE), lambda i, *_: (0, 0, 0), pipeline_mode=pl.Buffered(1))
    flat_spec = pl.BlockSpec((SIZE, SIZE), lambda i, *_: (0, 0))
    in_specs = [
        whole_spec,
        plane_spec,
        plane_spec,
        pl.BlockSpec((1,) + plane, lambda i, *_: (step, i, 0, 0)),
        flat_spec,
        flat_spec,
    ]
    operands = [q, p, v, s, damp, jnp.asarray(band())]
    out_specs = [plane_spec]
    out_shape = [jax.ShapeDtypeStruct((SLAB, SIZE, SIZE), f32)]
    scratch = [
        pltpu.VMEM((SIZE, SIZE), bf16),
        pltpu.VMEM((SIZE, SIZE), bf16),
        pltpu.VMEM((SIZE, SIZE), f32),
    ]
    mib = 20

    def accel_spec(t):
        return pl.BlockSpec((1, 1) + plane, lambda i, *_: (0, t, i, 0, 0))

    if step == 2:
        in_specs += [accel_spec(0), accel_spec(1)]
        operands += [accel, accel]
        out_specs.append(plane_spec)
        out_shape.append(jax.ShapeDtypeStruct((SLAB, SIZE, SIZE), f32))
        mib = 28
    if step == 3:
        in_specs += [accel_spec(2), accel_spec(3), plane_spec]
        operands += [accel, accel, part]
        out_specs.append(
            pl.BlockSpec(plane, lambda i, *_: (jnp.where(i < 4, i, jnp.where(i < 12, 3, i - 8)), 0, 0))
        )
        out_shape.append(jax.ShapeDtypeStruct((8, SIZE, SIZE), f32))
        quarter = pl.BlockSpec((1, 2, 64, SIZE), lambda i, *_: (jnp.clip(i - 4, 0, 7), 0, 0, 0))
        out_specs += [quarter, quarter]
        out_shape += [jax.ShapeDtypeStruct((8, 2, 64, SIZE), f32)] * 2
        scratch.append(pltpu.VMEM((SIZE, SIZE), f32))
        mib = 33
    return pl.pallas_call(
        functools.partial(local_body, step),
        out_shape=out_shape,
        grid_spec=pltpu.PrefetchScalarGridSpec(
            num_scalar_prefetch=2,
            grid=(SLAB,),
            in_specs=in_specs,
            out_specs=out_specs,
            scratch_shapes=scratch,
        ),
        compiler_params=params(30),
        cost_estimate=cost(4e9, mib),
        name=f"local_step{step}",
    )(scalars, damp_x, *operands)


def edge_body(last, scalar_ref, damp_x_ref, even_ref, odd_ref, n_in, v_ref, damp_ref, *rest):
    if last:
        a_ref, loc_ref, n_ref, send_ref, keep_ref, grad = rest
    else:
        n_ref, e_ref, o_ref = rest
    group = pl.program_id(0)
    upper = side_of(group, scalar_ref[0])
    core = scalar_ref[1]
    rows = 16
    weights = [
        [
            jnp.where(
                upper == 1,
                COEFFS[4 + m - j] if m <= j else 0.0,
                COEFFS[4 + j - m] if m >= j else 0.0,
            ).astype(f32)
            for m in range(4)
        ]
        for j in range(4)
    ]

    def run(halo_ref, edge_ref):
        @pl.loop(0, HALF // rows)
        def _(i):
            row = pl.ds(pl.multiple_of(i * rows, rows), rows)
            halo = [halo_ref[m, row, :] for m in range(4)]
            damp = damp_ref[row, :]
            for j in range(4):
                speed = v_ref[j, row, :]
                _, gain = factor(speed, damp + damp_x_ref[upper * 12 + j])
                across = weights[j][0] * halo[0]
                for m in range(1, 4):
                    across = across + weights[j][m] * halo[m]
                extra = gain * across
                after = n_in[j, row, :] + extra
                n_ref[j, row, :] = after
                if last:
                    grad[j, row, :] = loc_ref[j, row, :] + extra * a_ref[0, 0, j, row, :].astype(f32) * (
                        2.0 / (speed * speed * speed)
                    )
                else:
                    edge_ref[j, row, :] = after

    @pl.when(group == 0)
    def _():
        run(even_ref, None if last else e_ref)

    @pl.when(group == 1)
    def _():
        run(odd_ref, None if last else o_ref)

    if last:
        send_ref[0, :, 0] = grad[:, pl.ds(pl.multiple_of(64 * (1 - core), 64), 64), :]
        keep_ref[0, :, 0] = grad[:, pl.ds(pl.multiple_of(64 * core, 64), 64), :]


def edge_step(last, half, scalars, damp_x, even, odd, n, v, damp, accel, loc):
    block = (4, HALF, HALF)

    def edge_block(g, y, s, _):
        return (3 * side_of(g, s[0]), y, half)

    edge_spec = pl.BlockSpec(block, edge_block)
    even_spec = pl.BlockSpec(block, lambda g, y, *_: (0, jnp.where(g == 0, y, 1), 0))
    odd_spec = pl.BlockSpec(block, lambda g, y, *_: (0, jnp.where(g == 0, 0, y), 0))
    in_specs = [
        even_spec,
        odd_spec,
        edge_spec,
        edge_spec,
        pl.BlockSpec((HALF, HALF), lambda g, y, *_: (y, half)),
    ]
    operands = [even, odd, n, v, damp]
    out_specs = [edge_spec]
    out_shape = [jax.ShapeDtypeStruct((SLAB, SIZE, SIZE), f32)]
    scratch = []
    if last:
        in_specs += [
            pl.BlockSpec((1, 1) + block, lambda g, y, s, _: (0, 3, 3 * side_of(g, s[0]), y, half)),
            pl.BlockSpec(block, lambda g, y, s, _: (side_of(g, s[0]), y, half)),
        ]
        operands += [accel, loc]
        quarter = pl.BlockSpec((1, 4, 1, 64, HALF), lambda g, y, *_: (g, 0, y, 0, 0))
        out_specs += [quarter, quarter]
        out_shape += [jax.ShapeDtypeStruct((2, 4, 2, 64, HALF), f32)] * 2
        scratch = [pltpu.VMEM(block, f32)]
    else:
        out_specs += [even_spec, odd_spec]
        out_shape += [jax.ShapeDtypeStruct((4, SIZE, HALF), f32)] * 2
    return pl.pallas_call(
        functools.partial(edge_body, last),
        out_shape=out_shape,
        grid_spec=pltpu.PrefetchScalarGridSpec(
            num_scalar_prefetch=2,
            grid=(2, 2),
            in_specs=in_specs,
            out_specs=out_specs,
            scratch_shapes=scratch,
        ),
        input_output_aliases={4: 0},
        compiler_params=params(16, 2),
        cost_estimate=cost(1e7, 7),
        name=f"edge_step{half}",
    )(scalars, damp_x, *operands)


def split_body(scalar_ref, got_ref, own_ref, send_ref, keep_ref):
    y = scalar_ref[2]
    send_ref[0] = got_ref[0, 1 - y] + own_ref[0, 1 - y]
    keep_ref[0] = got_ref[0, y] + own_ref[0, y]


def split_sum(scalars, got, own):
    layers, _, rows, width = got.shape
    step = pl.BlockSpec((1, 2, rows, width), lambda i, s: (i, 0, 0, 0))
    out = pl.BlockSpec((1, rows, width), lambda i, s: (i, 0, 0))
    return pl.pallas_call(
        split_body,
        out_shape=[jax.ShapeDtypeStruct((layers, rows, width), f32)] * 2,
        grid_spec=pltpu.PrefetchScalarGridSpec(
            num_scalar_prefetch=1, grid=(layers,), in_specs=[step, step], out_specs=[out, out]
        ),
        compiler_params=params(8),
        cost_estimate=cost(1e5, 3),
        name="split_sum",
    )(scalars, got, own)


def gather_body(scalar_ref, *refs):
    inner_a, inner_b, first_a, first_b, second_a, second_b, out_ref = refs
    block = pl.program_id(0)
    inside = jnp.logical_or(block == 1, block == 2)

    @pl.when(inside)
    def _():
        out_ref[...] = inner_a[...] + inner_b[...]

    @pl.when(jnp.logical_not(inside))
    def _():
        out_ref[:, :, 0:HALF] = first_a[...] + first_b[...]
        out_ref[:, :, HALF:SIZE] = second_a[...] + second_b[...]


def gather_sum(scalars, inner, first, second):
    inner_spec = pl.BlockSpec((4, 64, SIZE), lambda i, s: (jnp.clip(i - 1, 0, 1), 0, 0))

    def group(i, s):
        upper = (i == 3).astype(jnp.int32)
        return (upper + s[0] + 1) % 2, 0, 0

    edge_spec = pl.BlockSpec((4, 64, HALF), group)
    return pl.pallas_call(
        gather_body,
        out_shape=jax.ShapeDtypeStruct((SLAB, 64, SIZE), f32),
        grid_spec=pltpu.PrefetchScalarGridSpec(
            num_scalar_prefetch=1,
            grid=(4,),
            in_specs=[inner_spec, inner_spec] + [edge_spec] * 4,
            out_specs=pl.BlockSpec((4, 64, SIZE), lambda i, s: (i, 0, 0)),
        ),
        compiler_params=params(8),
        cost_estimate=cost(1e5, 3),
        name="gather_sum",
    )(scalars, *inner, *first, *second)


def shards(velocity, adjoint_now, adjoint_prev, forward_accel, traces, receiver_sub, receiver_cell):
    slabs = lax.axis_size("sub")
    slab = lax.axis_index("sub")
    shot = lax.axis_index("shot")
    pairs_even = [(i, i ^ 1) for i in range(slabs)]
    pairs_odd = [pair for a in range(1, slabs - 1, 2) for pair in ((a, a + 1), (a + 1, a))]
    shots = lax.axis_size("shot")
    swap_core = [(i, i ^ 1) for i in range(shots)]
    swap_row = [(i, i ^ 2) for i in range(shots)]
    scalars = jnp.stack([slab % 2, shot % 2, shot // 2]).astype(jnp.int32)
    start_x = (slab * SLAB).astype(f32)
    damp_x = DAMP_MAX * profile(start_x + jnp.arange(SLAB, dtype=f32), SLAB * slabs)
    line = profile(jnp.arange(SIZE, dtype=f32), SIZE)
    damp = DAMP_MAX * (line[:, None] + line[None, :])

    def exchange(even, odd):
        return lax.ppermute(even, "sub", pairs_even), lax.ppermute(odd, "sub", pairs_odd)

    current = adjoint_now[0]
    previous = adjoint_prev[0]
    even_a, odd_a, even_b, odd_b = first_edges(current, scalars)
    arrived_a = exchange(even_a, odd_a)
    arrived_b = exchange(even_b, odd_b)

    listed = receiver_sub.shape[1]
    sent = route(
        receiver_sub.reshape(1, listed), receiver_cell.reshape(1, listed), traces[0], slabs
    )
    got = lax.all_to_all(sent, "sub", split_axis=0, concat_axis=0, tiled=True)
    cells = got[:, 4, :].reshape(slabs * CAP).astype(jnp.int32)
    source = inject(cells, got)

    part = None
    for step in range(STEPS):
        out = local_step(
            step, scalars, damp_x, current, previous, velocity, source, damp, forward_accel, part
        )
        after = out[0]
        last = step == STEPS - 1
        loc = None
        if step == 2:
            part = out[1]
        if last:
            loc, send, keep = out[1:]
            send, inner_keep = split_sum(scalars, lax.ppermute(send, "shot", swap_core), keep)
            inner = (lax.ppermute(send, "shot", swap_row), inner_keep)
        outs = []
        for half, arrived in enumerate((arrived_a, arrived_b)):
            after, x, y = edge_step(
                last, half, scalars, damp_x, *arrived, after, velocity, damp, forward_accel, loc
            )
            if last:
                x = x.reshape(8, 2, 64, HALF)
                y = y.reshape(8, 2, 64, HALF)
                send, edge_keep = split_sum(scalars, lax.ppermute(x, "shot", swap_core), y)
                outs.append((lax.ppermute(send, "shot", swap_row), edge_keep))
            else:
                outs.append(exchange(x, y))
        previous = current
        current = after
        if not last:
            arrived_a, arrived_b = outs
    share = gather_sum(scalars, inner, *outs)
    return current[None], share


def solution(mesh):
    in_specs = (
        P("sub", None, None),
        P("shot", "sub", None, None),
        P("shot", "sub", None, None),
        P("shot", None, "sub", None, None),
        P("shot", None, "sub"),
        P("shot", "sub", None),
        P("shot", "sub"),
    )
    out_specs = (P("shot", "sub", None, None), P("sub", "shot", None))
    return jax.shard_map(shards, mesh=mesh, in_specs=in_specs, out_specs=out_specs, check_vma=False)
```

time: 494 us -> 240 us (0.49); the launches traced: 485 us -> 238 us
  other arithmetic: 239 us -> 1.05 us
  Pallas kernels: 0 us -> 119 us
  blocking collectives: 72.4 us -> 0 us
  local copies, waits for them, and re-layouts: 49 us -> 9.48 us
  between operations: 14.6 us -> 1.09 us
  waiting for transfers between devices: 55.6 us -> 49.1 us
    pallas_call x0 -> x19, Pallas kernels: none -> 119 us  [the longest x4 67.3 us: local_step(): pl.pallas_call(functools.partial(local_body, step), out_shape=out_shape,...]
    div x3 -> x0, other arithmetic: 77.7 us -> none  [shards(): (2.0 * current - (1.0 - damp) * previous + speed_sq * (laplace(padded, cu...]
    all_to_all x3 -> x0, blocking collectives: 72.4 us -> none  [shards(): lax.all_to_all(value_buffer[step:step + 1], 'sub', split_axis=1, concat_a...]
    add x2 -> x0, other arithmetic: 62.8 us -> none  [the longest x1 62.7 us: shards(): partial_value = partial_value + term]
    scatter-add x4 -> x0, other arithmetic: 54.6 us -> none  [shards(): source = jnp.zeros((slab_cells,), jnp.float32).at[arrived_cells].add(step...]
    reduce_scatter x1 -> x0, waiting for transfers between devices: 46.5 us -> none  [shards(): lax.psum_scatter(partial_value, 'shot', scatter_dimension=1, tiled=True)]
    ppermute x8 -> x22, waiting for transfers between devices: 0.02 us -> 38.2 us  [the longest x2 21.3 us: shards(): outs.append((lax.ppermute(send, 'shot', swap_row), edge_keep))]
    concatenate x4 -> x0, other arithmetic: 29.5 us -> none  [with_halo(): jnp.concatenate([lax.ppermute(tail, axis, [(i, (i + 1) % count) for i in...]
  transfers between devices with their start and end apart: 11 -> 23, of which waited for: 2 -> 6; matrix products, arithmetic and copies ran while one was open for 19% -> 1% of each run, Pallas kernels for 0% -> 39%
where the time goes in v1:
time: 240 us; the launch traced here: 238 us
  Pallas kernels  119 us (50%)
  starting transfers between devices  58.2 us (24%)
  waiting for transfers between devices  49.1 us (20%)
  local copies, waits for them, and re-layouts  9.48 us (4%)
    pallas_call x4, Pallas kernels, local_step(): pl.pallas_call(functools.partial(local_body, step), out_shape=out_shape,...  67.3 us
    ppermute x8, starting transfers between devices, exchange(): lax.ppermute(odd, 'sub', pairs_odd)  41.1 us
    pallas_call x8, Pallas kernels, edge_step(): pl.pallas_call(functools.partial(edge_body, last), out_shape=out_shape, g...  24.3 us
    ppermute x2, waiting for transfers between devices, shards(): outs.append((lax.ppermute(send, 'shot', swap_row), edge_keep))  21.3 us
    pallas_call x1, Pallas kernels, inject(): pl.pallas_call(inject_body, out_shape=jax.ShapeDtypeStruct((STEPS, SLAB,...  18.7 us
    ppermute x8, waiting for transfers between devices, exchange(): lax.ppermute(odd, 'sub', pairs_odd)  12.6 us
    all_to_all x1, waiting for transfers between devices, shards(): got = lax.all_to_all(sent, 'sub', split_axis=0, concat_axis=0, tiled=True)  10.9 us
    all_to_all x1, starting transfers between devices, shards(): got = lax.all_to_all(sent, 'sub', split_axis=0, concat_axis=0, tiled=True)  9.38 us
  transfers between devices with their start and end apart: 23, of which 6 were waited for; matrix products, arithmetic and copies ran while one was open for 1% of the time, Pallas kernels for 39%

profile of v1, /device:TPU:2, one launch (start us, length us, event | category | flops | bytes accessed | tf_op | source)
XLA Modules:
  0.0 237.8 jit_solution(14251239345096453315)
XLA Ops:
  7.5 7.0 %collective-permute-start.1 = (f32[4,256,128]{2,1,0:T(8,128)}, f32[4,256,128]{2,1,0:T(8,128)S(1)}, u32[]{:S(2)}, u32[]{:S(2)}) collective-permute-start(f32[4,256,128]{2,1,0:T(8,128)} %get-tuple-element.43), channel_id=1, source_target_pairs={{1,2},{2,1},{3,4},{4,3},{5,6},{6,5},{7,8},{8,7},{9,10},{10,9},{11,... | collective-permute-start | bytes 1572872 | tf_op jit(solution)/shard_map/ppermute | solution.py:528
  14.6 3.5 %collective-permute-start.3 = (f32[4,256,128]{2,1,0:T(8,128)}, f32[4,256,128]{2,1,0:T(8,128)}, u32[]{:S(2)}, u32[]{:S(2)}) collective-permute-start(f32[4,256,128]{2,1,0:T(8,128)} %get-tuple-element.45), channel_id=1, source_target_pairs={{1,2},{2,1},{3,4},{4,3},{5,6},{6,5},{7,8},{8,7},{9,10},{10,9},{11,... | collective-permute-start | bytes 1572872 | tf_op jit(solution)/shard_map/ppermute | solution.py:528
  20.6 9.4 %all-to-all-start = ((f32[32,1,512]{2,1,0:T(1,128)}), f32[32,1,512]{2,1,0:T(1,128)S(1)}, u32[]{:S(2)}, u32[]{:S(2)}) async-start(f32[32,1,512]{2,1,0:T(1,128)} %reshape.52), calls=%async_computation | async-start | bytes 131072 | tf_op jit(solution)/shard_map/all_to_all | solution.py:540
  30.1 10.9 %all-to-all-done = f32[32,1,512]{2,1,0:T(1,128)S(1)} async-done(((f32[32,1,512]{2,1,0:T(1,128)}), f32[32,1,512]{2,1,0:T(1,128)S(1)}, u32[]{:S(2)}, u32[]{:S(2)}) %all-to-all-start) | async-done | bytes 65568 | tf_op jit(solution)/shard_map/all_to_all | solution.py:540
  42.6 18.7 %inject.1.s_ref = f32[4,16,256,256]{3,2,1,0:T(8,128)S(1)} custom-call(s32[2048]{0:T(1024)S(1)} %convert_element_type.10.cell_ref, f32[32,8,64]{2,1,0:T(8,128)S(1)} %reshape.53.value_ref), custom_call_target="tpu_custom_call" | custom-call | flops 10000000 | bytes 33554432 | tf_op jit(solution)/shard_map/inject/pallas_call | solution.py:147
  61.3 5.8 %copy-done.1 = f32[4,16,256,256]{3,2,1,0:T(8,128)} copy-done((f32[4,16,256,256]{3,2,1,0:T(8,128)}, f32[4,16,256,256]{3,2,1,0:T(8,128)S(1)}, u32[]{:S(2)}) %copy-start.1) | copy-done | bytes 16777240
  67.1 15.6 %local_step0.1.n_in = f32[16,256,256]{2,1,0:T(8,128)S(1)} custom-call(s32[3]{0:T(128)S(1)} %pad_add_fusion.scalar_ref, f32[16]{0:T(128)S(1)} %multiply_multiply_fusion.damp_x_ref, f32[16,256,256]{2,1,0:T(8,128)S(1)} %bitcast.18, f32[16,256,256]{2,1,0:T(8,128)S(1)} %bitcast.20, f32[16,256,256]{2,1,0:T(8,128)S(1)} %copy-done, f32[4,16,256,256]{3,2,1,0:T(8,128)} %copy-done.1, ...), custom_call_target="tpu_custom_call" | custom-call | flops 4000000000 | bytes 20971520 | tf_op jit(solution)/shard_map/local_step0/pallas_call | solution.py:330
  82.7 3.6 %edge_step0.4 = (f32[16,256,256]{2,1,0:T(8,128)S(1)}, f32[4,256,128]{2,1,0:T(8,128)S(1)}, f32[4,256,128]{2,1,0:T(8,128)S(1)}) custom-call(s32[3]{0:T(128)S(1)} %pad_add_fusion.scalar_ref, f32[16]{0:T(128)S(1)} %multiply_multiply_fusion.damp_x_ref, f32[4,256,128]{2,1,0:T(8,128)} %collective-permute-done.2.even_ref, ...), custom_call_target="tpu_custom_call", output_to_operand_aliasing={{0}: (4, {})} | custom-call | flops 10000000 | bytes 7340032 | tf_op jit(solution)/shard_map/edge_step0/pallas_call | solution.py:435
  87.6 5.3 %collective-permute-start.7 = (f32[4,256,128]{2,1,0:T(8,128)S(1)}, f32[4,256,128]{2,1,0:T(8,128)S(1)}, u32[]{:S(2)}, u32[]{:S(2)}) collective-permute-start(f32[4,256,128]{2,1,0:T(8,128)S(1)} %get-tuple-element.50), channel_id=1, source_target_pairs={{1,2},{2,1},{3,4},{4,3},{5,6},{6,5},{7,8},{8,7},{9,10},{10,9},{11,... | collective-permute-start | bytes 1572872 | tf_op jit(solution)/shard_map/ppermute | solution.py:528
  95.3 5.0 %collective-permute-start.5 = (f32[4,256,128]{2,1,0:T(8,128)S(1)}, f32[4,256,128]{2,1,0:T(8,128)S(1)}, u32[]{:S(2)}, u32[]{:S(2)}) collective-permute-start(f32[4,256,128]{2,1,0:T(8,128)S(1)} %get-tuple-element.48), channel_id=1, source_target_pairs={{1,2},{2,1},{3,4},{4,3},{5,6},{6,5},{7,8},{8,7},{9,10},{10,9},{11,... | collective-permute-start | bytes 1572872 | tf_op jit(solution)/shard_map/ppermute | solution.py:528
  100.4 15.6 %local_step1.1.n_in = f32[16,256,256]{2,1,0:T(8,128)S(1)} custom-call(s32[3]{0:T(128)S(1)} %pad_add_fusion.scalar_ref, f32[16]{0:T(128)S(1)} %multiply_multiply_fusion.damp_x_ref, f32[16,256,256]{2,1,0:T(8,128)S(1)} %get-tuple-element.51.q_ref.p_ref, f32[16,256,256]{2,1,0:T(8,128)S(1)} %bitcast.19, f32[16,256,256]{2,1,0:T(8,128)S(1)} %copy-done, ...), custom_call_target="tpu_custom_call" | custom-call | flops 4000000000 | bytes 20971520 | tf_op jit(solution)/shard_map/local_step1/pallas_call | solution.py:330
  119.0 4.6 %collective-permute-start.11 = (f32[4,256,128]{2,1,0:T(8,128)S(1)}, f32[4,256,128]{2,1,0:T(8,128)S(1)}, u32[]{:S(2)}, u32[]{:S(2)}) collective-permute-start(f32[4,256,128]{2,1,0:T(8,128)S(1)} %get-tuple-element.56), channel_id=1, source_target_pairs={{1,2},{2,1},{3,4},{4,3},{5,6},{6,5},{7,8},{8,7},{9,10},{10,9},{11,... | collective-permute-start | bytes 1572872 | tf_op jit(solution)/shard_map/ppermute | solution.py:528
  126.1 5.7 %collective-permute-start.9 = (f32[4,256,128]{2,1,0:T(8,128)S(1)}, f32[4,256,128]{2,1,0:T(8,128)S(1)}, u32[]{:S(2)}, u32[]{:S(2)}) collective-permute-start(f32[4,256,128]{2,1,0:T(8,128)S(1)} %get-tuple-element.54), channel_id=1, source_target_pairs={{1,2},{2,1},{3,4},{4,3},{5,6},{6,5},{7,8},{8,7},{9,10},{10,9},{11,... | collective-permute-start | bytes 1572872 | tf_op jit(solution)/shard_map/ppermute | solution.py:528
  131.8 16.8 %local_step2.1 = (f32[16,256,256]{2,1,0:T(8,128)S(1)}, f32[16,256,256]{2,1,0:T(8,128)S(1)}) custom-call(s32[3]{0:T(128)S(1)} %pad_add_fusion.scalar_ref, f32[16]{0:T(128)S(1)} %multiply_multiply_fusion.damp_x_ref, f32[16,256,256]{2,1,0:T(8,128)S(1)} %get-tuple-element.57.q_ref.p_ref, f32[16,256,256]{2,1,0:T(8,128)S(1)} %get-tuple-element.51.q_ref.p_ref, ...), custom_call_target="tpu_custom_call" | custom-call | flops 4000000000 | bytes 29360128 | tf_op jit(solution)/shard_map/local_step2/pallas_call | solution.py:330
  153.3 19.3 %local_step3.1 = (f32[16,256,256]{2,1,0:T(8,128)}, f32[8,256,256]{2,1,0:T(8,128)S(1)}, f32[8,2,64,256]{3,2,1,0:T(8,128)S(1)}, f32[8,2,64,256]{3,2,1,0:T(8,128)S(1)}) custom-call(s32[3]{0:T(128)S(1)} %pad_add_fusion.scalar_ref, f32[16]{0:T(128)S(1)} %multiply_multiply_fusion.damp_x_ref, f32[16,256,256]{2,1,0:T(8,128)S(1)} %get-tuple-element.64.q_ref, ...), custom_call_target="tpu_custom_call" | custom-call | flops 4000000000 | bytes 34603008 | tf_op jit(solution)/shard_map/local_step3/pallas_call | solution.py:330
  172.7 4.6 %collective-permute-start.15 = (f32[4,256,128]{2,1,0:T(8,128)S(1)}, f32[4,256,128]{2,1,0:T(8,128)S(1)}, u32[]{:S(2)}, u32[]{:S(2)}) collective-permute-start(f32[4,256,128]{2,1,0:T(8,128)S(1)} %get-tuple-element.63), channel_id=1, source_target_pairs={{1,2},{2,1},{3,4},{4,3},{5,6},{6,5},{7,8},{8,7},{9,10},{10,9},{11,... | collective-permute-start | bytes 1572872 | tf_op jit(solution)/shard_map/ppermute | solution.py:528
  177.9 5.2 %collective-permute-start.13 = (f32[4,256,128]{2,1,0:T(8,128)S(1)}, f32[4,256,128]{2,1,0:T(8,128)S(1)}, u32[]{:S(2)}, u32[]{:S(2)}) collective-permute-start(f32[4,256,128]{2,1,0:T(8,128)S(1)} %get-tuple-element.61), channel_id=1, source_target_pairs={{1,2},{2,1},{3,4},{4,3},{5,6},{6,5},{7,8},{8,7},{9,10},{10,9},{11,... | collective-permute-start | bytes 1572872 | tf_op jit(solution)/shard_map/ppermute | solution.py:528
  183.1 4.2 %collective-permute-done.14.even_ref = f32[4,256,128]{2,1,0:T(8,128)S(1)} collective-permute-done((f32[4,256,128]{2,1,0:T(8,128)S(1)}, f32[4,256,128]{2,1,0:T(8,128)S(1)}, u32[]{:S(2)}, u32[]{:S(2)}) %collective-permute-start.14) | collective-permute-done | bytes 524320 | tf_op jit(solution)/shard_map/ppermute | solution.py:528
  187.4 6.4 %collective-permute-done.15.odd_ref = f32[4,256,128]{2,1,0:T(8,128)S(1)} collective-permute-done((f32[4,256,128]{2,1,0:T(8,128)S(1)}, f32[4,256,128]{2,1,0:T(8,128)S(1)}, u32[]{:S(2)}, u32[]{:S(2)}) %collective-permute-start.15) | collective-permute-done | bytes 524320 | tf_op jit(solution)/shard_map/ppermute | solution.py:528
  193.8 4.6 %edge_step0.7 = (f32[16,256,256]{2,1,0:T(8,128)}, f32[2,4,2,64,128]{4,3,2,1,0:T(8,128)S(1)}, f32[2,4,2,64,128]{4,3,2,1,0:T(8,128)S(1)}) custom-call(s32[3]{0:T(128)S(1)} %pad_add_fusion.scalar_ref, f32[16]{0:T(128)S(1)} %multiply_multiply_fusion.damp_x_ref, f32[4,256,128]{2,1,0:T(8,128)S(1)} %collective-permute-done.14.even_ref, ...), custom_call_target="tpu_custom_call", output_to_operand_aliasing={{0}: (4, {})} | custom-call | flops 10000000 | bytes 7340032 | tf_op jit(solution)/shard_map/edge_step0/pallas_call | solution.py:435
  198.4 6.2 %collective-permute-done.13.odd_ref = f32[4,256,128]{2,1,0:T(8,128)S(1)} collective-permute-done((f32[4,256,128]{2,1,0:T(8,128)S(1)}, f32[4,256,128]{2,1,0:T(8,128)S(1)}, u32[]{:S(2)}, u32[]{:S(2)}) %collective-permute-start.13) | collective-permute-done | bytes 524320 | tf_op jit(solution)/shard_map/ppermute | solution.py:528
  204.6 4.6 %edge_step1.7 = (f32[16,256,256]{2,1,0:T(8,128)}, f32[2,4,2,64,128]{4,3,2,1,0:T(8,128)S(1)}, f32[2,4,2,64,128]{4,3,2,1,0:T(8,128)S(1)}) custom-call(s32[3]{0:T(128)S(1)} %pad_add_fusion.scalar_ref, f32[16]{0:T(128)S(1)} %multiply_multiply_fusion.damp_x_ref, f32[4,256,128]{2,1,0:T(8,128)S(1)} %collective-permute-done.12.even_ref, ...), custom_call_target="tpu_custom_call", output_to_operand_aliasing={{0}: (4, {})} | custom-call | flops 10000000 | bytes 7340032 | tf_op jit(solution)/shard_map/edge_step1/pallas_call | solution.py:435
  214.4 16.0 %collective-permute-done.19.refs_2_ = f32[8,64,128]{2,1,0:T(8,128)S(1)} collective-permute-done((f32[8,64,128]{2,1,0:T(8,128)S(1)}, f32[8,64,128]{2,1,0:T(8,128)S(1)}, u32[]{:S(2)}, u32[]{:S(2)}) %collective-permute-start.19) | collective-permute-done | bytes 262176 | tf_op jit(solution)/shard_map/ppermute | solution.py:567
  230.5 5.2 %collective-permute-done.21.refs_4_ = f32[8,64,128]{2,1,0:T(8,128)S(1)} collective-permute-done((f32[8,64,128]{2,1,0:T(8,128)S(1)}, f32[8,64,128]{2,1,0:T(8,128)S(1)}, u32[]{:S(2)}, u32[]{:S(2)}) %collective-permute-start.21) | collective-permute-done | bytes 262176 | tf_op jit(solution)/shard_map/ppermute | solution.py:567
  (78 shorter events, 32.7 us)
Async XLA Ops:
  5.6 87.4 %collective-permute-start = (f32[4,256,128]{2,1,0:T(8,128)}, f32[4,256,128]{2,1,0:T(8,128)S(1)}, u32[]{:S(2)}, u32[]{:S(2)}) collective-permute-start(f32[4,256,128]{2,1,0:T(8,128)} %get-tuple-element.42), channel_id=1, source_target_pairs={{0,1},{1,0},{2,3},{3,2},{4,5},{5,4},{6,7},{7,6},{8,9},{9,8},{10,11... | collective-permute-start | bytes 1572872 | tf_op jit(solution)/shard_map/ppermute | solution.py:528
  7.5 85.5 %collective-permute-start.1 = (f32[4,256,128]{2,1,0:T(8,128)}, f32[4,256,128]{2,1,0:T(8,128)S(1)}, u32[]{:S(2)}, u32[]{:S(2)}) collective-permute-start(f32[4,256,128]{2,1,0:T(8,128)} %get-tuple-element.43), channel_id=1, source_target_pairs={{1,2},{2,1},{3,4},{4,3},{5,6},{6,5},{7,8},{8,7},{9,10},{10,9},{11,... | collective-permute-start | bytes 1572872 | tf_op jit(solution)/shard_map/ppermute | solution.py:528
  14.5 68.2 %collective-permute-start.2 = (f32[4,256,128]{2,1,0:T(8,128)}, f32[4,256,128]{2,1,0:T(8,128)}, u32[]{:S(2)}, u32[]{:S(2)}) collective-permute-start(f32[4,256,128]{2,1,0:T(8,128)} %get-tuple-element.44), channel_id=1, source_target_pairs={{0,1},{1,0},{2,3},{3,2},{4,5},{5,4},{6,7},{7,6},{8,9},{9,8},{10,11... | collective-permute-start | bytes 1572872 | tf_op jit(solution)/shard_map/ppermute | solution.py:528
  14.6 68.1 %collective-permute-start.3 = (f32[4,256,128]{2,1,0:T(8,128)}, f32[4,256,128]{2,1,0:T(8,128)}, u32[]{:S(2)}, u32[]{:S(2)}) collective-permute-start(f32[4,256,128]{2,1,0:T(8,128)} %get-tuple-element.45), channel_id=1, source_target_pairs={{1,2},{2,1},{3,4},{4,3},{5,6},{6,5},{7,8},{8,7},{9,10},{10,9},{11,... | collective-permute-start | bytes 1572872 | tf_op jit(solution)/shard_map/ppermute | solution.py:528
  20.6 20.4 %all-to-all-start = ((f32[32,1,512]{2,1,0:T(1,128)}), f32[32,1,512]{2,1,0:T(1,128)S(1)}, u32[]{:S(2)}, u32[]{:S(2)}) async-start(f32[32,1,512]{2,1,0:T(1,128)} %reshape.52), calls=%async_computation | async-start | bytes 131072 | tf_op jit(solution)/shard_map/all_to_all | solution.py:540
  86.3 29.7 %collective-permute-start.6 = (f32[4,256,128]{2,1,0:T(8,128)S(1)}, f32[4,256,128]{2,1,0:T(8,128)S(1)}, u32[]{:S(2)}, u32[]{:S(2)}) collective-permute-start(f32[4,256,128]{2,1,0:T(8,128)S(1)} %get-tuple-element.49), channel_id=1, source_target_pairs={{0,1},{1,0},{2,3},{3,2},{4,5},{5,4},{6,7},{7,6},{8,9},{9,8},{10,11... | collective-permute-start | bytes 1572872 | tf_op jit(solution)/shard_map/ppermute | solution.py:528
  87.6 28.4 %collective-permute-start.7 = (f32[4,256,128]{2,1,0:T(8,128)S(1)}, f32[4,256,128]{2,1,0:T(8,128)S(1)}, u32[]{:S(2)}, u32[]{:S(2)}) collective-permute-start(f32[4,256,128]{2,1,0:T(8,128)S(1)} %get-tuple-element.50), channel_id=1, source_target_pairs={{1,2},{2,1},{3,4},{4,3},{5,6},{6,5},{7,8},{8,7},{9,10},{10,9},{11,... | collective-permute-start | bytes 1572872 | tf_op jit(solution)/shard_map/ppermute | solution.py:528
  95.2 28.4 %collective-permute-start.4 = (f32[4,256,128]{2,1,0:T(8,128)S(1)}, f32[4,256,128]{2,1,0:T(8,128)S(1)}, u32[]{:S(2)}, u32[]{:S(2)}) collective-permute-start(f32[4,256,128]{2,1,0:T(8,128)S(1)} %get-tuple-element.47), channel_id=1, source_target_pairs={{0,1},{1,0},{2,3},{3,2},{4,5},{5,4},{6,7},{7,6},{8,9},{9,8},{10,11... | collective-permute-start | bytes 1572872 | tf_op jit(solution)/shard_map/ppermute | solution.py:528
  95.3 28.4 %collective-permute-start.5 = (f32[4,256,128]{2,1,0:T(8,128)S(1)}, f32[4,256,128]{2,1,0:T(8,128)S(1)}, u32[]{:S(2)}, u32[]{:S(2)}) collective-permute-start(f32[4,256,128]{2,1,0:T(8,128)S(1)} %get-tuple-element.48), channel_id=1, source_target_pairs={{1,2},{2,1},{3,4},{4,3},{5,6},{6,5},{7,8},{8,7},{9,10},{10,9},{11,... | collective-permute-start | bytes 1572872 | tf_op jit(solution)/shard_map/ppermute | solution.py:528
  118.3 30.4 %collective-permute-start.10 = (f32[4,256,128]{2,1,0:T(8,128)S(1)}, f32[4,256,128]{2,1,0:T(8,128)S(1)}, u32[]{:S(2)}, u32[]{:S(2)}) collective-permute-start(f32[4,256,128]{2,1,0:T(8,128)S(1)} %get-tuple-element.55), channel_id=1, source_target_pairs={{0,1},{1,0},{2,3},{3,2},{4,5},{5,4},{6,7},{7,6},{8,9},{9,8},{10,11... | collective-permute-start | bytes 1572872 | tf_op jit(solution)/shard_map/ppermute | solution.py:528
  119.0 29.6 %collective-permute-start.11 = (f32[4,256,128]{2,1,0:T(8,128)S(1)}, f32[4,256,128]{2,1,0:T(8,128)S(1)}, u32[]{:S(2)}, u32[]{:S(2)}) collective-permute-start(f32[4,256,128]{2,1,0:T(8,128)S(1)} %get-tuple-element.56), channel_id=1, source_target_pairs={{1,2},{2,1},{3,4},{4,3},{5,6},{6,5},{7,8},{8,7},{9,10},{10,9},{11,... | collective-permute-start | bytes 1572872 | tf_op jit(solution)/shard_map/ppermute | solution.py:528
  126.0 24.9 %collective-permute-start.8 = (f32[4,256,128]{2,1,0:T(8,128)S(1)}, f32[4,256,128]{2,1,0:T(8,128)S(1)}, u32[]{:S(2)}, u32[]{:S(2)}) collective-permute-start(f32[4,256,128]{2,1,0:T(8,128)S(1)} %get-tuple-element.53), channel_id=1, source_target_pairs={{0,1},{1,0},{2,3},{3,2},{4,5},{5,4},{6,7},{7,6},{8,9},{9,8},{10,11... | collective-permute-start | bytes 1572872 | tf_op jit(solution)/shard_map/ppermute | solution.py:528
  126.1 24.9 %collective-permute-start.9 = (f32[4,256,128]{2,1,0:T(8,128)S(1)}, f32[4,256,128]{2,1,0:T(8,128)S(1)}, u32[]{:S(2)}, u32[]{:S(2)}) collective-permute-start(f32[4,256,128]{2,1,0:T(8,128)S(1)} %get-tuple-element.54), channel_id=1, source_target_pairs={{1,2},{2,1},{3,4},{4,3},{5,6},{6,5},{7,8},{8,7},{9,10},{10,9},{11,... | collective-permute-start | bytes 1572872 | tf_op jit(solution)/shard_map/ppermute | solution.py:528
  153.3 40.5 %slice-start = ((s8[8388608]{0:T(1024)(128)(4,1)}), s8[4194304]{0:T(1024)(128)(4,1)S(1)}, s32[]{:S(2)}) async-start(s8[8388608]{0:T(1024)(128)(4,1)} %bitcast.12), calls=%async_computation.1 | async-start | bytes 8388608
  172.7 36.6 %collective-permute-start.16 = (f32[8,2,64,256]{3,2,1,0:T(8,128)S(1)}, f32[8,2,64,256]{3,2,1,0:T(8,128)S(1)}, u32[]{:S(2)}, u32[]{:S(2)}) collective-permute-start(f32[8,2,64,256]{3,2,1,0:T(8,128)S(1)} %get-tuple-element.70), channel_id=1, source_target_pairs={{0,32},{32,0},{64,96},{96,64},{1,33},{33,1},{65,97},{97,65},{2,34}... | collective-permute-start | bytes 3145736 | tf_op jit(solution)/shard_map/ppermute | solution.py:556
  172.7 14.7 %collective-permute-start.14 = (f32[4,256,128]{2,1,0:T(8,128)S(1)}, f32[4,256,128]{2,1,0:T(8,128)S(1)}, u32[]{:S(2)}, u32[]{:S(2)}) collective-permute-start(f32[4,256,128]{2,1,0:T(8,128)S(1)} %get-tuple-element.62), channel_id=1, source_target_pairs={{0,1},{1,0},{2,3},{3,2},{4,5},{5,4},{6,7},{7,6},{8,9},{9,8},{10,11... | collective-permute-start | bytes 1572872 | tf_op jit(solution)/shard_map/ppermute | solution.py:528
  172.7 21.1 %collective-permute-start.15 = (f32[4,256,128]{2,1,0:T(8,128)S(1)}, f32[4,256,128]{2,1,0:T(8,128)S(1)}, u32[]{:S(2)}, u32[]{:S(2)}) collective-permute-start(f32[4,256,128]{2,1,0:T(8,128)S(1)} %get-tuple-element.63), channel_id=1, source_target_pairs={{1,2},{2,1},{3,4},{4,3},{5,6},{6,5},{7,8},{8,7},{9,10},{10,9},{11,... | collective-permute-start | bytes 1572872 | tf_op jit(solution)/shard_map/ppermute | solution.py:528
  177.3 21.1 %collective-permute-start.12 = (f32[4,256,128]{2,1,0:T(8,128)S(1)}, f32[4,256,128]{2,1,0:T(8,128)S(1)}, u32[]{:S(2)}, u32[]{:S(2)}) collective-permute-start(f32[4,256,128]{2,1,0:T(8,128)S(1)} %get-tuple-element.60), channel_id=1, source_target_pairs={{0,1},{1,0},{2,3},{3,2},{4,5},{5,4},{6,7},{7,6},{8,9},{9,8},{10,11... | collective-permute-start | bytes 1572872 | tf_op jit(solution)/shard_map/ppermute | solution.py:528
  177.9 26.7 %collective-permute-start.13 = (f32[4,256,128]{2,1,0:T(8,128)S(1)}, f32[4,256,128]{2,1,0:T(8,128)S(1)}, u32[]{:S(2)}, u32[]{:S(2)}) collective-permute-start(f32[4,256,128]{2,1,0:T(8,128)S(1)} %get-tuple-element.61), channel_id=1, source_target_pairs={{1,2},{2,1},{3,4},{4,3},{5,6},{6,5},{7,8},{8,7},{9,10},{10,9},{11,... | collective-permute-start | bytes 1572872 | tf_op jit(solution)/shard_map/ppermute | solution.py:528
  198.4 12.3 %collective-permute-start.18 = (f32[8,2,64,128]{3,2,1,0:T(8,128)S(1)}, f32[8,2,64,128]{3,2,1,0:T(8,128)S(1)}, u32[]{:S(2)}, u32[]{:S(2)}) collective-permute-start(f32[8,2,64,128]{3,2,1,0:T(8,128)S(1)} %bitcast.23), channel_id=1, source_target_pairs={{0,32},{32,0},{64,96},{96,64},{1,33},{33,1},{65,97},{97,65},{2,34}... | collective-permute-start | bytes 1572872 | tf_op jit(solution)/shard_map/ppermute | solution.py:566
  209.2 3.7 %collective-permute-start.20 = (f32[8,2,64,128]{3,2,1,0:T(8,128)S(1)}, f32[8,2,64,128]{3,2,1,0:T(8,128)S(1)}, u32[]{:S(2)}, u32[]{:S(2)}) collective-permute-start(f32[8,2,64,128]{3,2,1,0:T(8,128)S(1)} %bitcast.24), channel_id=1, source_target_pairs={{0,32},{32,0},{64,96},{96,64},{1,33},{33,1},{65,97},{97,65},{2,34}... | collective-permute-start | bytes 1572872 | tf_op jit(solution)/shard_map/ppermute | solution.py:566
  210.0 25.7 %collective-permute-start.17 = (f32[8,64,256]{2,1,0:T(8,128)S(1)}, f32[8,64,256]{2,1,0:T(8,128)S(1)}, u32[]{:S(2)}, u32[]{:S(2)}) collective-permute-start(f32[8,64,256]{2,1,0:T(8,128)S(1)} %get-tuple-element.72), channel_id=1, source_target_pairs={{0,64},{32,96},{64,0},{96,32},{1,65},{33,97},{65,1},{97,33},{2,66}... | collective-permute-start | bytes 1572872 | tf_op jit(solution)/shard_map/ppermute | solution.py:557
  211.5 19.0 %collective-permute-start.19 = (f32[8,64,128]{2,1,0:T(8,128)S(1)}, f32[8,64,128]{2,1,0:T(8,128)S(1)}, u32[]{:S(2)}, u32[]{:S(2)}) collective-permute-start(f32[8,64,128]{2,1,0:T(8,128)S(1)} %get-tuple-element.76), channel_id=1, source_target_pairs={{0,64},{32,96},{64,0},{96,32},{1,65},{33,97},{65,1},{97,33},{2,66}... | collective-permute-start | bytes 786440 | tf_op jit(solution)/shard_map/ppermute | solution.py:567
  213.7 22.0 %collective-permute-start.21 = (f32[8,64,128]{2,1,0:T(8,128)S(1)}, f32[8,64,128]{2,1,0:T(8,128)S(1)}, u32[]{:S(2)}, u32[]{:S(2)}) collective-permute-start(f32[8,64,128]{2,1,0:T(8,128)S(1)} %get-tuple-element.80), channel_id=1, source_target_pairs={{0,64},{32,96},{64,0},{96,32},{1,65},{33,97},{65,1},{97,33},{2,66}... | collective-permute-start | bytes 786440 | tf_op jit(solution)/shard_map/ppermute | solution.py:567
  (12 other events, 217.0 us)

commit v2 on v1

v2 whole, which is shorter than its diff:
```python
import functools

import jax
import jax.numpy as jnp
import ml_dtypes
import numpy as np
from jax import lax
from jax.experimental import pallas as pl
from jax.experimental.pallas import tpu as pltpu
from jax.sharding import PartitionSpec as P

PML = 16
STEPS = 4
COEFFS = (-205.0 / 72.0, 8.0 / 5.0, -1.0 / 5.0, 8.0 / 315.0, -1.0 / 560.0)
COURANT = 0.09
DAMP_MAX = 0.3
RATIO = tuple(c / COEFFS[1] for c in COEFFS)
SLAB = 16
SIZE = 256
HALF = 128
CAP = 64
MIB = 1 << 20

bf16 = jnp.bfloat16
f32 = jnp.float32
VMEM = pl.BlockSpec(memory_space=pltpu.VMEM)
SMEM = pl.BlockSpec(memory_space=pltpu.SMEM)
ANY = pl.BlockSpec(memory_space=pl.ANY)


def params(mib, dims=1):
    return pltpu.CompilerParams(
        vmem_limit_bytes=mib * MIB, dimension_semantics=("arbitrary",) * dims if dims else None
    )


def pinned(x):
    return pltpu.with_memory_space_constraint(x, pltpu.VMEM)


def in_hbm(x):
    return pltpu.with_memory_space_constraint(x, pltpu.HBM)


def cost(flops, mib):
    return pl.CostEstimate(flops=int(flops), bytes_accessed=int(mib * MIB), transcendentals=0)


def profile(index, count):
    depth = jnp.maximum(jnp.maximum(PML - index, index - (count - 1 - PML)), 0.0) / PML
    return depth * depth


def band():
    m = np.zeros((SIZE, SIZE), np.float32)
    for k in range(1, 5):
        m += RATIO[k] * (np.eye(SIZE, k=k, dtype=np.float32) + np.eye(SIZE, k=-k, dtype=np.float32))
    return m.astype(ml_dtypes.bfloat16)


def route_body(slabs, target_ref, cell_ref, trace_ref, out_ref, pick):
    listed = target_ref.shape[1]
    slots = slabs * CAP
    target = target_ref[...]
    hot = (lax.broadcasted_iota(jnp.int32, (slabs, listed), 0) == target).astype(bf16)
    earlier = (
        lax.broadcasted_iota(jnp.int32, (listed, listed), 0)
        < lax.broadcasted_iota(jnp.int32, (listed, listed), 1)
    ).astype(bf16)
    before = jnp.dot(hot, earlier, preferred_element_type=f32)
    rank = jnp.sum(before * hot.astype(f32), axis=0, keepdims=True)
    place = target * CAP + rank.astype(jnp.int32)
    value = trace_ref[...]
    top = value.astype(bf16)
    rest = value - top.astype(f32)
    middle = rest.astype(bf16)
    last = (rest - middle.astype(f32)).astype(bf16)
    cell = cell_ref[...]
    pieces = jnp.concatenate(
        [(cell >> 12).astype(f32), ((cell >> 4) & 255).astype(f32), (cell & 15).astype(f32), jnp.zeros((1, listed), f32)],
        axis=0,
    ).astype(bf16)
    table = jnp.concatenate([top, middle, last, pieces], axis=0)
    out_ref[...] = jnp.zeros_like(out_ref)
    chunk = pick.shape[0]
    for start in range(0, slots, chunk):
        pick[...] = (
            lax.broadcasted_iota(jnp.int32, (chunk, listed), 0) + start == place
        ).astype(f32).astype(bf16)
        got = lax.dot_general(
            table, pick[...], (((1,), (1,)), ((), ())), preferred_element_type=f32
        )
        values = got[0:4] + got[4:8] + got[8:12]
        cells = got[12:13] * 4096.0 + got[13:14] * 16.0 + got[14:15]
        block = jnp.concatenate([values, jnp.broadcast_to(cells, (4, chunk))], axis=0)
        for j in range(chunk // CAP):
            out_ref[start // CAP + j, :, 0:CAP] = block[:, j * CAP : (j + 1) * CAP]


def route(target, cell, trace, slabs):
    return pl.pallas_call(
        functools.partial(route_body, slabs),
        out_shape=jax.ShapeDtypeStruct((slabs, 8, 128), f32),
        scratch_shapes=[pltpu.VMEM((256, target.shape[1]), bf16)],
        compiler_params=params(10, 0),
        cost_estimate=cost(1, 0),
        name="route",
    )(target, cell, trace)


def inject_body(value_ref, dense, cells_vmem, cell_ref, sem):
    cells_vmem[...] = value_ref[:, 4, :].astype(jnp.int32)
    copy = pltpu.make_async_copy(cells_vmem, cell_ref, sem)
    copy.start()
    zero = jnp.zeros((256, 128), f32)

    @pl.loop(0, dense.shape[0] // 256)
    def _(i):
        dense[pl.ds(pl.multiple_of(i * 256, 256), 256), :] = zero

    copy.wait()
    position = lax.broadcasted_iota(jnp.int32, (8, 128), 1) + 128 * (
        lax.broadcasted_iota(jnp.int32, (8, 128), 0) >> 2
    )
    batch = 4

    @pl.loop(0, value_ref.shape[0])
    def _(source):
        tile = value_ref[source]
        eight = jnp.concatenate([tile[0:4], tile[0:4]], axis=0)

        def some(first):
            cells = [cell_ref[source, first + j] for j in range(batch)]
            rows = [c >> 8 for c in cells]
            add = [
                jnp.where(position == (c & 255), eight[:, first + j : first + j + 1], 0.0)
                for j, c in enumerate(cells)
            ]
            at = [pl.ds(pl.multiple_of(r * 8, 8), 8) for r in rows]
            total = [dense[a, :] + u for a, u in zip(at, add)]
            for j in range(batch):
                for i in range(j):
                    same = (rows[i] == rows[j]).astype(f32)
                    total[j] = total[j] + same * add[i]
            for j in range(batch):
                dense[at[j], :] = total[j]

        for first in range(0, CAP, batch):
            some(first)


def source_of(dense, plane, start, step):
    base = (plane * SIZE + start) * 8 + step
    return jnp.concatenate([dense[pl.ds(base + half * 4, 8, stride=8), :] for half in range(2)], axis=1)


def inject(values):
    return pl.pallas_call(
        inject_body,
        out_shape=pltpu.VMEM((SLAB * SIZE * 8, 128), f32),
        in_specs=[VMEM],
        out_specs=VMEM,
        scratch_shapes=[
            pltpu.VMEM((values.shape[0], 128), jnp.int32),
            pltpu.SMEM((values.shape[0], 128), jnp.int32),
            pltpu.SemaphoreType.DMA,
        ],
        compiler_params=params(4, 0),
        cost_estimate=cost(1, 0),
        name="inject",
    )(values)


def side_of(group, parity):
    return (group + parity + 1) % 2


def first_edges_body(scalar_ref, source, *refs):
    sems = refs[4]
    copies = []
    for i in range(4):
        half, group = divmod(i, 2)
        start = 12 * side_of(group, scalar_ref[0])
        copies.append(
            pltpu.make_async_copy(
                source.at[pl.ds(start, 4), :, pl.ds(half * HALF, HALF)], refs[i], sems.at[i]
            )
        )
    for copy in copies:
        copy.start()
    for copy in copies:
        copy.wait()


def first_edges(current, scalars):
    return pl.pallas_call(
        first_edges_body,
        out_shape=[jax.ShapeDtypeStruct((4, SIZE, HALF), f32)] * 4,
        in_specs=[SMEM, ANY],
        out_specs=[VMEM] * 4,
        scratch_shapes=[pltpu.SemaphoreType.DMA((4,))],
        compiler_params=params(4, 0),
        cost_estimate=cost(1, 0),
        name="first_edges",
    )(scalars, in_hbm(current))


def factor(speed, damp):
    inverse = 1.0 / (1.0 + damp)
    return inverse, (COURANT * COURANT) * (speed * speed) * inverse


def local_body(step, scalar_ref, damp_x_ref, q_hbm, p_hbm, v_hbm, s_ref, damp_ref, band_ref, *rest):
    if step < 2:
        n_hbm, edge_ref, gain_ref, *scratch = rest
    elif step == 2:
        accel_hbm, n_hbm, edge_ref, gain_ref, part_hbm, *scratch = rest
    else:
        accel_hbm, part_hbm, n_hbm, loc_ref, *scratch = rest
        (send_ref, keep_ref), scratch = scratch[:2], scratch[2:]
    high, low, mixed0, mixed1, q_ref, n_ref, v_ref, load_sems, store_sems = scratch[:9]
    if step >= 2:
        accel, accel_sems, part, part_sems = scratch[9:13]
    if step == 3:
        shared = scratch[13]
    p_ref = n_ref
    mixed = (mixed0, mixed1)
    group_size = 4
    groups = SLAB // group_size
    span = SIZE // group_size
    rows = 8 if step < 2 else 16
    core = scalar_ref[1]
    first = 0 if step == 2 else 2

    def planes(group):
        return pl.ds(group_size * group, group_size)

    def load(i, group):
        source, target = ((q_hbm, q_ref), (v_hbm, v_ref), (p_hbm, p_ref))[i]
        return pltpu.make_async_copy(
            source.at[planes(group)], target.at[planes(group)], load_sems.at[i, group]
        )

    def fetch(group):
        return pltpu.make_async_copy(
            accel_hbm.at[0, pl.ds(first, 2), planes(group)], accel.at[group], accel_sems.at[group]
        )

    def load_part(group):
        return pltpu.make_async_copy(
            part_hbm.at[planes(group)], part.at[planes(group)], part_sems.at[group]
        )

    def stores(group):
        out = [pltpu.make_async_copy(n_ref.at[planes(group)], n_hbm.at[planes(group)], store_sems.at[group])]
        if step == 2:
            out.append(
                pltpu.make_async_copy(
                    part.at[planes(group)], part_hbm.at[planes(group)], part_sems.at[group]
                )
            )
        return out

    def others(group):
        out = [load(1, group), load(2, group)]
        if step >= 2:
            out.append(fetch(group))
        if step == 3:
            out.append(load_part(group))
        return out

    load(0, 0).start()
    for group in range(groups):
        if group + 1 < groups:
            load(0, group + 1).start()
        for copy in others(group):
            copy.start()
    load(0, 0).wait()

    def prepare(plane, into):
        here = q_ref[plane]
        top = here.astype(bf16)
        high[...] = top
        low[...] = (here - top.astype(f32)).astype(bf16)
        matrix = band_ref[...]
        into[...] = (
            jnp.dot(high[...], matrix, preferred_element_type=f32)
            + jnp.dot(low[...], matrix, preferred_element_type=f32)
            + jnp.dot(matrix, high[...], preferred_element_type=f32)
            + jnp.dot(matrix, low[...], preferred_element_type=f32)
        )

    def update(group, whole, offset):
        start = pl.multiple_of(whole + offset, rows)
        row = pl.ds(start, rows)
        lowest = group_size * group
        field = {x: q_ref[x, row, :] for x in range(max(0, lowest - 4), min(SLAB, lowest + group_size + 4))}
        damp = damp_ref[row, :]
        for plane in range(lowest, lowest + group_size):

            def rate(t):
                return accel[group, t, plane - lowest, row, :].astype(f32)

            around = mixed[group % 2][plane - lowest, row, :]
            for k in range(1, 5):
                both = [field[x] for x in (plane - k, plane + k) if 0 <= x < SLAB]
                term = both[0] if len(both) == 1 else both[0] + both[1]
                around = around + (term if k == 1 else RATIO[k] * term)
            now = field[plane]
            before = p_ref[plane, row, :]
            speed = v_ref[plane, row, :]
            inverse, gain = factor(speed, damp + damp_x_ref[plane])
            laplace = (3.0 * COEFFS[0]) * now + COEFFS[1] * around
            laplace = laplace + jnp.concatenate(
                [source_of(s_ref, plane, start + i * 8, step) for i in range(rows // 8)], axis=0
            )
            after = before + (2.0 * inverse) * (now - before) + gain * laplace
            n_ref[plane, row, :] = after
            if step == 2:
                part[plane, row, :] = before * rate(0) + now * rate(1)
            if step == 3:
                total = part[plane, row, :] + now * rate(0) + after * rate(1)
                grad = total * (2.0 / (speed * speed * speed))
                if plane < 4 or plane >= SLAB - 4:
                    loc_ref[plane if plane < 4 else plane - 8, row, :] = grad
                else:
                    shared[plane - lowest, pl.ds(start - whole, rows), :] = grad
            elif plane < 4 or plane >= SLAB - 4:
                edge_ref[plane if plane < 4 else plane - 8, row, :] = after
                gain_ref[plane if plane < 4 else plane - 8, row, :] = gain

    for plane in range(group_size):
        prepare(plane, mixed0.at[plane])
    for group in range(groups):
        if group + 1 < groups:
            load(0, group + 1).wait()
        for copy in others(group):
            copy.wait()

        @pl.loop(0, group_size)
        def _(j):
            if group + 1 < groups:
                prepare(group_size * (group + 1) + j, mixed[(group + 1) % 2].at[j])
            for i in range(span // rows):
                update(group, j * span, i * rows)
            if step == 3 and 0 < group < groups - 1:
                inner = pl.ds(group_size * (group - 1), group_size)

                @pl.when((j & 1) == core)
                def _():
                    keep_ref[inner, j >> 1] = shared[...]

                @pl.when((j & 1) != core)
                def _():
                    send_ref[inner, j >> 1] = shared[...]

        for copy in stores(group):
            copy.start()
    for group in range(groups):
        for copy in stores(group):
            copy.wait()


def local_step(step, scalars, damp_x, q, p, v, s, damp, accel, part=None):
    whole = (SLAB, SIZE, SIZE)
    in_specs = [SMEM, SMEM] + [ANY] * 3 + [VMEM] * 3
    operands = [scalars, damp_x, in_hbm(q), in_hbm(p), in_hbm(v), pinned(s), damp, jnp.asarray(band())]
    out_specs = [ANY]
    out_shape = [pltpu.HBM(whole, f32)]
    scratch = [
        pltpu.VMEM((SIZE, SIZE), bf16),
        pltpu.VMEM((SIZE, SIZE), bf16),
        pltpu.VMEM((4, SIZE, SIZE), f32),
        pltpu.VMEM((4, SIZE, SIZE), f32),
        pltpu.VMEM(whole, f32),
        pltpu.VMEM(whole, f32),
        pltpu.VMEM(whole, f32),
        pltpu.SemaphoreType.DMA((3, 4)),
        pltpu.SemaphoreType.DMA((4,)),
    ]
    if step >= 2:
        in_specs.append(ANY)
        operands.append(in_hbm(accel))
        scratch += [
            pltpu.VMEM((4, 2, 4, SIZE, SIZE), bf16),
            pltpu.SemaphoreType.DMA((4,)),
            pltpu.VMEM(whole, f32),
            pltpu.SemaphoreType.DMA((4,)),
        ]
    if step < 3:
        out_specs += [VMEM] * 2
        out_shape += [jax.ShapeDtypeStruct((8, SIZE, SIZE), f32)] * 2
    if step == 2:
        out_specs.append(ANY)
        out_shape.append(pltpu.HBM(whole, f32))
    if step == 3:
        in_specs.append(ANY)
        operands.append(in_hbm(part))
        out_specs += [VMEM] * 3
        out_shape.append(jax.ShapeDtypeStruct((8, SIZE, SIZE), f32))
        out_shape += [jax.ShapeDtypeStruct((8, 2, 64, SIZE), f32)] * 2
        scratch.append(pltpu.VMEM((4, 64, SIZE), f32))
    return pl.pallas_call(
        functools.partial(local_body, step),
        out_shape=out_shape,
        in_specs=in_specs,
        out_specs=out_specs,
        scratch_shapes=scratch,
        compiler_params=params(24, 0),
        cost_estimate=cost(4e9, 20),
        name=f"local_step{step}",
    )(*operands)


def halo_weights(upper):
    return [
        [
            jnp.where(
                upper == 1,
                COEFFS[4 + m - j] if m <= j else 0.0,
                COEFFS[4 + j - m] if m >= j else 0.0,
            ).astype(f32)
            for m in range(4)
        ]
        for j in range(4)
    ]


def edge_body(half, scalar_ref, even_ref, odd_ref, edge_ref, gain_ref, _, n_hbm, e_ref, o_ref, sems):
    rows = 16
    lanes = slice(half * HALF, (half + 1) * HALF)
    copies = []
    for group in range(2):
        upper = side_of(group, scalar_ref[0])
        halo_ref, out_ref = ((even_ref, e_ref), (odd_ref, o_ref))[group]
        weights = halo_weights(upper)

        @pl.loop(0, SIZE // rows)
        def _(i):
            row = pl.ds(pl.multiple_of(i * rows, rows), rows)
            halo = [halo_ref[m, row, :] for m in range(4)]
            for j in range(4):
                across = weights[j][0] * halo[0]
                for m in range(1, 4):
                    across = across + weights[j][m] * halo[m]
                layer = upper * 4 + j
                out_ref[j, row, :] = edge_ref[layer, row, lanes] + gain_ref[layer, row, lanes] * across

        copies.append(
            pltpu.make_async_copy(
                out_ref, n_hbm.at[pl.ds(12 * upper, 4), :, pl.ds(half * HALF, HALF)], sems.at[group]
            )
        )
        copies[-1].start()
    for copy in copies:
        copy.wait()


def edge_step(half, scalars, even, odd, edge, gain, n):
    return pl.pallas_call(
        functools.partial(edge_body, half),
        out_shape=[pltpu.HBM((SLAB, SIZE, SIZE), f32)] + [jax.ShapeDtypeStruct((4, SIZE, HALF), f32)] * 2,
        in_specs=[SMEM] + [VMEM] * 4 + [ANY],
        out_specs=[ANY, VMEM, VMEM],
        scratch_shapes=[pltpu.SemaphoreType.DMA((2,))],
        input_output_aliases={5: 0},
        compiler_params=params(12, 0),
        cost_estimate=cost(1, 0),
        name=f"edge_step{half}",
    )(scalars, even, odd, edge, gain, in_hbm(n))


def last_edge_body(
    scalar_ref, damp_x_ref, even_ref, odd_ref, n_in, v_ref, damp_ref, a_ref, loc_ref, n_ref, send_ref, keep_ref, grad
):
    group = pl.program_id(0)
    upper = side_of(group, scalar_ref[0])
    core = scalar_ref[1]
    rows = 16
    weights = halo_weights(upper)

    def run(halo_ref):
        @pl.loop(0, HALF // rows)
        def _(i):
            row = pl.ds(pl.multiple_of(i * rows, rows), rows)
            halo = [halo_ref[m, row, :] for m in range(4)]
            damp = damp_ref[row, :]
            for j in range(4):
                speed = v_ref[j, row, :]
                _, gain = factor(speed, damp + damp_x_ref[upper * 12 + j])
                across = weights[j][0] * halo[0]
                for m in range(1, 4):
                    across = across + weights[j][m] * halo[m]
                extra = gain * across
                after = n_in[j, row, :] + extra
                n_ref[j, row, :] = after
                grad[j, row, :] = loc_ref[j, row, :] + extra * a_ref[0, 0, j, row, :].astype(f32) * (
                    2.0 / (speed * speed * speed)
                )

    @pl.when(group == 0)
    def _():
        run(even_ref)

    @pl.when(group == 1)
    def _():
        run(odd_ref)

    send_ref[0, :, 0] = grad[:, pl.ds(pl.multiple_of(64 * (1 - core), 64), 64), :]
    keep_ref[0, :, 0] = grad[:, pl.ds(pl.multiple_of(64 * core, 64), 64), :]


def last_edge_step(half, scalars, damp_x, even, odd, n, v, damp, accel, loc):
    block = (4, HALF, HALF)

    def edge_block(g, y, s, _):
        return (3 * side_of(g, s[0]), y, half)

    edge_spec = pl.BlockSpec(block, edge_block)
    in_specs = [
        pl.BlockSpec(block, lambda g, y, *_: (0, jnp.where(g == 0, y, 1), 0)),
        pl.BlockSpec(block, lambda g, y, *_: (0, jnp.where(g == 0, 0, y), 0)),
        edge_spec,
        edge_spec,
        pl.BlockSpec((HALF, HALF), lambda g, y, *_: (y, half)),
        pl.BlockSpec((1, 1) + block, lambda g, y, s, _: (0, 3, 3 * side_of(g, s[0]), y, half)),
        pl.BlockSpec(block, lambda g, y, s, _: (side_of(g, s[0]), y, half)),
    ]
    quarter = pl.BlockSpec((1, 4, 1, 64, HALF), lambda g, y, *_: (g, 0, y, 0, 0))
    return pl.pallas_call(
        last_edge_body,
        out_shape=[jax.ShapeDtypeStruct((SLAB, SIZE, SIZE), f32)]
        + [jax.ShapeDtypeStruct((2, 4, 2, 64, HALF), f32)] * 2,
        grid_spec=pltpu.PrefetchScalarGridSpec(
            num_scalar_prefetch=2,
            grid=(2, 2),
            in_specs=in_specs,
            out_specs=[edge_spec, quarter, quarter],
            scratch_shapes=[pltpu.VMEM(block, f32)],
        ),
        input_output_aliases={4: 0},
        compiler_params=params(7, 2),
        cost_estimate=cost(1, 0),
        name=f"last_edge_step{half}",
    )(scalars, damp_x, even, odd, in_hbm(n), in_hbm(v), damp, in_hbm(accel), loc)


def split_body(scalar_ref, got_ref, own_ref, send_ref, keep_ref):
    y = scalar_ref[2]
    send_ref[0] = got_ref[0, 1 - y] + own_ref[0, 1 - y]
    keep_ref[0] = got_ref[0, y] + own_ref[0, y]


def split_sum(scalars, got, own):
    layers, _, rows, width = got.shape
    step = pl.BlockSpec((1, 2, rows, width), lambda i, s: (i, 0, 0, 0))
    out = pl.BlockSpec((1, rows, width), lambda i, s: (i, 0, 0))
    return pl.pallas_call(
        split_body,
        out_shape=[jax.ShapeDtypeStruct((layers, rows, width), f32)] * 2,
        grid_spec=pltpu.PrefetchScalarGridSpec(
            num_scalar_prefetch=1, grid=(layers,), in_specs=[step, step], out_specs=[out, out]
        ),
        compiler_params=params(4),
        cost_estimate=cost(1, 0),
        name="split_sum",
    )(scalars, got, own)


def gather_body(scalar_ref, *refs):
    inner_a, inner_b, first_a, first_b, second_a, second_b, out_ref = refs
    block = pl.program_id(0)
    inside = jnp.logical_or(block == 1, block == 2)

    @pl.when(inside)
    def _():
        out_ref[...] = inner_a[...] + inner_b[...]

    @pl.when(jnp.logical_not(inside))
    def _():
        out_ref[:, :, 0:HALF] = first_a[...] + first_b[...]
        out_ref[:, :, HALF:SIZE] = second_a[...] + second_b[...]


def gather_sum(scalars, inner, first, second):
    inner_spec = pl.BlockSpec((4, 64, SIZE), lambda i, s: (jnp.clip(i - 1, 0, 1), 0, 0))

    def group(i, s):
        upper = (i == 3).astype(jnp.int32)
        return (upper + s[0] + 1) % 2, 0, 0

    edge_spec = pl.BlockSpec((4, 64, HALF), group)
    return pl.pallas_call(
        gather_body,
        out_shape=jax.ShapeDtypeStruct((SLAB, 64, SIZE), f32),
        grid_spec=pltpu.PrefetchScalarGridSpec(
            num_scalar_prefetch=1,
            grid=(4,),
            in_specs=[inner_spec] * 2 + [edge_spec] * 4,
            out_specs=pl.BlockSpec((4, 64, SIZE), lambda i, s: (i, 0, 0)),
        ),
        compiler_params=params(4),
        cost_estimate=cost(1, 0),
        name="gather_sum",
    )(scalars, *inner, *first, *second)


def shards(velocity, adjoint_now, adjoint_prev, forward_accel, traces, receiver_sub, receiver_cell):
    slabs = lax.axis_size("sub")
    slab = lax.axis_index("sub")
    shot = lax.axis_index("shot")
    pairs_even = [(i, i ^ 1) for i in range(slabs)]
    pairs_odd = [pair for a in range(1, slabs - 1, 2) for pair in ((a, a + 1), (a + 1, a))]
    shots = lax.axis_size("shot")
    swap_core = [(i, i ^ 1) for i in range(shots)]
    swap_row = [(i, i ^ 2) for i in range(shots)]
    scalars = jnp.stack([slab % 2, shot % 2, shot // 2]).astype(jnp.int32)
    start_x = (slab * SLAB).astype(f32)
    damp_x = DAMP_MAX * profile(start_x + jnp.arange(SLAB, dtype=f32), SLAB * slabs)
    line = profile(jnp.arange(SIZE, dtype=f32), SIZE)
    damp = DAMP_MAX * (line[:, None] + line[None, :])

    def exchange(even, odd):
        return lax.ppermute(even, "sub", pairs_even), lax.ppermute(odd, "sub", pairs_odd)

    even_a, odd_a, even_b, odd_b = first_edges(adjoint_now[0], scalars)
    arrived_a = exchange(even_a, odd_a)
    arrived_b = exchange(even_b, odd_b)

    listed = receiver_sub.shape[1]
    sent = route(
        receiver_sub.reshape(1, listed), receiver_cell.reshape(1, listed), traces[0], slabs
    )
    got = lax.all_to_all(sent, "sub", split_axis=0, concat_axis=0, tiled=True)

    source = inject(got)

    current = adjoint_now[0]
    previous = adjoint_prev[0]
    part = []
    for step in range(STEPS):
        last = step == STEPS - 1
        after, *extra = local_step(
            step, scalars, damp_x, current, previous, velocity, source, damp, forward_accel, *part
        )
        outs = []
        if last:
            loc, inner_send, inner_keep = extra
            arrived_a, arrived_b = lax.optimization_barrier((arrived_a, arrived_b))
        else:
            edge, gain, *part = extra
        for half, arrived in enumerate((arrived_a, arrived_b)):
            if last:
                after, x, y = last_edge_step(
                    half, scalars, damp_x, *arrived, after, velocity, damp, forward_accel, loc
                )
                if half == 0:
                    inner_send, x = lax.optimization_barrier((inner_send, x))
                    send, inner_keep = split_sum(scalars, lax.ppermute(inner_send, "shot", swap_core), inner_keep)
                    send, after = lax.optimization_barrier((send, after))
                    inner = (lax.ppermute(send, "shot", swap_row), inner_keep)
                x = x.reshape(8, 2, 64, HALF)
                y = y.reshape(8, 2, 64, HALF)
                send, edge_keep = split_sum(scalars, lax.ppermute(x, "shot", swap_core), y)
                outs.append((lax.ppermute(send, "shot", swap_row), edge_keep))
            else:
                after, x, y = edge_step(half, scalars, *arrived, edge, gain, after)
                outs.append(exchange(x, y))
        previous = current
        current = after
        if not last:
            arrived_a, arrived_b = outs
    share = gather_sum(scalars, inner, *outs)
    return current[None], share


def solution(mesh):
    in_specs = (
        P("sub", None, None),
        P("shot", "sub", None, None),
        P("shot", "sub", None, None),
        P("shot", None, "sub", None, None),
        P("shot", None, "sub"),
        P("shot", "sub", None),
        P("shot", "sub"),
    )
    out_specs = (P("shot", "sub", None, None), P("sub", "shot", None))
    return jax.shard_map(shards, mesh=mesh, in_specs=in_specs, out_specs=out_specs, check_vma=False)
```

time: 240 us -> 183 us (0.76)
  Pallas kernels: 119 us -> 93.1 us
  waiting for transfers between devices: 49.1 us -> 26.6 us
  local copies, waits for them, and re-layouts: 9.48 us -> 2.09 us
    pallas_call x4, Pallas kernels: 67.3 us -> 51.3 us  [local_step(): pl.pallas_call(functools.partial(local_body, step), out_shape=out_shape,...]
    pallas_call x9, Pallas kernels: 43 us -> 31.8 us  [the longest x6 11.5 us: edge_step(): pl.pallas_call(functools.partial(edge_body, half), out_shape=[pltpu.HBM((...]
    all_to_all x1, waiting for transfers between devices: 10.9 us -> 0.01 us  [shards(): got = lax.all_to_all(sent, 'sub', split_axis=0, concat_axis=0, tiled=True)]
    ppermute x8, waiting for transfers between devices: 12.6 us -> 3.41 us  [exchange(): lax.ppermute(odd, 'sub', pairs_odd)]
    unnamed x28 -> x8, local copies, waits for them, and re-layouts: 8.83 us -> 2.09 us
    ppermute x8, waiting for transfers between devices: 4.27 us -> 0.02 us  [exchange(): lax.ppermute(even, 'sub', pairs_even)]
  transfers between devices with their start and end apart: 23 -> 23, of which waited for: 6 -> 5; matrix products, arithmetic and copies ran while one was open for 1% -> 0% of each run, Pallas kernels for 39% -> 45%
where the time goes in v2:
time: 183 us; the launch traced here: 182 us
  Pallas kernels  93.1 us (51%)
  starting transfers between devices  58.9 us (32%)
  waiting for transfers between devices  26.6 us (15%)
  local copies, waits for them, and re-layouts  2.09 us (1%)
    pallas_call x4, Pallas kernels, local_step(): pl.pallas_call(functools.partial(local_body, step), out_shape=out_shape,...  51.3 us
    ppermute x8, starting transfers between devices, exchange(): lax.ppermute(odd, 'sub', pairs_odd)  41.4 us
    ppermute x2, waiting for transfers between devices, shards(): outs.append((lax.ppermute(send, 'shot', swap_row), edge_keep))  21.1 us
    pallas_call x6, Pallas kernels, edge_step(): pl.pallas_call(functools.partial(edge_body, half), out_shape=[pltpu.HBM((...  11.5 us
    all_to_all x1, starting transfers between devices, shards(): got = lax.all_to_all(sent, 'sub', split_axis=0, concat_axis=0, tiled=True)  11.1 us
    pallas_call x1, Pallas kernels, inject(): pl.pallas_call(inject_body, out_shape=pltpu.VMEM((SLAB * SIZE * 8, 128),...  10.6 us
    pallas_call x2, Pallas kernels, last_edge_step(): pl.pallas_call(last_edge_body, out_shape=[jax.ShapeDtypeStruct((SLAB, SIZ...  9.77 us
  transfers between devices with their start and end apart: 23, of which 5 were waited for; matrix products, arithmetic and copies ran while one was open for 0% of the time, Pallas kernels for 45%

profile of v2, /device:TPU:2, one launch (start us, length us, event | category | flops | bytes accessed | tf_op | source)
XLA Modules:
  0.0 182.0 jit_solution(12458505235292376734)
XLA Ops:
  2.7 2.3 %route.1 = f32[32,8,128]{2,1,0:T(8,128)} custom-call(s32[1,1024]{1,0:T(1,128)S(1)} %bitcast.15, s32[1,1024]{1,0:T(1,128)S(1)} %copy-done.3, f32[4,1024]{1,0:T(4,128)S(1)} %bitcast.14), custom_call_target="tpu_custom_call" | custom-call | flops 1 | tf_op jit(solution)/shard_map/route/pallas_call | solution.py:101
  5.0 11.1 %all-to-all-start = ((f32[32,8,128]{2,1,0:T(8,128)}), f32[32,8,128]{2,1,0:T(8,128)S(1)}, u32[]{:S(2)}, u32[]{:S(2)}) async-start(f32[32,8,128]{2,1,0:T(8,128)} %route.1), calls=%async_computation | async-start | bytes 262144 | tf_op jit(solution)/shard_map/all_to_all | solution.py:634
  16.3 3.3 %first_edges.1 = (f32[4,256,128]{2,1,0:T(8,128)}, f32[4,256,128]{2,1,0:T(8,128)}, f32[4,256,128]{2,1,0:T(8,128)}, f32[4,256,128]{2,1,0:T(8,128)S(1)}) custom-call(s32[3]{0:T(128)S(1)} %pad_add_fusion.scalar_ref, f32[16,256,256]{2,1,0:T(8,128)} %bitcast.18), custom_call_target="tpu_custom_call" | custom-call | flops 1 | tf_op jit(solution)/shard_map/first_edges/pallas_call | solution.py:196
  21.1 6.4 %collective-permute-start.1 = (f32[4,256,128]{2,1,0:T(8,128)}, f32[4,256,128]{2,1,0:T(8,128)S(1)}, u32[]{:S(2)}, u32[]{:S(2)}) collective-permute-start(f32[4,256,128]{2,1,0:T(8,128)} %get-tuple-element.59), channel_id=1, source_target_pairs={{1,2},{2,1},{3,4},{4,3},{5,6},{6,5},{7,8},{8,7},{9,10},{10,9},{11,... | collective-permute-start | bytes 1572872 | tf_op jit(solution)/shard_map/ppermute | solution.py:624
  27.5 4.0 %collective-permute-start.5 = (f32[4,256,128]{2,1,0:T(8,128)S(1)}, f32[4,256,128]{2,1,0:T(8,128)S(1)}, u32[]{:S(2)}, u32[]{:S(2)}) collective-permute-start(f32[4,256,128]{2,1,0:T(8,128)S(1)} %get-tuple-element.66), channel_id=1, source_target_pairs={{1,2},{2,1},{3,4},{4,3},{5,6},{6,5},{7,8},{8,7},{9,10},{10,9},{11,... | collective-permute-start | bytes 1572872 | tf_op jit(solution)/shard_map/ppermute | solution.py:624
  31.7 10.6 %inject.1.s_ref = f32[32768,128]{1,0:T(8,128)S(1)} custom-call(f32[32,8,128]{2,1,0:T(8,128)S(1)} %all-to-all-done.value_ref), custom_call_target="tpu_custom_call" | custom-call | flops 1 | tf_op jit(solution)/shard_map/inject/pallas_call | solution.py:158
  42.3 11.2 %local_step0.1 = (f32[16,256,256]{2,1,0:T(8,128)}, f32[8,256,256]{2,1,0:T(8,128)S(1)}, f32[8,256,256]{2,1,0:T(8,128)S(1)}) custom-call(s32[3]{0:T(128)S(1)} %pad_add_fusion.scalar_ref, f32[16]{0:T(128)S(1)} %multiply_multiply_fusion.damp_x_ref, f32[16,256,256]{2,1,0:T(8,128)} %bitcast.19, f32[16,256,256]{2,1,0:T(8,128)} %bitcast.22, f32[16,256,256]{2,1,0:T(8,128)} %v_ref.3, ...), custom_call_target="tpu_custom_call" | custom-call | flops 4000000000 | bytes 20971520 | tf_op jit(solution)/shard_map/local_step0/pallas_call | solution.py:403
  56.0 5.9 %collective-permute-start.3 = (f32[4,256,128]{2,1,0:T(8,128)S(1)}, f32[4,256,128]{2,1,0:T(8,128)S(1)}, u32[]{:S(2)}, u32[]{:S(2)}) collective-permute-start(f32[4,256,128]{2,1,0:T(8,128)S(1)} %get-tuple-element.64), channel_id=1, source_target_pairs={{1,2},{2,1},{3,4},{4,3},{5,6},{6,5},{7,8},{8,7},{9,10},{10,9},{11,... | collective-permute-start | bytes 1572872 | tf_op jit(solution)/shard_map/ppermute | solution.py:624
  63.9 4.5 %collective-permute-start.9 = (f32[4,256,128]{2,1,0:T(8,128)S(1)}, f32[4,256,128]{2,1,0:T(8,128)S(1)}, u32[]{:S(2)}, u32[]{:S(2)}) collective-permute-start(f32[4,256,128]{2,1,0:T(8,128)S(1)} %get-tuple-element.75), channel_id=1, source_target_pairs={{1,2},{2,1},{3,4},{4,3},{5,6},{6,5},{7,8},{8,7},{9,10},{10,9},{11,... | collective-permute-start | bytes 1572872 | tf_op jit(solution)/shard_map/ppermute | solution.py:624
  68.3 11.2 %local_step1.1 = (f32[16,256,256]{2,1,0:T(8,128)}, f32[8,256,256]{2,1,0:T(8,128)S(1)}, f32[8,256,256]{2,1,0:T(8,128)S(1)}) custom-call(s32[3]{0:T(128)S(1)} %pad_add_fusion.scalar_ref, f32[16]{0:T(128)S(1)} %multiply_multiply_fusion.damp_x_ref, f32[16,256,256]{2,1,0:T(8,128)} %get-tuple-element.68.q_hbm.p_hbm, f32[16,256,256]{2,1,0:T(8,128)} %bitcast.20, ...), custom_call_target="tpu_custom_call" | custom-call | flops 4000000000 | bytes 20971520 | tf_op jit(solution)/shard_map/local_step1/pallas_call | solution.py:403
  79.6 1.9 %edge_step0.4 = (f32[16,256,256]{2,1,0:T(8,128)}, f32[4,256,128]{2,1,0:T(8,128)S(1)}, f32[4,256,128]{2,1,0:T(8,128)S(1)}) custom-call(s32[3]{0:T(128)S(1)} %pad_add_fusion.scalar_ref, f32[4,256,128]{2,1,0:T(8,128)S(1)} %collective-permute-done.2.even_ref, f32[4,256,128]{2,1,0:T(8,128)S(1)} %collective-permute-done.3.odd_ref, ...), custom_call_target="tpu_custom_call", output_to_operand_aliasing={{0}: (5, {})} | custom-call | flops 1 | tf_op jit(solution)/shard_map/edge_step0/pallas_call | solution.py:460
  81.6 5.9 %collective-permute-start.7 = (f32[4,256,128]{2,1,0:T(8,128)S(1)}, f32[4,256,128]{2,1,0:T(8,128)S(1)}, u32[]{:S(2)}, u32[]{:S(2)}) collective-permute-start(f32[4,256,128]{2,1,0:T(8,128)S(1)} %get-tuple-element.73), channel_id=1, source_target_pairs={{1,2},{2,1},{3,4},{4,3},{5,6},{6,5},{7,8},{8,7},{9,10},{10,9},{11,... | collective-permute-start | bytes 1572872 | tf_op jit(solution)/shard_map/ppermute | solution.py:624
  89.5 4.5 %collective-permute-start.13 = (f32[4,256,128]{2,1,0:T(8,128)S(1)}, f32[4,256,128]{2,1,0:T(8,128)S(1)}, u32[]{:S(2)}, u32[]{:S(2)}) collective-permute-start(f32[4,256,128]{2,1,0:T(8,128)S(1)} %get-tuple-element.84), channel_id=1, source_target_pairs={{1,2},{2,1},{3,4},{4,3},{5,6},{6,5},{7,8},{8,7},{9,10},{10,9},{11,... | collective-permute-start | bytes 1572872 | tf_op jit(solution)/shard_map/ppermute | solution.py:624
  94.1 14.2 %local_step2.1 = (f32[16,256,256]{2,1,0:T(8,128)}, f32[8,256,256]{2,1,0:T(8,128)S(1)}, f32[8,256,256]{2,1,0:T(8,128)S(1)}, f32[16,256,256]{2,1,0:T(8,128)}) custom-call(s32[3]{0:T(128)S(1)} %pad_add_fusion.scalar_ref, f32[16]{0:T(128)S(1)} %multiply_multiply_fusion.damp_x_ref, f32[16,256,256]{2,1,0:T(8,128)} %get-tuple-element.77.q_hbm.p_hbm, ...), custom_call_target="tpu_custom_call" | custom-call | flops 4000000000 | bytes 20971520 | tf_op jit(solution)/shard_map/local_step2/pallas_call | solution.py:403
  112.5 6.4 %collective-permute-start.15 = (f32[4,256,128]{2,1,0:T(8,128)S(1)}, f32[4,256,128]{2,1,0:T(8,128)S(1)}, u32[]{:S(2)}, u32[]{:S(2)}) collective-permute-start(f32[4,256,128]{2,1,0:T(8,128)S(1)} %get-tuple-element.87), channel_id=1, source_target_pairs={{1,2},{2,1},{3,4},{4,3},{5,6},{6,5},{7,8},{8,7},{9,10},{10,9},{11,... | collective-permute-start | bytes 1572872 | tf_op jit(solution)/shard_map/ppermute | solution.py:624
  119.2 4.0 %collective-permute-start.11 = (f32[4,256,128]{2,1,0:T(8,128)S(1)}, f32[4,256,128]{2,1,0:T(8,128)S(1)}, u32[]{:S(2)}, u32[]{:S(2)}) collective-permute-start(f32[4,256,128]{2,1,0:T(8,128)S(1)} %get-tuple-element.82), channel_id=1, source_target_pairs={{1,2},{2,1},{3,4},{4,3},{5,6},{6,5},{7,8},{8,7},{9,10},{10,9},{11,... | collective-permute-start | bytes 1572872 | tf_op jit(solution)/shard_map/ppermute | solution.py:624
  123.2 14.8 %local_step3.1 = (f32[16,256,256]{2,1,0:T(8,128)}, f32[8,256,256]{2,1,0:T(8,128)S(1)}, f32[8,2,64,256]{3,2,1,0:T(8,128)S(1)}, f32[8,2,64,256]{3,2,1,0:T(8,128)S(1)}) custom-call(s32[3]{0:T(128)S(1)} %pad_add_fusion.scalar_ref, f32[16]{0:T(128)S(1)} %multiply_multiply_fusion.damp_x_ref, f32[16,256,256]{2,1,0:T(8,128)} %get-tuple-element.90.q_hbm, ...), custom_call_target="tpu_custom_call" | custom-call | flops 4000000000 | bytes 20971520 | tf_op jit(solution)/shard_map/local_step3/pallas_call | solution.py:403
  138.0 3.1 %collective-permute-done.11.odd_ref = f32[4,256,128]{2,1,0:T(8,128)S(1)} collective-permute-done((f32[4,256,128]{2,1,0:T(8,128)S(1)}, f32[4,256,128]{2,1,0:T(8,128)S(1)}, u32[]{:S(2)}, u32[]{:S(2)}) %collective-permute-start.11) | collective-permute-done | bytes 524320 | tf_op jit(solution)/shard_map/ppermute | solution.py:624
  141.1 4.9 %last_edge_step0.1 = (f32[16,256,256]{2,1,0:T(8,128)}, f32[2,4,2,64,128]{4,3,2,1,0:T(8,128)S(1)}, f32[2,4,2,64,128]{4,3,2,1,0:T(8,128)S(1)}) custom-call(s32[3]{0:T(128)S(1)} %pad_add_fusion.scalar_ref, f32[16]{0:T(128)S(1)} %multiply_multiply_fusion.damp_x_ref, ...), custom_call_target="tpu_custom_call", output_to_operand_aliasing={{0}: (4, {})} | custom-call | flops 1 | tf_op jit(solution)/shard_map/last_edge_step0/pallas_call | solution.py:530
  146.4 2.1 %collective-permute-done.16.got_ref = f32[8,2,64,256]{3,2,1,0:T(8,128)S(1)} collective-permute-done((f32[8,2,64,256]{3,2,1,0:T(8,128)S(1)}, f32[8,2,64,256]{3,2,1,0:T(8,128)S(1)}, u32[]{:S(2)}, u32[]{:S(2)}) %collective-permute-start.16) | collective-permute-done | bytes 1048608 | tf_op jit(solution)/shard_map/ppermute | solution.py:659
  149.4 4.9 %last_edge_step1.1 = (f32[16,256,256]{2,1,0:T(8,128)}, f32[2,4,2,64,128]{4,3,2,1,0:T(8,128)S(1)}, f32[2,4,2,64,128]{4,3,2,1,0:T(8,128)S(1)}) custom-call(s32[3]{0:T(128)S(1)} %pad_add_fusion.scalar_ref, f32[16]{0:T(128)S(1)} %multiply_multiply_fusion.damp_x_ref, ...), custom_call_target="tpu_custom_call", output_to_operand_aliasing={{0}: (4, {})} | custom-call | flops 1 | tf_op jit(solution)/shard_map/last_edge_step1/pallas_call | solution.py:530
  158.8 16.0 %collective-permute-done.19.refs_2_ = f32[8,64,128]{2,1,0:T(8,128)S(1)} collective-permute-done((f32[8,64,128]{2,1,0:T(8,128)S(1)}, f32[8,64,128]{2,1,0:T(8,128)S(1)}, u32[]{:S(2)}, u32[]{:S(2)}) %collective-permute-start.19) | collective-permute-done | bytes 262176 | tf_op jit(solution)/shard_map/ppermute | solution.py:665
  174.8 5.1 %collective-permute-done.21.refs_4_ = f32[8,64,128]{2,1,0:T(8,128)S(1)} collective-permute-done((f32[8,64,128]{2,1,0:T(8,128)S(1)}, f32[8,64,128]{2,1,0:T(8,128)S(1)}, u32[]{:S(2)}, u32[]{:S(2)}) %collective-permute-start.21) | collective-permute-done | bytes 262176 | tf_op jit(solution)/shard_map/ppermute | solution.py:665
  179.9 2.1 %gather_sum.1 = f32[16,64,256]{2,1,0:T(8,128)} custom-call(s32[3]{0:T(128)S(1)} %pad_add_fusion.scalar_ref, f32[8,64,256]{2,1,0:T(8,128)S(1)} %collective-permute-done.17.refs_0_, f32[8,64,256]{2,1,0:T(8,128)S(1)} %get-tuple-element.105.refs_1_, f32[8,64,128]{2,1,0:T(8,128)S(1)} %collective-permute-done.19.refs_2_, ...), custom_call_target="tpu_custom_call" | custom-call | flops 1 | tf_op jit(solution)/shard_map/gather_sum/pallas_call | solution.py:593
  (53 shorter events, 20.8 us)
Async XLA Ops:
  5.0 26.6 %all-to-all-start = ((f32[32,8,128]{2,1,0:T(8,128)}), f32[32,8,128]{2,1,0:T(8,128)S(1)}, u32[]{:S(2)}, u32[]{:S(2)}) async-start(f32[32,8,128]{2,1,0:T(8,128)} %route.1), calls=%async_computation | async-start | bytes 262144 | tf_op jit(solution)/shard_map/all_to_all | solution.py:634
  19.5 33.9 %collective-permute-start = (f32[4,256,128]{2,1,0:T(8,128)}, f32[4,256,128]{2,1,0:T(8,128)S(1)}, u32[]{:S(2)}, u32[]{:S(2)}) collective-permute-start(f32[4,256,128]{2,1,0:T(8,128)} %get-tuple-element.58), channel_id=1, source_target_pairs={{0,1},{1,0},{2,3},{3,2},{4,5},{5,4},{6,7},{7,6},{8,9},{9,8},{10,11... | collective-permute-start | bytes 1572872 | tf_op jit(solution)/shard_map/ppermute | solution.py:624
  21.1 32.4 %collective-permute-start.1 = (f32[4,256,128]{2,1,0:T(8,128)}, f32[4,256,128]{2,1,0:T(8,128)S(1)}, u32[]{:S(2)}, u32[]{:S(2)}) collective-permute-start(f32[4,256,128]{2,1,0:T(8,128)} %get-tuple-element.59), channel_id=1, source_target_pairs={{1,2},{2,1},{3,4},{4,3},{5,6},{6,5},{7,8},{8,7},{9,10},{10,9},{11,... | collective-permute-start | bytes 1572872 | tf_op jit(solution)/shard_map/ppermute | solution.py:624
  27.4 34.4 %collective-permute-start.4 = (f32[4,256,128]{2,1,0:T(8,128)}, f32[4,256,128]{2,1,0:T(8,128)S(1)}, u32[]{:S(2)}, u32[]{:S(2)}) collective-permute-start(f32[4,256,128]{2,1,0:T(8,128)} %get-tuple-element.65), channel_id=1, source_target_pairs={{0,1},{1,0},{2,3},{3,2},{4,5},{5,4},{6,7},{7,6},{8,9},{9,8},{10,11... | collective-permute-start | bytes 1572872 | tf_op jit(solution)/shard_map/ppermute | solution.py:624
  27.5 34.3 %collective-permute-start.5 = (f32[4,256,128]{2,1,0:T(8,128)S(1)}, f32[4,256,128]{2,1,0:T(8,128)S(1)}, u32[]{:S(2)}, u32[]{:S(2)}) collective-permute-start(f32[4,256,128]{2,1,0:T(8,128)S(1)} %get-tuple-element.66), channel_id=1, source_target_pairs={{1,2},{2,1},{3,4},{4,3},{5,6},{6,5},{7,8},{8,7},{9,10},{10,9},{11,... | collective-permute-start | bytes 1572872 | tf_op jit(solution)/shard_map/ppermute | solution.py:624
  31.7 10.6 %copy-start = (bf16[256,256]{1,0:T(8,128)(2,1)S(1)}, bf16[256,256]{1,0:T(8,128)(2,1)}, u32[]{:S(2)}) copy-start(bf16[256,256]{1,0:T(8,128)(2,1)} %constant.59.clone.band_ref) | copy-start | bytes 393220
  55.4 24.2 %collective-permute-start.2 = (f32[4,256,128]{2,1,0:T(8,128)S(1)}, f32[4,256,128]{2,1,0:T(8,128)S(1)}, u32[]{:S(2)}, u32[]{:S(2)}) collective-permute-start(f32[4,256,128]{2,1,0:T(8,128)S(1)} %get-tuple-element.63), channel_id=1, source_target_pairs={{0,1},{1,0},{2,3},{3,2},{4,5},{5,4},{6,7},{7,6},{8,9},{9,8},{10,11... | collective-permute-start | bytes 1572872 | tf_op jit(solution)/shard_map/ppermute | solution.py:624
  56.0 23.6 %collective-permute-start.3 = (f32[4,256,128]{2,1,0:T(8,128)S(1)}, f32[4,256,128]{2,1,0:T(8,128)S(1)}, u32[]{:S(2)}, u32[]{:S(2)}) collective-permute-start(f32[4,256,128]{2,1,0:T(8,128)S(1)} %get-tuple-element.64), channel_id=1, source_target_pairs={{1,2},{2,1},{3,4},{4,3},{5,6},{6,5},{7,8},{8,7},{9,10},{10,9},{11,... | collective-permute-start | bytes 1572872 | tf_op jit(solution)/shard_map/ppermute | solution.py:624
  63.8 23.7 %collective-permute-start.8 = (f32[4,256,128]{2,1,0:T(8,128)S(1)}, f32[4,256,128]{2,1,0:T(8,128)S(1)}, u32[]{:S(2)}, u32[]{:S(2)}) collective-permute-start(f32[4,256,128]{2,1,0:T(8,128)S(1)} %get-tuple-element.74), channel_id=1, source_target_pairs={{0,1},{1,0},{2,3},{3,2},{4,5},{5,4},{6,7},{7,6},{8,9},{9,8},{10,11... | collective-permute-start | bytes 1572872 | tf_op jit(solution)/shard_map/ppermute | solution.py:624
  63.9 23.7 %collective-permute-start.9 = (f32[4,256,128]{2,1,0:T(8,128)S(1)}, f32[4,256,128]{2,1,0:T(8,128)S(1)}, u32[]{:S(2)}, u32[]{:S(2)}) collective-permute-start(f32[4,256,128]{2,1,0:T(8,128)S(1)} %get-tuple-element.75), channel_id=1, source_target_pairs={{1,2},{2,1},{3,4},{4,3},{5,6},{6,5},{7,8},{8,7},{9,10},{10,9},{11,... | collective-permute-start | bytes 1572872 | tf_op jit(solution)/shard_map/ppermute | solution.py:624
  81.5 26.7 %collective-permute-start.6 = (f32[4,256,128]{2,1,0:T(8,128)S(1)}, f32[4,256,128]{2,1,0:T(8,128)S(1)}, u32[]{:S(2)}, u32[]{:S(2)}) collective-permute-start(f32[4,256,128]{2,1,0:T(8,128)S(1)} %get-tuple-element.72), channel_id=1, source_target_pairs={{0,1},{1,0},{2,3},{3,2},{4,5},{5,4},{6,7},{7,6},{8,9},{9,8},{10,11... | collective-permute-start | bytes 1572872 | tf_op jit(solution)/shard_map/ppermute | solution.py:624
  81.6 26.6 %collective-permute-start.7 = (f32[4,256,128]{2,1,0:T(8,128)S(1)}, f32[4,256,128]{2,1,0:T(8,128)S(1)}, u32[]{:S(2)}, u32[]{:S(2)}) collective-permute-start(f32[4,256,128]{2,1,0:T(8,128)S(1)} %get-tuple-element.73), channel_id=1, source_target_pairs={{1,2},{2,1},{3,4},{4,3},{5,6},{6,5},{7,8},{8,7},{9,10},{10,9},{11,... | collective-permute-start | bytes 1572872 | tf_op jit(solution)/shard_map/ppermute | solution.py:624
  89.4 20.7 %collective-permute-start.12 = (f32[4,256,128]{2,1,0:T(8,128)S(1)}, f32[4,256,128]{2,1,0:T(8,128)S(1)}, u32[]{:S(2)}, u32[]{:S(2)}) collective-permute-start(f32[4,256,128]{2,1,0:T(8,128)S(1)} %get-tuple-element.83), channel_id=1, source_target_pairs={{0,1},{1,0},{2,3},{3,2},{4,5},{5,4},{6,7},{7,6},{8,9},{9,8},{10,11... | collective-permute-start | bytes 1572872 | tf_op jit(solution)/shard_map/ppermute | solution.py:624
  89.5 21.0 %collective-permute-start.13 = (f32[4,256,128]{2,1,0:T(8,128)S(1)}, f32[4,256,128]{2,1,0:T(8,128)S(1)}, u32[]{:S(2)}, u32[]{:S(2)}) collective-permute-start(f32[4,256,128]{2,1,0:T(8,128)S(1)} %get-tuple-element.84), channel_id=1, source_target_pairs={{1,2},{2,1},{3,4},{4,3},{5,6},{6,5},{7,8},{8,7},{9,10},{10,9},{11,... | collective-permute-start | bytes 1572872 | tf_op jit(solution)/shard_map/ppermute | solution.py:624
  112.4 25.5 %collective-permute-start.14 = (f32[4,256,128]{2,1,0:T(8,128)S(1)}, f32[4,256,128]{2,1,0:T(8,128)S(1)}, u32[]{:S(2)}, u32[]{:S(2)}) collective-permute-start(f32[4,256,128]{2,1,0:T(8,128)S(1)} %get-tuple-element.86), channel_id=1, source_target_pairs={{0,1},{1,0},{2,3},{3,2},{4,5},{5,4},{6,7},{7,6},{8,9},{9,8},{10,11... | collective-permute-start | bytes 1572872 | tf_op jit(solution)/shard_map/ppermute | solution.py:624
  112.5 25.4 %collective-permute-start.15 = (f32[4,256,128]{2,1,0:T(8,128)S(1)}, f32[4,256,128]{2,1,0:T(8,128)S(1)}, u32[]{:S(2)}, u32[]{:S(2)}) collective-permute-start(f32[4,256,128]{2,1,0:T(8,128)S(1)} %get-tuple-element.87), channel_id=1, source_target_pairs={{1,2},{2,1},{3,4},{4,3},{5,6},{6,5},{7,8},{8,7},{9,10},{10,9},{11,... | collective-permute-start | bytes 1572872 | tf_op jit(solution)/shard_map/ppermute | solution.py:624
  118.9 19.1 %collective-permute-start.10 = (f32[4,256,128]{2,1,0:T(8,128)S(1)}, f32[4,256,128]{2,1,0:T(8,128)S(1)}, u32[]{:S(2)}, u32[]{:S(2)}) collective-permute-start(f32[4,256,128]{2,1,0:T(8,128)S(1)} %get-tuple-element.81), channel_id=1, source_target_pairs={{0,1},{1,0},{2,3},{3,2},{4,5},{5,4},{6,7},{7,6},{8,9},{9,8},{10,11... | collective-permute-start | bytes 1572872 | tf_op jit(solution)/shard_map/ppermute | solution.py:624
  119.2 21.9 %collective-permute-start.11 = (f32[4,256,128]{2,1,0:T(8,128)S(1)}, f32[4,256,128]{2,1,0:T(8,128)S(1)}, u32[]{:S(2)}, u32[]{:S(2)}) collective-permute-start(f32[4,256,128]{2,1,0:T(8,128)S(1)} %get-tuple-element.82), channel_id=1, source_target_pairs={{1,2},{2,1},{3,4},{4,3},{5,6},{6,5},{7,8},{8,7},{9,10},{10,9},{11,... | collective-permute-start | bytes 1572872 | tf_op jit(solution)/shard_map/ppermute | solution.py:624
  145.9 2.7 %collective-permute-start.16 = (f32[8,2,64,256]{3,2,1,0:T(8,128)S(1)}, f32[8,2,64,256]{3,2,1,0:T(8,128)S(1)}, u32[]{:S(2)}, u32[]{:S(2)}) collective-permute-start(f32[8,2,64,256]{3,2,1,0:T(8,128)S(1)} %get-tuple-element.98), channel_id=1, source_target_pairs={{0,32},{32,0},{64,96},{96,64},{1,33},{33,1},{65,97},{97,65},{2,34}... | collective-permute-start | bytes 3145736 | tf_op jit(solution)/shard_map/ppermute | solution.py:659
  145.9 9.2 %collective-permute-start.18 = (f32[8,2,64,128]{3,2,1,0:T(8,128)S(1)}, f32[8,2,64,128]{3,2,1,0:T(8,128)S(1)}, u32[]{:S(2)}, u32[]{:S(2)}) collective-permute-start(f32[8,2,64,128]{3,2,1,0:T(8,128)S(1)} %bitcast.16), channel_id=1, source_target_pairs={{0,32},{32,0},{64,96},{96,64},{1,33},{33,1},{65,97},{97,65},{2,34}... | collective-permute-start | bytes 1572872 | tf_op jit(solution)/shard_map/ppermute | solution.py:664
  154.3 3.0 %collective-permute-start.20 = (f32[8,2,64,128]{3,2,1,0:T(8,128)S(1)}, f32[8,2,64,128]{3,2,1,0:T(8,128)S(1)}, u32[]{:S(2)}, u32[]{:S(2)}) collective-permute-start(f32[8,2,64,128]{3,2,1,0:T(8,128)S(1)} %bitcast.17), channel_id=1, source_target_pairs={{0,32},{32,0},{64,96},{96,64},{1,33},{33,1},{65,97},{97,65},{2,34}... | collective-permute-start | bytes 1572872 | tf_op jit(solution)/shard_map/ppermute | solution.py:664
  154.4 20.4 %collective-permute-start.17 = (f32[8,64,256]{2,1,0:T(8,128)S(1)}, f32[8,64,256]{2,1,0:T(8,128)S(1)}, u32[]{:S(2)}, u32[]{:S(2)}) collective-permute-start(f32[8,64,256]{2,1,0:T(8,128)S(1)} %get-tuple-element.104), channel_id=1, source_target_pairs={{0,64},{32,96},{64,0},{96,32},{1,65},{33,97},{65,1},{97,33},{2,66}... | collective-permute-start | bytes 1572872 | tf_op jit(solution)/shard_map/ppermute | solution.py:661
  155.9 18.9 %collective-permute-start.19 = (f32[8,64,128]{2,1,0:T(8,128)S(1)}, f32[8,64,128]{2,1,0:T(8,128)S(1)}, u32[]{:S(2)}, u32[]{:S(2)}) collective-permute-start(f32[8,64,128]{2,1,0:T(8,128)S(1)} %get-tuple-element.108), channel_id=1, source_target_pairs={{0,64},{32,96},{64,0},{96,32},{1,65},{33,97},{65,1},{97,33},{2,66}... | collective-permute-start | bytes 786440 | tf_op jit(solution)/shard_map/ppermute | solution.py:665
  158.0 21.8 %collective-permute-start.21 = (f32[8,64,128]{2,1,0:T(8,128)S(1)}, f32[8,64,128]{2,1,0:T(8,128)S(1)}, u32[]{:S(2)}, u32[]{:S(2)}) collective-permute-start(f32[8,64,128]{2,1,0:T(8,128)S(1)} %get-tuple-element.112), channel_id=1, source_target_pairs={{0,64},{32,96},{64,0},{96,32},{1,65},{33,97},{65,1},{97,33},{2,66}... | collective-permute-start | bytes 786440 | tf_op jit(solution)/shard_map/ppermute | solution.py:665
  (3 other events, 2.1 us)

commit v3 on v2

--- a/solution.py
+++ b/solution.py
@@ -122,7 +122,7 @@
     position = lax.broadcasted_iota(jnp.int32, (8, 128), 1) + 128 * (
         lax.broadcasted_iota(jnp.int32, (8, 128), 0) >> 2
     )
-    batch = 4
+    batch = 2
 
     @pl.loop(0, value_ref.shape[0])
     def _(source):
@@ -195,7 +195,7 @@
 def first_edges(current, scalars):
     return pl.pallas_call(
         first_edges_body,
-        out_shape=[jax.ShapeDtypeStruct((4, SIZE, HALF), f32)] * 4,
+        out_shape=[pltpu.VMEM((4, SIZE, HALF), f32)] * 4,
         in_specs=[SMEM, ANY],
         out_specs=[VMEM] * 4,
         scratch_shapes=[pltpu.SemaphoreType.DMA((4,))],
@@ -210,19 +210,22 @@
     return inverse, (COURANT * COURANT) * (speed * speed) * inverse
 
 
-def local_body(step, scalar_ref, damp_x_ref, q_hbm, p_hbm, v_hbm, s_ref, damp_ref, band_ref, *rest):
-    if step < 2:
+def local_body(step, scalar_ref, damp_x_ref, q_hbm, p_hbm, v_ref, s_ref, damp_ref, band_ref, *rest):
+    if step == 0:
+        v_hbm = v_ref
+        n_hbm, edge_ref, gain_ref, v_ref, *scratch = rest
+    elif step == 1:
         n_hbm, edge_ref, gain_ref, *scratch = rest
     elif step == 2:
-        accel_hbm, n_hbm, edge_ref, gain_ref, part_hbm, *scratch = rest
+        accel_hbm, n_hbm, edge_ref, gain_ref, part, *scratch = rest
     else:
-        accel_hbm, part_hbm, n_hbm, loc_ref, *scratch = rest
+        accel_hbm, part, n_hbm, loc_ref, *scratch = rest
         (send_ref, keep_ref), scratch = scratch[:2], scratch[2:]
-    high, low, mixed0, mixed1, q_ref, n_ref, v_ref, load_sems, store_sems = scratch[:9]
+    high, low, mixed0, mixed1, q_ref, n_ref, load_sems, store_sems = scratch[:8]
     if step >= 2:
-        accel, accel_sems, part, part_sems = scratch[9:13]
+        accel, accel_sems = scratch[8:10]
     if step == 3:
-        shared = scratch[13]
+        shared = scratch[10]
     p_ref = n_ref
     mixed = (mixed0, mixed1)
     group_size = 4
@@ -236,7 +239,7 @@
         return pl.ds(group_size * group, group_size)
 
     def load(i, group):
-        source, target = ((q_hbm, q_ref), (v_hbm, v_ref), (p_hbm, p_ref))[i]
+        source, target = (q_hbm, q_ref) if i == 0 else (p_hbm, p_ref) if i == 1 else (v_hbm, v_ref)
         return pltpu.make_async_copy(
             source.at[planes(group)], target.at[planes(group)], load_sems.at[i, group]
         )
@@ -246,27 +249,17 @@
             accel_hbm.at[0, pl.ds(first, 2), planes(group)], accel.at[group], accel_sems.at[group]
         )
 
-    def load_part(group):
+    def store(group):
         return pltpu.make_async_copy(
-            part_hbm.at[planes(group)], part.at[planes(group)], part_sems.at[group]
-        )
-
-    def stores(group):
-        out = [pltpu.make_async_copy(n_ref.at[planes(group)], n_hbm.at[planes(group)], store_sems.at[group])]
-        if step == 2:
-            out.append(
-                pltpu.make_async_copy(
-                    part.at[planes(group)], part_hbm.at[planes(group)], part_sems.at[group]
-                )
-            )
-        return out
+            n_ref.at[planes(group)], n_hbm.at[planes(group)], store_sems.at[group]
+        )
 
     def others(group):
-        out = [load(1, group), load(2, group)]
+        out = [load(1, group)]
+        if step == 0:
+            out.append(load(2, group))
         if step >= 2:
             out.append(fetch(group))
-        if step == 3:
-            out.append(load_part(group))
         return out
 
     load(0, 0).start()
@@ -354,17 +347,16 @@
                 def _():
                     send_ref[inner, j >> 1] = shared[...]
 
-        for copy in stores(group):
-            copy.start()
+        store(group).start()
     for group in range(groups):
-        for copy in stores(group):
-            copy.wait()
+        store(group).wait()
 
 
 def local_step(step, scalars, damp_x, q, p, v, s, damp, accel, part=None):
     whole = (SLAB, SIZE, SIZE)
-    in_specs = [SMEM, SMEM] + [ANY] * 3 + [VMEM] * 3
-    operands = [scalars, damp_x, in_hbm(q), in_hbm(p), in_hbm(v), pinned(s), damp, jnp.asarray(band())]
+    in_specs = [SMEM, SMEM, ANY, ANY, VMEM if step else ANY] + [VMEM] * 3
+    v = pinned(v) if step else in_hbm(v)
+    operands = [scalars, damp_x, in_hbm(q), in_hbm(p), v, pinned(s), damp, jnp.asarray(band())]
     out_specs = [ANY]
     out_shape = [pltpu.HBM(whole, f32)]
     scratch = [
@@ -372,7 +364,6 @@
         pltpu.VMEM((SIZE, SIZE), bf16),
         pltpu.VMEM((4, SIZE, SIZE), f32),
         pltpu.VMEM((4, SIZE, SIZE), f32),
-        pltpu.VMEM(whole, f32),
         pltpu.VMEM(whole, f32),
         pltpu.VMEM(whole, f32),
         pltpu.SemaphoreType.DMA((3, 4)),
@@ -384,18 +375,16 @@
         scratch += [
             pltpu.VMEM((4, 2, 4, SIZE, SIZE), bf16),
             pltpu.SemaphoreType.DMA((4,)),
-            pltpu.VMEM(whole, f32),
-            pltpu.SemaphoreType.DMA((4,)),
         ]
     if step < 3:
         out_specs += [VMEM] * 2
         out_shape += [jax.ShapeDtypeStruct((8, SIZE, SIZE), f32)] * 2
-    if step == 2:
-        out_specs.append(ANY)
-        out_shape.append(pltpu.HBM(whole, f32))
+    if step in (0, 2):
+        out_specs.append(VMEM)
+        out_shape.append(pltpu.VMEM(whole, f32))
     if step == 3:
-        in_specs.append(ANY)
-        operands.append(in_hbm(part))
+        in_specs.append(VMEM)
+        operands.append(pinned(part))
         out_specs += [VMEM] * 3
         out_shape.append(jax.ShapeDtypeStruct((8, SIZE, SIZE), f32))
         out_shape += [jax.ShapeDtypeStruct((8, 2, 64, SIZE), f32)] * 2
@@ -471,78 +460,93 @@
 
 
 def last_edge_body(
-    scalar_ref, damp_x_ref, even_ref, odd_ref, n_in, v_ref, damp_ref, a_ref, loc_ref, n_ref, send_ref, keep_ref, grad
+    half,
+    scalar_ref,
+    damp_x_ref,
+    even_ref,
+    odd_ref,
+    _,
+    v_ref,
+    damp_ref,
+    a_hbm,
+    loc_ref,
+    n_hbm,
+    send_ref,
+    keep_ref,
+    face,
+    accel,
+    grad,
+    sems,
 ):
-    group = pl.program_id(0)
-    upper = side_of(group, scalar_ref[0])
     core = scalar_ref[1]
     rows = 16
-    weights = halo_weights(upper)
-
-    def run(halo_ref):
-        @pl.loop(0, HALF // rows)
+    lanes = slice(half * HALF, (half + 1) * HALF)
+
+    def copy(group, which):
+        at = (pl.ds(12 * side_of(group, scalar_ref[0]), 4), slice(None), pl.ds(half * HALF, HALF))
+        there, here = n_hbm.at[at], face.at[group]
+        if which == 0:
+            return pltpu.make_async_copy(there, here, sems.at[group, 0])
+        if which == 1:
+            return pltpu.make_async_copy(a_hbm.at[(0, STEPS - 1, *at)], accel.at[group], sems.at[group, 1])
+        return pltpu.make_async_copy(here, there, sems.at[group, 2])
+
+    for group in range(2):
+        copy(group, 0).start()
+        copy(group, 1).start()
+    for group in range(2):
+        upper = side_of(group, scalar_ref[0])
+        halo_ref = (even_ref, odd_ref)[group]
+        weights = halo_weights(upper)
+        copy(group, 0).wait()
+        copy(group, 1).wait()
+
+        @pl.loop(0, SIZE // rows)
         def _(i):
             row = pl.ds(pl.multiple_of(i * rows, rows), rows)
             halo = [halo_ref[m, row, :] for m in range(4)]
-            damp = damp_ref[row, :]
+            damp = damp_ref[row, lanes]
             for j in range(4):
-                speed = v_ref[j, row, :]
-                _, gain = factor(speed, damp + damp_x_ref[upper * 12 + j])
+                layer = upper * 12 + j
+                speed = v_ref[layer, row, lanes]
+                _, gain = factor(speed, damp + damp_x_ref[layer])
                 across = weights[j][0] * halo[0]
                 for m in range(1, 4):
                     across = across + weights[j][m] * halo[m]
                 extra = gain * across
-                after = n_in[j, row, :] + extra
-                n_ref[j, row, :] = after
-                grad[j, row, :] = loc_ref[j, row, :] + extra * a_ref[0, 0, j, row, :].astype(f32) * (
-                    2.0 / (speed * speed * speed)
-                )
-
-    @pl.when(group == 0)
-    def _():
-        run(even_ref)
-
-    @pl.when(group == 1)
-    def _():
-        run(odd_ref)
-
-    send_ref[0, :, 0] = grad[:, pl.ds(pl.multiple_of(64 * (1 - core), 64), 64), :]
-    keep_ref[0, :, 0] = grad[:, pl.ds(pl.multiple_of(64 * core, 64), 64), :]
+                face[group, j, row, :] = face[group, j, row, :] + extra
+                grad[j, row, :] = loc_ref[upper * 4 + j, row, lanes] + extra * accel[group, j, row, :].astype(
+                    f32
+                ) * (2.0 / (speed * speed * speed))
+
+        copy(group, 2).start()
+        for y in range(2):
+            mine = pl.ds(pl.multiple_of(y * 128 + 64 * core, 64), 64)
+            yours = pl.ds(pl.multiple_of(y * 128 + 64 * (1 - core), 64), 64)
+            for j in range(4):
+                keep_ref[group * 4 + j, y] = grad[j, mine, :]
+                send_ref[group * 4 + j, y] = grad[j, yours, :]
+    for group in range(2):
+        copy(group, 2).wait()
 
 
 def last_edge_step(half, scalars, damp_x, even, odd, n, v, damp, accel, loc):
-    block = (4, HALF, HALF)
-
-    def edge_block(g, y, s, _):
-        return (3 * side_of(g, s[0]), y, half)
-
-    edge_spec = pl.BlockSpec(block, edge_block)
-    in_specs = [
-        pl.BlockSpec(block, lambda g, y, *_: (0, jnp.where(g == 0, y, 1), 0)),
-        pl.BlockSpec(block, lambda g, y, *_: (0, jnp.where(g == 0, 0, y), 0)),
-        edge_spec,
-        edge_spec,
-        pl.BlockSpec((HALF, HALF), lambda g, y, *_: (y, half)),
-        pl.BlockSpec((1, 1) + block, lambda g, y, s, _: (0, 3, 3 * side_of(g, s[0]), y, half)),
-        pl.BlockSpec(block, lambda g, y, s, _: (side_of(g, s[0]), y, half)),
-    ]
-    quarter = pl.BlockSpec((1, 4, 1, 64, HALF), lambda g, y, *_: (g, 0, y, 0, 0))
-    return pl.pallas_call(
-        last_edge_body,
-        out_shape=[jax.ShapeDtypeStruct((SLAB, SIZE, SIZE), f32)]
-        + [jax.ShapeDtypeStruct((2, 4, 2, 64, HALF), f32)] * 2,
-        grid_spec=pltpu.PrefetchScalarGridSpec(
-            num_scalar_prefetch=2,
-            grid=(2, 2),
-            in_specs=in_specs,
-            out_specs=[edge_spec, quarter, quarter],
-            scratch_shapes=[pltpu.VMEM(block, f32)],
-        ),
+    return pl.pallas_call(
+        functools.partial(last_edge_body, half),
+        out_shape=[pltpu.HBM((SLAB, SIZE, SIZE), f32)] + [jax.ShapeDtypeStruct((8, 2, 64, HALF), f32)] * 2,
+        in_specs=[SMEM, SMEM, VMEM, VMEM, ANY, VMEM, VMEM, ANY, VMEM],
+        out_specs=[ANY, VMEM, VMEM],
+        scratch_shapes=[
+            pltpu.VMEM((2, 4, SIZE, HALF), f32),
+            pltpu.VMEM((2, 4, SIZE, HALF), bf16),
+            pltpu.VMEM((4, SIZE, HALF), f32),
+            pltpu.SemaphoreType.DMA((2, 3)),
+        ],
         input_output_aliases={4: 0},
-        compiler_params=params(7, 2),
+        compiler_params=params(12, 0),
         cost_estimate=cost(1, 0),
         name=f"last_edge_step{half}",
-    )(scalars, damp_x, even, odd, in_hbm(n), in_hbm(v), damp, in_hbm(accel), loc)
+    )(scalars, damp_x, even, odd, in_hbm(n), pinned(v), damp, in_hbm(accel), loc)
 
 
 def split_body(scalar_ref, got_ref, own_ref, send_ref, keep_ref):
@@ -567,39 +571,23 @@
     )(scalars, got, own)
 
 
-def gather_body(scalar_ref, *refs):
-    inner_a, inner_b, first_a, first_b, second_a, second_b, out_ref = refs
-    block = pl.program_id(0)
-    inside = jnp.logical_or(block == 1, block == 2)
-
-    @pl.when(inside)
-    def _():
-        out_ref[...] = inner_a[...] + inner_b[...]
-
-    @pl.when(jnp.logical_not(inside))
-    def _():
-        out_ref[:, :, 0:HALF] = first_a[...] + first_b[...]
-        out_ref[:, :, HALF:SIZE] = second_a[...] + second_b[...]
+def gather_body(scalar_ref, inner_a, inner_b, first_a, first_b, second_a, second_b, out_ref):
+    out_ref[4 : SLAB - 4] = inner_a[...] + inner_b[...]
+    for upper in range(2):
+        group = (upper + scalar_ref[0] + 1) % 2
+        face = pl.ds(group * 4, 4)
+        layers = slice(12 * upper, 12 * upper + 4)
+        out_ref[layers, :, 0:HALF] = first_a[face] + first_b[face]
+        out_ref[layers, :, HALF:SIZE] = second_a[face] + second_b[face]
 
 
 def gather_sum(scalars, inner, first, second):
-    inner_spec = pl.BlockSpec((4, 64, SIZE), lambda i, s: (jnp.clip(i - 1, 0, 1), 0, 0))
-
-    def group(i, s):
-        upper = (i == 3).astype(jnp.int32)
-        return (upper + s[0] + 1) % 2, 0, 0
-
-    edge_spec = pl.BlockSpec((4, 64, HALF), group)
     return pl.pallas_call(
         gather_body,
         out_shape=jax.ShapeDtypeStruct((SLAB, 64, SIZE), f32),
-        grid_spec=pltpu.PrefetchScalarGridSpec(
-            num_scalar_prefetch=1,
-            grid=(4,),
-            in_specs=[inner_spec] * 2 + [edge_spec] * 4,
-            out_specs=pl.BlockSpec((4, 64, SIZE), lambda i, s: (i, 0, 0)),
-        ),
-        compiler_params=params(4),
+        in_specs=[SMEM] + [VMEM] * 6,
+        out_specs=VMEM,
+        compiler_params=params(8, 0),
         cost_estimate=cost(1, 0),
         name="gather_sum",
     )(scalars, *inner, *first, *second)
@@ -649,6 +637,8 @@
             arrived_a, arrived_b = lax.optimization_barrier((arrived_a, arrived_b))
         else:
             edge, gain, *part = extra
+            if step == 0:
+                (velocity,), part = part, []
         for half, arrived in enumerate((arrived_a, arrived_b)):
             if last:
                 after, x, y = last_edge_step(
@@ -659,8 +649,6 @@
                     send, inner_keep = split_sum(scalars, lax.ppermute(inner_send, "shot", swap_core), inner_keep)
                     send, after = lax.optimization_barrier((send, after))
                     inner = (lax.ppermute(send, "shot", swap_row), inner_keep)
-                x = x.reshape(8, 2, 64, HALF)
-                y = y.reshape(8, 2, 64, HALF)
                 send, edge_keep = split_sum(scalars, lax.ppermute(x, "shot", swap_core), y)
                 outs.append((lax.ppermute(send, "shot", swap_row), edge_keep))
             else:

time: 183 us -> 180 us (0.984)
  Pallas kernels: 93.1 us -> 87.6 us
  waiting for transfers between devices: 26.6 us -> 29.5 us
    pallas_call x4, Pallas kernels: 51.3 us -> 48.2 us  [local_step(): pl.pallas_call(functools.partial(local_body, step), out_shape=out_shape,...]
    ppermute x8, waiting for transfers between devices: 3.41 us -> 6.22 us  [exchange(): lax.ppermute(odd, 'sub', pairs_odd)]
    pallas_call x3, Pallas kernels: 13 us -> 10.6 us  [the longest x2 7.29 us: last_edge_step(): pl.pallas_call(functools.partial(last_edge_body, half), out_shape=[pltpu....]
  transfers between devices with their start and end apart: 23 -> 23, of which waited for: 5 -> 5; matrix products, arithmetic and copies ran while one was open for 0% -> 0% of each run, Pallas kernels for 45% -> 43%
where the time goes in v3:
time: 180 us
  Pallas kernels  87.6 us (49%)
  starting transfers between devices  59.4 us (33%)
  waiting for transfers between devices  29.5 us (16%)
  local copies, waits for them, and re-layouts  2.09 us (1%)
    pallas_call x4, Pallas kernels, local_step(): pl.pallas_call(functools.partial(local_body, step), out_shape=out_shape,...  48.2 us
    ppermute x8, starting transfers between devices, exchange(): lax.ppermute(odd, 'sub', pairs_odd)  42.3 us
    ppermute x2, waiting for transfers between devices, shards(): outs.append((lax.ppermute(send, 'shot', swap_row), edge_keep))  21.1 us
    pallas_call x6, Pallas kernels, edge_step(): pl.pallas_call(functools.partial(edge_body, half), out_shape=[pltpu.HBM((...  11.5 us
    pallas_call x1, Pallas kernels, inject(): pl.pallas_call(inject_body, out_shape=pltpu.VMEM((SLAB * SIZE * 8, 128),...  11.2 us
    all_to_all x1, starting transfers between devices, shards(): got = lax.all_to_all(sent, 'sub', split_axis=0, concat_axis=0, tiled=True)  11.1 us
    pallas_call x2, Pallas kernels, last_edge_step(): pl.pallas_call(functools.partial(last_edge_body, half), out_shape=[pltpu....  7.29 us
    ppermute x8, waiting for transfers between devices, exchange(): lax.ppermute(odd, 'sub', pairs_odd)  6.22 us
  transfers between devices with their start and end apart: 23, of which 5 were waited for; matrix products, arithmetic and copies ran while one was open for 0% of the time, Pallas kernels for 43%

profile of v3, /device:TPU:2, one launch (start us, length us, event | category | flops | bytes accessed | tf_op | source)
XLA Modules:
  0.0 179.9 jit_solution(11047058922941122480)
XLA Ops:
  2.7 2.3 %route.1 = f32[32,8,128]{2,1,0:T(8,128)} custom-call(s32[1,1024]{1,0:T(1,128)S(1)} %bitcast.9, s32[1,1024]{1,0:T(1,128)S(1)} %copy-done.3, f32[4,1024]{1,0:T(4,128)S(1)} %bitcast.8), custom_call_target="tpu_custom_call" | custom-call | flops 1 | tf_op jit(solution)/shard_map/route/pallas_call | solution.py:101
  5.0 11.1 %all-to-all-start = ((f32[32,8,128]{2,1,0:T(8,128)}), f32[32,8,128]{2,1,0:T(8,128)S(1)}, u32[]{:S(2)}, u32[]{:S(2)}) async-start(f32[32,8,128]{2,1,0:T(8,128)} %route.1), calls=%async_computation | async-start | bytes 262144 | tf_op jit(solution)/shard_map/all_to_all | solution.py:622
  16.3 3.3 %first_edges.1 = (f32[4,256,128]{2,1,0:T(8,128)}, f32[4,256,128]{2,1,0:T(8,128)}, f32[4,256,128]{2,1,0:T(8,128)}, f32[4,256,128]{2,1,0:T(8,128)S(1)}) custom-call(s32[3]{0:T(128)S(1)} %pad_add_fusion.scalar_ref, f32[16,256,256]{2,1,0:T(8,128)} %bitcast.10), custom_call_target="tpu_custom_call" | custom-call | flops 1 | tf_op jit(solution)/shard_map/first_edges/pallas_call | solution.py:196
  21.1 6.4 %collective-permute-start.1 = (f32[4,256,128]{2,1,0:T(8,128)}, f32[4,256,128]{2,1,0:T(8,128)S(1)}, u32[]{:S(2)}, u32[]{:S(2)}) collective-permute-start(f32[4,256,128]{2,1,0:T(8,128)} %get-tuple-element.60), channel_id=1, source_target_pairs={{1,2},{2,1},{3,4},{4,3},{5,6},{6,5},{7,8},{8,7},{9,10},{10,9},{11,... | collective-permute-start | bytes 1572872 | tf_op jit(solution)/shard_map/ppermute | solution.py:612
  27.5 4.0 %collective-permute-start.5 = (f32[4,256,128]{2,1,0:T(8,128)S(1)}, f32[4,256,128]{2,1,0:T(8,128)S(1)}, u32[]{:S(2)}, u32[]{:S(2)}) collective-permute-start(f32[4,256,128]{2,1,0:T(8,128)S(1)} %get-tuple-element.67), channel_id=1, source_target_pairs={{1,2},{2,1},{3,4},{4,3},{5,6},{6,5},{7,8},{8,7},{9,10},{10,9},{11,... | collective-permute-start | bytes 1572872 | tf_op jit(solution)/shard_map/ppermute | solution.py:612
  31.7 11.2 %inject.1.s_ref = f32[32768,128]{1,0:T(8,128)S(1)} custom-call(f32[32,8,128]{2,1,0:T(8,128)S(1)} %all-to-all-done.value_ref), custom_call_target="tpu_custom_call" | custom-call | flops 1 | tf_op jit(solution)/shard_map/inject/pallas_call | solution.py:158
  42.9 11.2 %local_step0.1 = (f32[16,256,256]{2,1,0:T(8,128)}, f32[8,256,256]{2,1,0:T(8,128)S(1)}, f32[8,256,256]{2,1,0:T(8,128)S(1)}, f32[16,256,256]{2,1,0:T(8,128)S(1)}) custom-call(s32[3]{0:T(128)S(1)} %pad_add_fusion.scalar_ref, f32[16]{0:T(128)S(1)} %multiply_multiply_fusion.damp_x_ref, f32[16,256,256]{2,1,0:T(8,128)} %bitcast.11, f32[16,256,256]{2,1,0:T(8,128)} %bitcast.14, ...), custom_call_target="tpu_custom_call" | custom-call | flops 4000000000 | bytes 20971520 | tf_op jit(solution)/shard_map/local_step0/pallas_call | solution.py:392
  56.1 6.6 %collective-permute-start.3 = (f32[4,256,128]{2,1,0:T(8,128)S(1)}, f32[4,256,128]{2,1,0:T(8,128)S(1)}, u32[]{:S(2)}, u32[]{:S(2)}) collective-permute-start(f32[4,256,128]{2,1,0:T(8,128)S(1)} %get-tuple-element.65), channel_id=1, source_target_pairs={{1,2},{2,1},{3,4},{4,3},{5,6},{6,5},{7,8},{8,7},{9,10},{10,9},{11,... | collective-permute-start | bytes 1572872 | tf_op jit(solution)/shard_map/ppermute | solution.py:612
  64.7 3.9 %collective-permute-start.9 = (f32[4,256,128]{2,1,0:T(8,128)S(1)}, f32[4,256,128]{2,1,0:T(8,128)S(1)}, u32[]{:S(2)}, u32[]{:S(2)}) collective-permute-start(f32[4,256,128]{2,1,0:T(8,128)S(1)} %get-tuple-element.77), channel_id=1, source_target_pairs={{1,2},{2,1},{3,4},{4,3},{5,6},{6,5},{7,8},{8,7},{9,10},{10,9},{11,... | collective-permute-start | bytes 1572872 | tf_op jit(solution)/shard_map/ppermute | solution.py:612
  68.6 11.0 %local_step1.1 = (f32[16,256,256]{2,1,0:T(8,128)}, f32[8,256,256]{2,1,0:T(8,128)S(1)}, f32[8,256,256]{2,1,0:T(8,128)S(1)}) custom-call(s32[3]{0:T(128)S(1)} %pad_add_fusion.scalar_ref, f32[16]{0:T(128)S(1)} %multiply_multiply_fusion.damp_x_ref, f32[16,256,256]{2,1,0:T(8,128)} %get-tuple-element.69.q_hbm.p_hbm, f32[16,256,256]{2,1,0:T(8,128)} %bitcast.12, ...), custom_call_target="tpu_custom_call" | custom-call | flops 4000000000 | bytes 20971520 | tf_op jit(solution)/shard_map/local_step1/pallas_call | solution.py:392
  81.7 6.4 %collective-permute-start.7 = (f32[4,256,128]{2,1,0:T(8,128)S(1)}, f32[4,256,128]{2,1,0:T(8,128)S(1)}, u32[]{:S(2)}, u32[]{:S(2)}) collective-permute-start(f32[4,256,128]{2,1,0:T(8,128)S(1)} %get-tuple-element.75), channel_id=1, source_target_pairs={{1,2},{2,1},{3,4},{4,3},{5,6},{6,5},{7,8},{8,7},{9,10},{10,9},{11,... | collective-permute-start | bytes 1572872 | tf_op jit(solution)/shard_map/ppermute | solution.py:612
  90.2 4.5 %collective-permute-start.13 = (f32[4,256,128]{2,1,0:T(8,128)S(1)}, f32[4,256,128]{2,1,0:T(8,128)S(1)}, u32[]{:S(2)}, u32[]{:S(2)}) collective-permute-start(f32[4,256,128]{2,1,0:T(8,128)S(1)} %get-tuple-element.86), channel_id=1, source_target_pairs={{1,2},{2,1},{3,4},{4,3},{5,6},{6,5},{7,8},{8,7},{9,10},{10,9},{11,... | collective-permute-start | bytes 1572872 | tf_op jit(solution)/shard_map/ppermute | solution.py:612
  94.7 12.6 %local_step2.1 = (f32[16,256,256]{2,1,0:T(8,128)}, f32[8,256,256]{2,1,0:T(8,128)S(1)}, f32[8,256,256]{2,1,0:T(8,128)S(1)}, f32[16,256,256]{2,1,0:T(8,128)S(1)}) custom-call(s32[3]{0:T(128)S(1)} %pad_add_fusion.scalar_ref, f32[16]{0:T(128)S(1)} %multiply_multiply_fusion.damp_x_ref, f32[16,256,256]{2,1,0:T(8,128)} %get-tuple-element.79.q_hbm.p_hbm, ...), custom_call_target="tpu_custom_call" | custom-call | flops 4000000000 | bytes 20971520 | tf_op jit(solution)/shard_map/local_step2/pallas_call | solution.py:392
  107.4 1.9 %edge_step0.5 = (f32[16,256,256]{2,1,0:T(8,128)}, f32[4,256,128]{2,1,0:T(8,128)S(1)}, f32[4,256,128]{2,1,0:T(8,128)S(1)}) custom-call(s32[3]{0:T(128)S(1)} %pad_add_fusion.scalar_ref, f32[4,256,128]{2,1,0:T(8,128)S(1)} %collective-permute-done.6.even_ref, f32[4,256,128]{2,1,0:T(8,128)S(1)} %collective-permute-done.7.odd_ref, ...), custom_call_target="tpu_custom_call", output_to_operand_aliasing={{0}: (5, {})} | custom-call | flops 1 | tf_op jit(solution)/shard_map/edge_step0/pallas_call | solution.py:449
  111.0 1.9 %edge_step1.5 = (f32[16,256,256]{2,1,0:T(8,128)}, f32[4,256,128]{2,1,0:T(8,128)S(1)}, f32[4,256,128]{2,1,0:T(8,128)S(1)}) custom-call(s32[3]{0:T(128)S(1)} %pad_add_fusion.scalar_ref, f32[4,256,128]{2,1,0:T(8,128)S(1)} %collective-permute-done.12.even_ref, f32[4,256,128]{2,1,0:T(8,128)S(1)} %collective-permute-done.13.odd_ref, ...), custom_call_target="tpu_custom_call", output_to_operand_aliasing={{0}: (5, {})} | custom-call | flops 1 | tf_op jit(solution)/shard_map/edge_step1/pallas_call | solution.py:449
  113.0 6.6 %collective-permute-start.15 = (f32[4,256,128]{2,1,0:T(8,128)S(1)}, f32[4,256,128]{2,1,0:T(8,128)S(1)}, u32[]{:S(2)}, u32[]{:S(2)}) collective-permute-start(f32[4,256,128]{2,1,0:T(8,128)S(1)} %get-tuple-element.89), channel_id=1, source_target_pairs={{1,2},{2,1},{3,4},{4,3},{5,6},{6,5},{7,8},{8,7},{9,10},{10,9},{11,... | collective-permute-start | bytes 1572872 | tf_op jit(solution)/shard_map/ppermute | solution.py:612
  119.9 3.9 %collective-permute-start.11 = (f32[4,256,128]{2,1,0:T(8,128)S(1)}, f32[4,256,128]{2,1,0:T(8,128)S(1)}, u32[]{:S(2)}, u32[]{:S(2)}) collective-permute-start(f32[4,256,128]{2,1,0:T(8,128)S(1)} %get-tuple-element.84), channel_id=1, source_target_pairs={{1,2},{2,1},{3,4},{4,3},{5,6},{6,5},{7,8},{8,7},{9,10},{10,9},{11,... | collective-permute-start | bytes 1572872 | tf_op jit(solution)/shard_map/ppermute | solution.py:612
  123.8 13.4 %local_step3.1 = (f32[16,256,256]{2,1,0:T(8,128)}, f32[8,256,256]{2,1,0:T(8,128)S(1)}, f32[8,2,64,256]{3,2,1,0:T(8,128)S(1)}, f32[8,2,64,256]{3,2,1,0:T(8,128)S(1)}) custom-call(s32[3]{0:T(128)S(1)} %pad_add_fusion.scalar_ref, f32[16]{0:T(128)S(1)} %multiply_multiply_fusion.damp_x_ref, f32[16,256,256]{2,1,0:T(8,128)} %get-tuple-element.92.q_hbm, ...), custom_call_target="tpu_custom_call" | custom-call | flops 4000000000 | bytes 20971520 | tf_op jit(solution)/shard_map/local_step3/pallas_call | solution.py:392
  137.2 4.5 %collective-permute-done.11.odd_ref = f32[4,256,128]{2,1,0:T(8,128)S(1)} collective-permute-done((f32[4,256,128]{2,1,0:T(8,128)S(1)}, f32[4,256,128]{2,1,0:T(8,128)S(1)}, u32[]{:S(2)}, u32[]{:S(2)}) %collective-permute-start.11) | collective-permute-done | bytes 524320 | tf_op jit(solution)/shard_map/ppermute | solution.py:612
  141.7 3.6 %last_edge_step0.1 = (f32[16,256,256]{2,1,0:T(8,128)}, f32[8,2,64,128]{3,2,1,0:T(8,128)S(1)}, f32[8,2,64,128]{3,2,1,0:T(8,128)S(1)}) custom-call(s32[3]{0:T(128)S(1)} %pad_add_fusion.scalar_ref, f32[16]{0:T(128)S(1)} %multiply_multiply_fusion.damp_x_ref, f32[4,256,128]{2,1,0:T(8,128)S(1)} %collective-permute-done.10.even_ref, ...), custom_call_target="tpu_custom_call", output_to_operand_aliasing={{0}: (4, {})} | custom-call | flops 1 | tf_op jit(solution)/shard_map/last_edge_step0/pallas_call | solution.py:534
  146.0 2.1 %collective-permute-done.16.got_ref = f32[8,2,64,256]{3,2,1,0:T(8,128)S(1)} collective-permute-done((f32[8,2,64,256]{3,2,1,0:T(8,128)S(1)}, f32[8,2,64,256]{3,2,1,0:T(8,128)S(1)}, u32[]{:S(2)}, u32[]{:S(2)}) %collective-permute-start.16) | collective-permute-done | bytes 1048608 | tf_op jit(solution)/shard_map/ppermute | solution.py:649
  148.9 3.7 %last_edge_step1.1 = (f32[16,256,256]{2,1,0:T(8,128)}, f32[8,2,64,128]{3,2,1,0:T(8,128)S(1)}, f32[8,2,64,128]{3,2,1,0:T(8,128)S(1)}) custom-call(s32[3]{0:T(128)S(1)} %pad_add_fusion.scalar_ref, f32[16]{0:T(128)S(1)} %multiply_multiply_fusion.damp_x_ref, f32[4,256,128]{2,1,0:T(8,128)S(1)} %collective-permute-done.14.even_ref, ...), custom_call_target="tpu_custom_call", output_to_operand_aliasing={{0}: (4, {})} | custom-call | flops 1 | tf_op jit(solution)/shard_map/last_edge_step1/pallas_call | solution.py:534
  157.1 16.0 %collective-permute-done.19.first_a = f32[8,64,128]{2,1,0:T(8,128)S(1)} collective-permute-done((f32[8,64,128]{2,1,0:T(8,128)S(1)}, f32[8,64,128]{2,1,0:T(8,128)S(1)}, u32[]{:S(2)}, u32[]{:S(2)}) %collective-permute-start.19) | collective-permute-done | bytes 262176 | tf_op jit(solution)/shard_map/ppermute | solution.py:653
  173.2 5.1 %collective-permute-done.21.second_a = f32[8,64,128]{2,1,0:T(8,128)S(1)} collective-permute-done((f32[8,64,128]{2,1,0:T(8,128)S(1)}, f32[8,64,128]{2,1,0:T(8,128)S(1)}, u32[]{:S(2)}, u32[]{:S(2)}) %collective-permute-start.21) | collective-permute-done | bytes 262176 | tf_op jit(solution)/shard_map/ppermute | solution.py:653
  (53 shorter events, 21.5 us)
Async XLA Ops:
  5.0 26.6 %all-to-all-start = ((f32[32,8,128]{2,1,0:T(8,128)}), f32[32,8,128]{2,1,0:T(8,128)S(1)}, u32[]{:S(2)}, u32[]{:S(2)}) async-start(f32[32,8,128]{2,1,0:T(8,128)} %route.1), calls=%async_computation | async-start | bytes 262144 | tf_op jit(solution)/shard_map/all_to_all | solution.py:622
  19.5 34.6 %collective-permute-start = (f32[4,256,128]{2,1,0:T(8,128)}, f32[4,256,128]{2,1,0:T(8,128)S(1)}, u32[]{:S(2)}, u32[]{:S(2)}) collective-permute-start(f32[4,256,128]{2,1,0:T(8,128)} %get-tuple-element.59), channel_id=1, source_target_pairs={{0,1},{1,0},{2,3},{3,2},{4,5},{5,4},{6,7},{7,6},{8,9},{9,8},{10,11... | collective-permute-start | bytes 1572872 | tf_op jit(solution)/shard_map/ppermute | solution.py:612
  21.1 33.0 %collective-permute-start.1 = (f32[4,256,128]{2,1,0:T(8,128)}, f32[4,256,128]{2,1,0:T(8,128)S(1)}, u32[]{:S(2)}, u32[]{:S(2)}) collective-permute-start(f32[4,256,128]{2,1,0:T(8,128)} %get-tuple-element.60), channel_id=1, source_target_pairs={{1,2},{2,1},{3,4},{4,3},{5,6},{6,5},{7,8},{8,7},{9,10},{10,9},{11,... | collective-permute-start | bytes 1572872 | tf_op jit(solution)/shard_map/ppermute | solution.py:612
  27.4 35.3 %collective-permute-start.4 = (f32[4,256,128]{2,1,0:T(8,128)}, f32[4,256,128]{2,1,0:T(8,128)S(1)}, u32[]{:S(2)}, u32[]{:S(2)}) collective-permute-start(f32[4,256,128]{2,1,0:T(8,128)} %get-tuple-element.66), channel_id=1, source_target_pairs={{0,1},{1,0},{2,3},{3,2},{4,5},{5,4},{6,7},{7,6},{8,9},{9,8},{10,11... | collective-permute-start | bytes 1572872 | tf_op jit(solution)/shard_map/ppermute | solution.py:612
  27.5 35.2 %collective-permute-start.5 = (f32[4,256,128]{2,1,0:T(8,128)S(1)}, f32[4,256,128]{2,1,0:T(8,128)S(1)}, u32[]{:S(2)}, u32[]{:S(2)}) collective-permute-start(f32[4,256,128]{2,1,0:T(8,128)S(1)} %get-tuple-element.67), channel_id=1, source_target_pairs={{1,2},{2,1},{3,4},{4,3},{5,6},{6,5},{7,8},{8,7},{9,10},{10,9},{11,... | collective-permute-start | bytes 1572872 | tf_op jit(solution)/shard_map/ppermute | solution.py:612
  31.7 11.2 %copy-start = (bf16[256,256]{1,0:T(8,128)(2,1)S(1)}, bf16[256,256]{1,0:T(8,128)(2,1)}, u32[]{:S(2)}) copy-start(bf16[256,256]{1,0:T(8,128)(2,1)} %constant.59.clone.band_ref) | copy-start | bytes 393220
  56.0 23.6 %collective-permute-start.2 = (f32[4,256,128]{2,1,0:T(8,128)S(1)}, f32[4,256,128]{2,1,0:T(8,128)S(1)}, u32[]{:S(2)}, u32[]{:S(2)}) collective-permute-start(f32[4,256,128]{2,1,0:T(8,128)S(1)} %get-tuple-element.64), channel_id=1, source_target_pairs={{0,1},{1,0},{2,3},{3,2},{4,5},{5,4},{6,7},{7,6},{8,9},{9,8},{10,11... | collective-permute-start | bytes 1572872 | tf_op jit(solution)/shard_map/ppermute | solution.py:612
  56.1 23.5 %collective-permute-start.3 = (f32[4,256,128]{2,1,0:T(8,128)S(1)}, f32[4,256,128]{2,1,0:T(8,128)S(1)}, u32[]{:S(2)}, u32[]{:S(2)}) collective-permute-start(f32[4,256,128]{2,1,0:T(8,128)S(1)} %get-tuple-element.65), channel_id=1, source_target_pairs={{1,2},{2,1},{3,4},{4,3},{5,6},{6,5},{7,8},{8,7},{9,10},{10,9},{11,... | collective-permute-start | bytes 1572872 | tf_op jit(solution)/shard_map/ppermute | solution.py:612
  64.6 23.5 %collective-permute-start.8 = (f32[4,256,128]{2,1,0:T(8,128)S(1)}, f32[4,256,128]{2,1,0:T(8,128)S(1)}, u32[]{:S(2)}, u32[]{:S(2)}) collective-permute-start(f32[4,256,128]{2,1,0:T(8,128)S(1)} %get-tuple-element.76), channel_id=1, source_target_pairs={{0,1},{1,0},{2,3},{3,2},{4,5},{5,4},{6,7},{7,6},{8,9},{9,8},{10,11... | collective-permute-start | bytes 1572872 | tf_op jit(solution)/shard_map/ppermute | solution.py:612
  64.7 23.4 %collective-permute-start.9 = (f32[4,256,128]{2,1,0:T(8,128)S(1)}, f32[4,256,128]{2,1,0:T(8,128)S(1)}, u32[]{:S(2)}, u32[]{:S(2)}) collective-permute-start(f32[4,256,128]{2,1,0:T(8,128)S(1)} %get-tuple-element.77), channel_id=1, source_target_pairs={{1,2},{2,1},{3,4},{4,3},{5,6},{6,5},{7,8},{8,7},{9,10},{10,9},{11,... | collective-permute-start | bytes 1572872 | tf_op jit(solution)/shard_map/ppermute | solution.py:612
  81.6 25.8 %collective-permute-start.6 = (f32[4,256,128]{2,1,0:T(8,128)S(1)}, f32[4,256,128]{2,1,0:T(8,128)S(1)}, u32[]{:S(2)}, u32[]{:S(2)}) collective-permute-start(f32[4,256,128]{2,1,0:T(8,128)S(1)} %get-tuple-element.74), channel_id=1, source_target_pairs={{0,1},{1,0},{2,3},{3,2},{4,5},{5,4},{6,7},{7,6},{8,9},{9,8},{10,11... | collective-permute-start | bytes 1572872 | tf_op jit(solution)/shard_map/ppermute | solution.py:612
  81.7 25.7 %collective-permute-start.7 = (f32[4,256,128]{2,1,0:T(8,128)S(1)}, f32[4,256,128]{2,1,0:T(8,128)S(1)}, u32[]{:S(2)}, u32[]{:S(2)}) collective-permute-start(f32[4,256,128]{2,1,0:T(8,128)S(1)} %get-tuple-element.75), channel_id=1, source_target_pairs={{1,2},{2,1},{3,4},{4,3},{5,6},{6,5},{7,8},{8,7},{9,10},{10,9},{11,... | collective-permute-start | bytes 1572872 | tf_op jit(solution)/shard_map/ppermute | solution.py:612
  90.1 19.2 %collective-permute-start.12 = (f32[4,256,128]{2,1,0:T(8,128)S(1)}, f32[4,256,128]{2,1,0:T(8,128)S(1)}, u32[]{:S(2)}, u32[]{:S(2)}) collective-permute-start(f32[4,256,128]{2,1,0:T(8,128)S(1)} %get-tuple-element.85), channel_id=1, source_target_pairs={{0,1},{1,0},{2,3},{3,2},{4,5},{5,4},{6,7},{7,6},{8,9},{9,8},{10,11... | collective-permute-start | bytes 1572872 | tf_op jit(solution)/shard_map/ppermute | solution.py:612
  90.2 20.8 %collective-permute-start.13 = (f32[4,256,128]{2,1,0:T(8,128)S(1)}, f32[4,256,128]{2,1,0:T(8,128)S(1)}, u32[]{:S(2)}, u32[]{:S(2)}) collective-permute-start(f32[4,256,128]{2,1,0:T(8,128)S(1)} %get-tuple-element.86), channel_id=1, source_target_pairs={{1,2},{2,1},{3,4},{4,3},{5,6},{6,5},{7,8},{8,7},{9,10},{10,9},{11,... | collective-permute-start | bytes 1572872 | tf_op jit(solution)/shard_map/ppermute | solution.py:612
  112.9 24.3 %collective-permute-start.14 = (f32[4,256,128]{2,1,0:T(8,128)S(1)}, f32[4,256,128]{2,1,0:T(8,128)S(1)}, u32[]{:S(2)}, u32[]{:S(2)}) collective-permute-start(f32[4,256,128]{2,1,0:T(8,128)S(1)} %get-tuple-element.88), channel_id=1, source_target_pairs={{0,1},{1,0},{2,3},{3,2},{4,5},{5,4},{6,7},{7,6},{8,9},{9,8},{10,11... | collective-permute-start | bytes 1572872 | tf_op jit(solution)/shard_map/ppermute | solution.py:612
  113.0 24.2 %collective-permute-start.15 = (f32[4,256,128]{2,1,0:T(8,128)S(1)}, f32[4,256,128]{2,1,0:T(8,128)S(1)}, u32[]{:S(2)}, u32[]{:S(2)}) collective-permute-start(f32[4,256,128]{2,1,0:T(8,128)S(1)} %get-tuple-element.89), channel_id=1, source_target_pairs={{1,2},{2,1},{3,4},{4,3},{5,6},{6,5},{7,8},{8,7},{9,10},{10,9},{11,... | collective-permute-start | bytes 1572872 | tf_op jit(solution)/shard_map/ppermute | solution.py:612
  119.6 17.6 %collective-permute-start.10 = (f32[4,256,128]{2,1,0:T(8,128)S(1)}, f32[4,256,128]{2,1,0:T(8,128)S(1)}, u32[]{:S(2)}, u32[]{:S(2)}) collective-permute-start(f32[4,256,128]{2,1,0:T(8,128)S(1)} %get-tuple-element.83), channel_id=1, source_target_pairs={{0,1},{1,0},{2,3},{3,2},{4,5},{5,4},{6,7},{7,6},{8,9},{9,8},{10,11... | collective-permute-start | bytes 1572872 | tf_op jit(solution)/shard_map/ppermute | solution.py:612
  119.9 21.9 %collective-permute-start.11 = (f32[4,256,128]{2,1,0:T(8,128)S(1)}, f32[4,256,128]{2,1,0:T(8,128)S(1)}, u32[]{:S(2)}, u32[]{:S(2)}) collective-permute-start(f32[4,256,128]{2,1,0:T(8,128)S(1)} %get-tuple-element.84), channel_id=1, source_target_pairs={{1,2},{2,1},{3,4},{4,3},{5,6},{6,5},{7,8},{8,7},{9,10},{10,9},{11,... | collective-permute-start | bytes 1572872 | tf_op jit(solution)/shard_map/ppermute | solution.py:612
  145.4 2.7 %collective-permute-start.16 = (f32[8,2,64,256]{3,2,1,0:T(8,128)S(1)}, f32[8,2,64,256]{3,2,1,0:T(8,128)S(1)}, u32[]{:S(2)}, u32[]{:S(2)}) collective-permute-start(f32[8,2,64,256]{3,2,1,0:T(8,128)S(1)} %get-tuple-element.100), channel_id=1, source_target_pairs={{0,32},{32,0},{64,96},{96,64},{1,33},{33,1},{65,97},{97,65},{2,34}... | collective-permute-start | bytes 3145736 | tf_op jit(solution)/shard_map/ppermute | solution.py:649
  145.5 8.0 %collective-permute-start.18 = (f32[8,2,64,128]{3,2,1,0:T(8,128)S(1)}, f32[8,2,64,128]{3,2,1,0:T(8,128)S(1)}, u32[]{:S(2)}, u32[]{:S(2)}) collective-permute-start(f32[8,2,64,128]{3,2,1,0:T(8,128)S(1)} %get-tuple-element.108), channel_id=1, source_target_pairs={{0,32},{32,0},{64,96},{96,64},{1,33},{33,1},{65,97},{97,65},{2,34}... | collective-permute-start | bytes 1572872 | tf_op jit(solution)/shard_map/ppermute | solution.py:652
  152.6 3.1 %collective-permute-start.20 = (f32[8,2,64,128]{3,2,1,0:T(8,128)S(1)}, f32[8,2,64,128]{3,2,1,0:T(8,128)S(1)}, u32[]{:S(2)}, u32[]{:S(2)}) collective-permute-start(f32[8,2,64,128]{3,2,1,0:T(8,128)S(1)} %get-tuple-element.112), channel_id=1, source_target_pairs={{0,32},{32,0},{64,96},{96,64},{1,33},{33,1},{65,97},{97,65},{2,34}... | collective-permute-start | bytes 1572872 | tf_op jit(solution)/shard_map/ppermute | solution.py:652
  152.8 20.4 %collective-permute-start.17 = (f32[8,64,256]{2,1,0:T(8,128)S(1)}, f32[8,64,256]{2,1,0:T(8,128)S(1)}, u32[]{:S(2)}, u32[]{:S(2)}) collective-permute-start(f32[8,64,256]{2,1,0:T(8,128)S(1)} %get-tuple-element.106), channel_id=1, source_target_pairs={{0,64},{32,96},{64,0},{96,32},{1,65},{33,97},{65,1},{97,33},{2,66}... | collective-permute-start | bytes 1572872 | tf_op jit(solution)/shard_map/ppermute | solution.py:651
  154.2 19.0 %collective-permute-start.19 = (f32[8,64,128]{2,1,0:T(8,128)S(1)}, f32[8,64,128]{2,1,0:T(8,128)S(1)}, u32[]{:S(2)}, u32[]{:S(2)}) collective-permute-start(f32[8,64,128]{2,1,0:T(8,128)S(1)} %get-tuple-element.110), channel_id=1, source_target_pairs={{0,64},{32,96},{64,0},{96,32},{1,65},{33,97},{65,1},{97,33},{2,66}... | collective-permute-start | bytes 786440 | tf_op jit(solution)/shard_map/ppermute | solution.py:653
  156.4 21.8 %collective-permute-start.21 = (f32[8,64,128]{2,1,0:T(8,128)S(1)}, f32[8,64,128]{2,1,0:T(8,128)S(1)}, u32[]{:S(2)}, u32[]{:S(2)}) collective-permute-start(f32[8,64,128]{2,1,0:T(8,128)S(1)} %get-tuple-element.114), channel_id=1, source_target_pairs={{0,64},{32,96},{64,0},{96,32},{1,65},{33,97},{65,1},{97,33},{2,66}... | collective-permute-start | bytes 786440 | tf_op jit(solution)/shard_map/ppermute | solution.py:653
  (3 other events, 2.1 us)

commit v4 on v3

--- a/solution.py
+++ b/solution.py
@@ -58,7 +58,17 @@
     return m.astype(ml_dtypes.bfloat16)
 
 
-def route_body(slabs, target_ref, cell_ref, trace_ref, out_ref, pick):
+def route_body(slabs, target_hbm, cell_hbm, trace_hbm, out_ref, target_ref, cell_ref, trace_ref, pick, sems):
+    loads = [
+        pltpu.make_async_copy(source, here, sems.at[i])
+        for i, (source, here) in enumerate(
+            ((target_hbm, target_ref), (cell_hbm, cell_ref), (trace_hbm, trace_ref))
+        )
+    ]
+    for load in loads:
+        load.start()
+    for load in loads:
+        load.wait()
     listed = target_ref.shape[1]
     slots = slabs * CAP
     target = target_ref[...]
@@ -101,11 +111,19 @@
     return pl.pallas_call(
         functools.partial(route_body, slabs),
         out_shape=jax.ShapeDtypeStruct((slabs, 8, 128), f32),
-        scratch_shapes=[pltpu.VMEM((256, target.shape[1]), bf16)],
+        in_specs=[ANY] * 3,
+        out_specs=VMEM,
+        scratch_shapes=[
+            pltpu.VMEM(target.shape, jnp.int32),
+            pltpu.VMEM(cell.shape, jnp.int32),
+            pltpu.VMEM(trace.shape, f32),
+            pltpu.VMEM((256, target.shape[1]), bf16),
+            pltpu.SemaphoreType.DMA((3,)),
+        ],
         compiler_params=params(10, 0),
         cost_estimate=cost(1, 0),
         name="route",
-    )(target, cell, trace)
+    )(in_hbm(target), in_hbm(cell), in_hbm(trace))
 
 
 def inject_body(value_ref, dense, cells_vmem, cell_ref, sem):
@@ -181,11 +199,12 @@
     for i in range(4):
         half, group = divmod(i, 2)
         start = 12 * side_of(group, scalar_ref[0])
-        copies.append(
-            pltpu.make_async_copy(
-                source.at[pl.ds(start, 4), :, pl.ds(half * HALF, HALF)], refs[i], sems.at[i]
+        for layer in range(4):
+            copies.append(
+                pltpu.make_async_copy(
+                    source.at[start + layer, :, pl.ds(half * HALF, HALF)], refs[i].at[layer], sems.at[i, layer]
+                )
             )
-        )
     for copy in copies:
         copy.start()
     for copy in copies:
@@ -198,7 +217,7 @@
         out_shape=[pltpu.VMEM((4, SIZE, HALF), f32)] * 4,
         in_specs=[SMEM, ANY],
         out_specs=[VMEM] * 4,
-        scratch_shapes=[pltpu.SemaphoreType.DMA((4,))],
+        scratch_shapes=[pltpu.SemaphoreType.DMA((4, 4))],
         compiler_params=params(4, 0),
         cost_estimate=cost(1, 0),
         name="first_edges",
@@ -253,6 +272,10 @@
         return pltpu.make_async_copy(
             n_ref.at[planes(group)], n_hbm.at[planes(group)], store_sems.at[group]
         )
+
+    def store_rows(j):
+        at = (planes(groups - 1), pl.ds(pl.multiple_of(j * span, span), span))
+        return pltpu.make_async_copy(n_ref.at[at], n_hbm.at[at], store_sems.at[groups - 1 + j])
 
     def others(group):
         out = [load(1, group)]
@@ -347,9 +370,15 @@
                 def _():
                     send_ref[inner, j >> 1] = shared[...]
 
-        store(group).start()
-    for group in range(groups):
+            if group == groups - 1:
+                store_rows(j).start()
+
+        if group < groups - 1:
+            store(group).start()
+    for group in range(groups - 1):
         store(group).wait()
+    for j in range(group_size):
+        store_rows(j).wait()
 
 
 def local_step(step, scalars, damp_x, q, p, v, s, damp, accel, part=None):
@@ -367,7 +396,7 @@
         pltpu.VMEM(whole, f32),
         pltpu.VMEM(whole, f32),
         pltpu.SemaphoreType.DMA((3, 4)),
-        pltpu.SemaphoreType.DMA((4,)),
+        pltpu.SemaphoreType.DMA((7,)),
     ]
     if step >= 2:
         in_specs.append(ANY)

time: 180 us -> 179 us (level); the launches traced: 180 us -> 177 us
  local copies, waits for them, and re-layouts: 2.09 us -> 0.01 us
    unnamed x8 -> x2, local copies, waits for them, and re-layouts: 2.09 us -> 0.01 us
where the time goes in v4:
time: 179 us; the launch traced here: 177 us
  Pallas kernels  86.2 us (48%)
  starting transfers between devices  60 us (34%)
  waiting for transfers between devices  29.4 us (16%)
    pallas_call x4, Pallas kernels, local_step(): pl.pallas_call(functools.partial(local_body, step), out_shape=out_shape,...  47.2 us
    ppermute x8, starting transfers between devices, exchange(): lax.ppermute(odd, 'sub', pairs_odd)  41.2 us
    ppermute x2, waiting for transfers between devices, shards(): outs.append((lax.ppermute(send, 'shot', swap_row), edge_keep))  21.1 us
    pallas_call x6, Pallas kernels, edge_step(): pl.pallas_call(functools.partial(edge_body, half), out_shape=[pltpu.HBM((...  11.4 us
    all_to_all x1, starting transfers between devices, shards(): got = lax.all_to_all(sent, 'sub', split_axis=0, concat_axis=0, tiled=True)  11.1 us
    pallas_call x1, Pallas kernels, inject(): pl.pallas_call(inject_body, out_shape=pltpu.VMEM((SLAB * SIZE * 8, 128),...  9.85 us
    pallas_call x2, Pallas kernels, last_edge_step(): pl.pallas_call(functools.partial(last_edge_body, half), out_shape=[pltpu....  7.29 us
    ppermute x8, waiting for transfers between devices, exchange(): lax.ppermute(odd, 'sub', pairs_odd)  6.13 us
  transfers between devices with their start and end apart: 23, of which 5 were waited for; matrix products, arithmetic and copies ran while one was open for 0% of the time, Pallas kernels for 43%

profile of v4, /device:TPU:2, one launch (start us, length us, event | category | flops | bytes accessed | tf_op | source)
XLA Modules:
  0.0 176.8 jit_solution(10705975333852164531)
XLA Ops:
  0.6 3.1 %route.1 = f32[32,8,128]{2,1,0:T(8,128)} custom-call(s32[1,1024]{1,0:T(1,128)} %bitcast.14, s32[1,1024]{1,0:T(1,128)} %cell_hbm.1, f32[4,1024]{1,0:T(4,128)} %bitcast.13), custom_call_target="tpu_custom_call" | custom-call | flops 1 | tf_op jit(solution)/shard_map/route/pallas_call | solution.py:111
  3.7 11.1 %all-to-all-start = ((f32[32,8,128]{2,1,0:T(8,128)}), f32[32,8,128]{2,1,0:T(8,128)S(1)}, u32[]{:S(2)}, u32[]{:S(2)}) async-start(f32[32,8,128]{2,1,0:T(8,128)} %route.1), calls=%async_computation | async-start | bytes 262144 | tf_op jit(solution)/shard_map/all_to_all | solution.py:651
  14.9 3.4 %first_edges.1 = (f32[4,256,128]{2,1,0:T(8,128)}, f32[4,256,128]{2,1,0:T(8,128)}, f32[4,256,128]{2,1,0:T(8,128)}, f32[4,256,128]{2,1,0:T(8,128)S(1)}) custom-call(s32[3]{0:T(128)S(1)} %pad_add_fusion.scalar_ref, f32[16,256,256]{2,1,0:T(8,128)} %bitcast.8), custom_call_target="tpu_custom_call" | custom-call | flops 1 | tf_op jit(solution)/shard_map/first_edges/pallas_call | solution.py:215
  19.9 6.4 %collective-permute-start.1 = (f32[4,256,128]{2,1,0:T(8,128)}, f32[4,256,128]{2,1,0:T(8,128)S(1)}, u32[]{:S(2)}, u32[]{:S(2)}) collective-permute-start(f32[4,256,128]{2,1,0:T(8,128)} %get-tuple-element.60), channel_id=1, source_target_pairs={{1,2},{2,1},{3,4},{4,3},{5,6},{6,5},{7,8},{8,7},{9,10},{10,9},{11,... | collective-permute-start | bytes 1572872 | tf_op jit(solution)/shard_map/ppermute | solution.py:641
  26.4 4.0 %collective-permute-start.5 = (f32[4,256,128]{2,1,0:T(8,128)S(1)}, f32[4,256,128]{2,1,0:T(8,128)S(1)}, u32[]{:S(2)}, u32[]{:S(2)}) collective-permute-start(f32[4,256,128]{2,1,0:T(8,128)S(1)} %get-tuple-element.67), channel_id=1, source_target_pairs={{1,2},{2,1},{3,4},{4,3},{5,6},{6,5},{7,8},{8,7},{9,10},{10,9},{11,... | collective-permute-start | bytes 1572872 | tf_op jit(solution)/shard_map/ppermute | solution.py:641
  30.6 9.8 %inject.1.s_ref = f32[32768,128]{1,0:T(8,128)S(1)} custom-call(f32[32,8,128]{2,1,0:T(8,128)S(1)} %all-to-all-done.value_ref), custom_call_target="tpu_custom_call" | custom-call | flops 1 | tf_op jit(solution)/shard_map/inject/pallas_call | solution.py:176
  40.4 11.0 %local_step0.1 = (f32[16,256,256]{2,1,0:T(8,128)}, f32[8,256,256]{2,1,0:T(8,128)S(1)}, f32[8,256,256]{2,1,0:T(8,128)S(1)}, f32[16,256,256]{2,1,0:T(8,128)S(1)}) custom-call(s32[3]{0:T(128)S(1)} %pad_add_fusion.scalar_ref, f32[16]{0:T(128)S(1)} %multiply_multiply_fusion.damp_x_ref, f32[16,256,256]{2,1,0:T(8,128)} %bitcast.9, f32[16,256,256]{2,1,0:T(8,128)} %bitcast.12, ...), custom_call_target="tpu_custom_call" | custom-call | flops 4000000000 | bytes 20971520 | tf_op jit(solution)/shard_map/local_step0/pallas_call | solution.py:421
  54.9 5.0 %collective-permute-start.3 = (f32[4,256,128]{2,1,0:T(8,128)S(1)}, f32[4,256,128]{2,1,0:T(8,128)S(1)}, u32[]{:S(2)}, u32[]{:S(2)}) collective-permute-start(f32[4,256,128]{2,1,0:T(8,128)S(1)} %get-tuple-element.65), channel_id=1, source_target_pairs={{1,2},{2,1},{3,4},{4,3},{5,6},{6,5},{7,8},{8,7},{9,10},{10,9},{11,... | collective-permute-start | bytes 1572872 | tf_op jit(solution)/shard_map/ppermute | solution.py:641
  61.9 5.3 %collective-permute-start.9 = (f32[4,256,128]{2,1,0:T(8,128)S(1)}, f32[4,256,128]{2,1,0:T(8,128)S(1)}, u32[]{:S(2)}, u32[]{:S(2)}) collective-permute-start(f32[4,256,128]{2,1,0:T(8,128)S(1)} %get-tuple-element.77), channel_id=1, source_target_pairs={{1,2},{2,1},{3,4},{4,3},{5,6},{6,5},{7,8},{8,7},{9,10},{10,9},{11,... | collective-permute-start | bytes 1572872 | tf_op jit(solution)/shard_map/ppermute | solution.py:641
  67.2 10.8 %local_step1.1 = (f32[16,256,256]{2,1,0:T(8,128)}, f32[8,256,256]{2,1,0:T(8,128)S(1)}, f32[8,256,256]{2,1,0:T(8,128)S(1)}) custom-call(s32[3]{0:T(128)S(1)} %pad_add_fusion.scalar_ref, f32[16]{0:T(128)S(1)} %multiply_multiply_fusion.damp_x_ref, f32[16,256,256]{2,1,0:T(8,128)} %get-tuple-element.69.q_hbm.p_hbm, f32[16,256,256]{2,1,0:T(8,128)} %bitcast.10, ...), custom_call_target="tpu_custom_call" | custom-call | flops 4000000000 | bytes 20971520 | tf_op jit(solution)/shard_map/local_step1/pallas_call | solution.py:421
  78.0 1.9 %edge_step0.4 = (f32[16,256,256]{2,1,0:T(8,128)}, f32[4,256,128]{2,1,0:T(8,128)S(1)}, f32[4,256,128]{2,1,0:T(8,128)S(1)}) custom-call(s32[3]{0:T(128)S(1)} %pad_add_fusion.scalar_ref, f32[4,256,128]{2,1,0:T(8,128)S(1)} %collective-permute-done.2.even_ref, f32[4,256,128]{2,1,0:T(8,128)S(1)} %collective-permute-done.3.odd_ref, ...), custom_call_target="tpu_custom_call", output_to_operand_aliasing={{0}: (5, {})} | custom-call | flops 1 | tf_op jit(solution)/shard_map/edge_step0/pallas_call | solution.py:478
  80.0 5.0 %collective-permute-start.7 = (f32[4,256,128]{2,1,0:T(8,128)S(1)}, f32[4,256,128]{2,1,0:T(8,128)S(1)}, u32[]{:S(2)}, u32[]{:S(2)}) collective-permute-start(f32[4,256,128]{2,1,0:T(8,128)S(1)} %get-tuple-element.75), channel_id=1, source_target_pairs={{1,2},{2,1},{3,4},{4,3},{5,6},{6,5},{7,8},{8,7},{9,10},{10,9},{11,... | collective-permute-start | bytes 1572872 | tf_op jit(solution)/shard_map/ppermute | solution.py:641
  87.4 5.1 %collective-permute-start.13 = (f32[4,256,128]{2,1,0:T(8,128)S(1)}, f32[4,256,128]{2,1,0:T(8,128)S(1)}, u32[]{:S(2)}, u32[]{:S(2)}) collective-permute-start(f32[4,256,128]{2,1,0:T(8,128)S(1)} %get-tuple-element.86), channel_id=1, source_target_pairs={{1,2},{2,1},{3,4},{4,3},{5,6},{6,5},{7,8},{8,7},{9,10},{10,9},{11,... | collective-permute-start | bytes 1572872 | tf_op jit(solution)/shard_map/ppermute | solution.py:641
  92.5 12.3 %local_step2.1 = (f32[16,256,256]{2,1,0:T(8,128)}, f32[8,256,256]{2,1,0:T(8,128)S(1)}, f32[8,256,256]{2,1,0:T(8,128)S(1)}, f32[16,256,256]{2,1,0:T(8,128)S(1)}) custom-call(s32[3]{0:T(128)S(1)} %pad_add_fusion.scalar_ref, f32[16]{0:T(128)S(1)} %multiply_multiply_fusion.damp_x_ref, f32[16,256,256]{2,1,0:T(8,128)} %get-tuple-element.79.q_hbm.p_hbm, ...), custom_call_target="tpu_custom_call" | custom-call | flops 4000000000 | bytes 20971520 | tf_op jit(solution)/shard_map/local_step2/pallas_call | solution.py:421
  106.7 2.1 %collective-permute-done.13.odd_ref = f32[4,256,128]{2,1,0:T(8,128)S(1)} collective-permute-done((f32[4,256,128]{2,1,0:T(8,128)S(1)}, f32[4,256,128]{2,1,0:T(8,128)S(1)}, u32[]{:S(2)}, u32[]{:S(2)}) %collective-permute-start.13) | collective-permute-done | bytes 524320 | tf_op jit(solution)/shard_map/ppermute | solution.py:641
  110.8 5.6 %collective-permute-start.15 = (f32[4,256,128]{2,1,0:T(8,128)S(1)}, f32[4,256,128]{2,1,0:T(8,128)S(1)}, u32[]{:S(2)}, u32[]{:S(2)}) collective-permute-start(f32[4,256,128]{2,1,0:T(8,128)S(1)} %get-tuple-element.89), channel_id=1, source_target_pairs={{1,2},{2,1},{3,4},{4,3},{5,6},{6,5},{7,8},{8,7},{9,10},{10,9},{11,... | collective-permute-start | bytes 1572872 | tf_op jit(solution)/shard_map/ppermute | solution.py:641
  116.7 4.7 %collective-permute-start.11 = (f32[4,256,128]{2,1,0:T(8,128)S(1)}, f32[4,256,128]{2,1,0:T(8,128)S(1)}, u32[]{:S(2)}, u32[]{:S(2)}) collective-permute-start(f32[4,256,128]{2,1,0:T(8,128)S(1)} %get-tuple-element.84), channel_id=1, source_target_pairs={{1,2},{2,1},{3,4},{4,3},{5,6},{6,5},{7,8},{8,7},{9,10},{10,9},{11,... | collective-permute-start | bytes 1572872 | tf_op jit(solution)/shard_map/ppermute | solution.py:641
  121.5 13.2 %local_step3.1 = (f32[16,256,256]{2,1,0:T(8,128)}, f32[8,256,256]{2,1,0:T(8,128)S(1)}, f32[8,2,64,256]{3,2,1,0:T(8,128)S(1)}, f32[8,2,64,256]{3,2,1,0:T(8,128)S(1)}) custom-call(s32[3]{0:T(128)S(1)} %pad_add_fusion.scalar_ref, f32[16]{0:T(128)S(1)} %multiply_multiply_fusion.damp_x_ref, f32[16,256,256]{2,1,0:T(8,128)} %get-tuple-element.92.q_hbm, ...), custom_call_target="tpu_custom_call" | custom-call | flops 4000000000 | bytes 20971520 | tf_op jit(solution)/shard_map/local_step3/pallas_call | solution.py:421
  134.7 4.0 %collective-permute-done.11.odd_ref = f32[4,256,128]{2,1,0:T(8,128)S(1)} collective-permute-done((f32[4,256,128]{2,1,0:T(8,128)S(1)}, f32[4,256,128]{2,1,0:T(8,128)S(1)}, u32[]{:S(2)}, u32[]{:S(2)}) %collective-permute-start.11) | collective-permute-done | bytes 524320 | tf_op jit(solution)/shard_map/ppermute | solution.py:641
  138.7 3.6 %last_edge_step0.1 = (f32[16,256,256]{2,1,0:T(8,128)}, f32[8,2,64,128]{3,2,1,0:T(8,128)S(1)}, f32[8,2,64,128]{3,2,1,0:T(8,128)S(1)}) custom-call(s32[3]{0:T(128)S(1)} %pad_add_fusion.scalar_ref, f32[16]{0:T(128)S(1)} %multiply_multiply_fusion.damp_x_ref, f32[4,256,128]{2,1,0:T(8,128)S(1)} %collective-permute-done.10.even_ref, ...), custom_call_target="tpu_custom_call", output_to_operand_aliasing={{0}: (4, {})} | custom-call | flops 1 | tf_op jit(solution)/shard_map/last_edge_step0/pallas_call | solution.py:563
  142.9 2.1 %collective-permute-done.16.got_ref = f32[8,2,64,256]{3,2,1,0:T(8,128)S(1)} collective-permute-done((f32[8,2,64,256]{3,2,1,0:T(8,128)S(1)}, f32[8,2,64,256]{3,2,1,0:T(8,128)S(1)}, u32[]{:S(2)}, u32[]{:S(2)}) %collective-permute-start.16) | collective-permute-done | bytes 1048608 | tf_op jit(solution)/shard_map/ppermute | solution.py:678
  145.9 3.7 %last_edge_step1.1 = (f32[16,256,256]{2,1,0:T(8,128)}, f32[8,2,64,128]{3,2,1,0:T(8,128)S(1)}, f32[8,2,64,128]{3,2,1,0:T(8,128)S(1)}) custom-call(s32[3]{0:T(128)S(1)} %pad_add_fusion.scalar_ref, f32[16]{0:T(128)S(1)} %multiply_multiply_fusion.damp_x_ref, f32[4,256,128]{2,1,0:T(8,128)S(1)} %collective-permute-done.14.even_ref, ...), custom_call_target="tpu_custom_call", output_to_operand_aliasing={{0}: (4, {})} | custom-call | flops 1 | tf_op jit(solution)/shard_map/last_edge_step1/pallas_call | solution.py:563
  154.1 16.1 %collective-permute-done.19.first_a = f32[8,64,128]{2,1,0:T(8,128)S(1)} collective-permute-done((f32[8,64,128]{2,1,0:T(8,128)S(1)}, f32[8,64,128]{2,1,0:T(8,128)S(1)}, u32[]{:S(2)}, u32[]{:S(2)}) %collective-permute-start.19) | collective-permute-done | bytes 262176 | tf_op jit(solution)/shard_map/ppermute | solution.py:682
  170.1 5.1 %collective-permute-done.21.second_a = f32[8,64,128]{2,1,0:T(8,128)S(1)} collective-permute-done((f32[8,64,128]{2,1,0:T(8,128)S(1)}, f32[8,64,128]{2,1,0:T(8,128)S(1)}, u32[]{:S(2)}, u32[]{:S(2)}) %collective-permute-start.21) | collective-permute-done | bytes 262176 | tf_op jit(solution)/shard_map/ppermute | solution.py:682
  (47 shorter events, 21.4 us)
Async XLA Ops:
  3.7 26.8 %all-to-all-start = ((f32[32,8,128]{2,1,0:T(8,128)}), f32[32,8,128]{2,1,0:T(8,128)S(1)}, u32[]{:S(2)}, u32[]{:S(2)}) async-start(f32[32,8,128]{2,1,0:T(8,128)} %route.1), calls=%async_computation | async-start | bytes 262144 | tf_op jit(solution)/shard_map/all_to_all | solution.py:651
  18.4 33.0 %collective-permute-start = (f32[4,256,128]{2,1,0:T(8,128)}, f32[4,256,128]{2,1,0:T(8,128)S(1)}, u32[]{:S(2)}, u32[]{:S(2)}) collective-permute-start(f32[4,256,128]{2,1,0:T(8,128)} %get-tuple-element.59), channel_id=1, source_target_pairs={{0,1},{1,0},{2,3},{3,2},{4,5},{5,4},{6,7},{7,6},{8,9},{9,8},{10,11... | collective-permute-start | bytes 1572872 | tf_op jit(solution)/shard_map/ppermute | solution.py:641
  19.9 31.5 %collective-permute-start.1 = (f32[4,256,128]{2,1,0:T(8,128)}, f32[4,256,128]{2,1,0:T(8,128)S(1)}, u32[]{:S(2)}, u32[]{:S(2)}) collective-permute-start(f32[4,256,128]{2,1,0:T(8,128)} %get-tuple-element.60), channel_id=1, source_target_pairs={{1,2},{2,1},{3,4},{4,3},{5,6},{6,5},{7,8},{8,7},{9,10},{10,9},{11,... | collective-permute-start | bytes 1572872 | tf_op jit(solution)/shard_map/ppermute | solution.py:641
  26.3 33.6 %collective-permute-start.4 = (f32[4,256,128]{2,1,0:T(8,128)}, f32[4,256,128]{2,1,0:T(8,128)S(1)}, u32[]{:S(2)}, u32[]{:S(2)}) collective-permute-start(f32[4,256,128]{2,1,0:T(8,128)} %get-tuple-element.66), channel_id=1, source_target_pairs={{0,1},{1,0},{2,3},{3,2},{4,5},{5,4},{6,7},{7,6},{8,9},{9,8},{10,11... | collective-permute-start | bytes 1572872 | tf_op jit(solution)/shard_map/ppermute | solution.py:641
  26.4 33.5 %collective-permute-start.5 = (f32[4,256,128]{2,1,0:T(8,128)S(1)}, f32[4,256,128]{2,1,0:T(8,128)S(1)}, u32[]{:S(2)}, u32[]{:S(2)}) collective-permute-start(f32[4,256,128]{2,1,0:T(8,128)S(1)} %get-tuple-element.67), channel_id=1, source_target_pairs={{1,2},{2,1},{3,4},{4,3},{5,6},{6,5},{7,8},{8,7},{9,10},{10,9},{11,... | collective-permute-start | bytes 1572872 | tf_op jit(solution)/shard_map/ppermute | solution.py:641
  30.5 9.9 %copy-start = (bf16[256,256]{1,0:T(8,128)(2,1)S(1)}, bf16[256,256]{1,0:T(8,128)(2,1)}, u32[]{:S(2)}) copy-start(bf16[256,256]{1,0:T(8,128)(2,1)} %constant.59.clone.band_ref) | copy-start | bytes 393220
  53.3 24.7 %collective-permute-start.2 = (f32[4,256,128]{2,1,0:T(8,128)S(1)}, f32[4,256,128]{2,1,0:T(8,128)S(1)}, u32[]{:S(2)}, u32[]{:S(2)}) collective-permute-start(f32[4,256,128]{2,1,0:T(8,128)S(1)} %get-tuple-element.64), channel_id=1, source_target_pairs={{0,1},{1,0},{2,3},{3,2},{4,5},{5,4},{6,7},{7,6},{8,9},{9,8},{10,11... | collective-permute-start | bytes 1572872 | tf_op jit(solution)/shard_map/ppermute | solution.py:641
  54.9 23.2 %collective-permute-start.3 = (f32[4,256,128]{2,1,0:T(8,128)S(1)}, f32[4,256,128]{2,1,0:T(8,128)S(1)}, u32[]{:S(2)}, u32[]{:S(2)}) collective-permute-start(f32[4,256,128]{2,1,0:T(8,128)S(1)} %get-tuple-element.65), channel_id=1, source_target_pairs={{1,2},{2,1},{3,4},{4,3},{5,6},{6,5},{7,8},{8,7},{9,10},{10,9},{11,... | collective-permute-start | bytes 1572872 | tf_op jit(solution)/shard_map/ppermute | solution.py:641
  61.8 23.3 %collective-permute-start.8 = (f32[4,256,128]{2,1,0:T(8,128)S(1)}, f32[4,256,128]{2,1,0:T(8,128)S(1)}, u32[]{:S(2)}, u32[]{:S(2)}) collective-permute-start(f32[4,256,128]{2,1,0:T(8,128)S(1)} %get-tuple-element.76), channel_id=1, source_target_pairs={{0,1},{1,0},{2,3},{3,2},{4,5},{5,4},{6,7},{7,6},{8,9},{9,8},{10,11... | collective-permute-start | bytes 1572872 | tf_op jit(solution)/shard_map/ppermute | solution.py:641
  61.9 23.2 %collective-permute-start.9 = (f32[4,256,128]{2,1,0:T(8,128)S(1)}, f32[4,256,128]{2,1,0:T(8,128)S(1)}, u32[]{:S(2)}, u32[]{:S(2)}) collective-permute-start(f32[4,256,128]{2,1,0:T(8,128)S(1)} %get-tuple-element.77), channel_id=1, source_target_pairs={{1,2},{2,1},{3,4},{4,3},{5,6},{6,5},{7,8},{8,7},{9,10},{10,9},{11,... | collective-permute-start | bytes 1572872 | tf_op jit(solution)/shard_map/ppermute | solution.py:641
  79.9 24.8 %collective-permute-start.6 = (f32[4,256,128]{2,1,0:T(8,128)S(1)}, f32[4,256,128]{2,1,0:T(8,128)S(1)}, u32[]{:S(2)}, u32[]{:S(2)}) collective-permute-start(f32[4,256,128]{2,1,0:T(8,128)S(1)} %get-tuple-element.74), channel_id=1, source_target_pairs={{0,1},{1,0},{2,3},{3,2},{4,5},{5,4},{6,7},{7,6},{8,9},{9,8},{10,11... | collective-permute-start | bytes 1572872 | tf_op jit(solution)/shard_map/ppermute | solution.py:641
  80.0 24.7 %collective-permute-start.7 = (f32[4,256,128]{2,1,0:T(8,128)S(1)}, f32[4,256,128]{2,1,0:T(8,128)S(1)}, u32[]{:S(2)}, u32[]{:S(2)}) collective-permute-start(f32[4,256,128]{2,1,0:T(8,128)S(1)} %get-tuple-element.75), channel_id=1, source_target_pairs={{1,2},{2,1},{3,4},{4,3},{5,6},{6,5},{7,8},{8,7},{9,10},{10,9},{11,... | collective-permute-start | bytes 1572872 | tf_op jit(solution)/shard_map/ppermute | solution.py:641
  87.0 19.7 %collective-permute-start.12 = (f32[4,256,128]{2,1,0:T(8,128)S(1)}, f32[4,256,128]{2,1,0:T(8,128)S(1)}, u32[]{:S(2)}, u32[]{:S(2)}) collective-permute-start(f32[4,256,128]{2,1,0:T(8,128)S(1)} %get-tuple-element.85), channel_id=1, source_target_pairs={{0,1},{1,0},{2,3},{3,2},{4,5},{5,4},{6,7},{7,6},{8,9},{9,8},{10,11... | collective-permute-start | bytes 1572872 | tf_op jit(solution)/shard_map/ppermute | solution.py:641
  87.4 21.5 %collective-permute-start.13 = (f32[4,256,128]{2,1,0:T(8,128)S(1)}, f32[4,256,128]{2,1,0:T(8,128)S(1)}, u32[]{:S(2)}, u32[]{:S(2)}) collective-permute-start(f32[4,256,128]{2,1,0:T(8,128)S(1)} %get-tuple-element.86), channel_id=1, source_target_pairs={{1,2},{2,1},{3,4},{4,3},{5,6},{6,5},{7,8},{8,7},{9,10},{10,9},{11,... | collective-permute-start | bytes 1572872 | tf_op jit(solution)/shard_map/ppermute | solution.py:641
  110.7 23.9 %collective-permute-start.14 = (f32[4,256,128]{2,1,0:T(8,128)S(1)}, f32[4,256,128]{2,1,0:T(8,128)S(1)}, u32[]{:S(2)}, u32[]{:S(2)}) collective-permute-start(f32[4,256,128]{2,1,0:T(8,128)S(1)} %get-tuple-element.88), channel_id=1, source_target_pairs={{0,1},{1,0},{2,3},{3,2},{4,5},{5,4},{6,7},{7,6},{8,9},{9,8},{10,11... | collective-permute-start | bytes 1572872 | tf_op jit(solution)/shard_map/ppermute | solution.py:641
  110.8 23.8 %collective-permute-start.15 = (f32[4,256,128]{2,1,0:T(8,128)S(1)}, f32[4,256,128]{2,1,0:T(8,128)S(1)}, u32[]{:S(2)}, u32[]{:S(2)}) collective-permute-start(f32[4,256,128]{2,1,0:T(8,128)S(1)} %get-tuple-element.89), channel_id=1, source_target_pairs={{1,2},{2,1},{3,4},{4,3},{5,6},{6,5},{7,8},{8,7},{9,10},{10,9},{11,... | collective-permute-start | bytes 1572872 | tf_op jit(solution)/shard_map/ppermute | solution.py:641
  116.5 18.2 %collective-permute-start.10 = (f32[4,256,128]{2,1,0:T(8,128)S(1)}, f32[4,256,128]{2,1,0:T(8,128)S(1)}, u32[]{:S(2)}, u32[]{:S(2)}) collective-permute-start(f32[4,256,128]{2,1,0:T(8,128)S(1)} %get-tuple-element.83), channel_id=1, source_target_pairs={{0,1},{1,0},{2,3},{3,2},{4,5},{5,4},{6,7},{7,6},{8,9},{9,8},{10,11... | collective-permute-start | bytes 1572872 | tf_op jit(solution)/shard_map/ppermute | solution.py:641
  116.7 21.9 %collective-permute-start.11 = (f32[4,256,128]{2,1,0:T(8,128)S(1)}, f32[4,256,128]{2,1,0:T(8,128)S(1)}, u32[]{:S(2)}, u32[]{:S(2)}) collective-permute-start(f32[4,256,128]{2,1,0:T(8,128)S(1)} %get-tuple-element.84), channel_id=1, source_target_pairs={{1,2},{2,1},{3,4},{4,3},{5,6},{6,5},{7,8},{8,7},{9,10},{10,9},{11,... | collective-permute-start | bytes 1572872 | tf_op jit(solution)/shard_map/ppermute | solution.py:641
  142.3 2.7 %collective-permute-start.16 = (f32[8,2,64,256]{3,2,1,0:T(8,128)S(1)}, f32[8,2,64,256]{3,2,1,0:T(8,128)S(1)}, u32[]{:S(2)}, u32[]{:S(2)}) collective-permute-start(f32[8,2,64,256]{3,2,1,0:T(8,128)S(1)} %get-tuple-element.100), channel_id=1, source_target_pairs={{0,32},{32,0},{64,96},{96,64},{1,33},{33,1},{65,97},{97,65},{2,34}... | collective-permute-start | bytes 3145736 | tf_op jit(solution)/shard_map/ppermute | solution.py:678
  142.4 8.0 %collective-permute-start.18 = (f32[8,2,64,128]{3,2,1,0:T(8,128)S(1)}, f32[8,2,64,128]{3,2,1,0:T(8,128)S(1)}, u32[]{:S(2)}, u32[]{:S(2)}) collective-permute-start(f32[8,2,64,128]{3,2,1,0:T(8,128)S(1)} %get-tuple-element.108), channel_id=1, source_target_pairs={{0,32},{32,0},{64,96},{96,64},{1,33},{33,1},{65,97},{97,65},{2,34}... | collective-permute-start | bytes 1572872 | tf_op jit(solution)/shard_map/ppermute | solution.py:681
  149.5 3.1 %collective-permute-start.20 = (f32[8,2,64,128]{3,2,1,0:T(8,128)S(1)}, f32[8,2,64,128]{3,2,1,0:T(8,128)S(1)}, u32[]{:S(2)}, u32[]{:S(2)}) collective-permute-start(f32[8,2,64,128]{3,2,1,0:T(8,128)S(1)} %get-tuple-element.112), channel_id=1, source_target_pairs={{0,32},{32,0},{64,96},{96,64},{1,33},{33,1},{65,97},{97,65},{2,34}... | collective-permute-start | bytes 1572872 | tf_op jit(solution)/shard_map/ppermute | solution.py:681
  149.7 20.4 %collective-permute-start.17 = (f32[8,64,256]{2,1,0:T(8,128)S(1)}, f32[8,64,256]{2,1,0:T(8,128)S(1)}, u32[]{:S(2)}, u32[]{:S(2)}) collective-permute-start(f32[8,64,256]{2,1,0:T(8,128)S(1)} %get-tuple-element.106), channel_id=1, source_target_pairs={{0,64},{32,96},{64,0},{96,32},{1,65},{33,97},{65,1},{97,33},{2,66}... | collective-permute-start | bytes 1572872 | tf_op jit(solution)/shard_map/ppermute | solution.py:680
  151.1 19.0 %collective-permute-start.19 = (f32[8,64,128]{2,1,0:T(8,128)S(1)}, f32[8,64,128]{2,1,0:T(8,128)S(1)}, u32[]{:S(2)}, u32[]{:S(2)}) collective-permute-start(f32[8,64,128]{2,1,0:T(8,128)S(1)} %get-tuple-element.110), channel_id=1, source_target_pairs={{0,64},{32,96},{64,0},{96,32},{1,65},{33,97},{65,1},{97,33},{2,66}... | collective-permute-start | bytes 786440 | tf_op jit(solution)/shard_map/ppermute | solution.py:682
  153.4 21.8 %collective-permute-start.21 = (f32[8,64,128]{2,1,0:T(8,128)S(1)}, f32[8,64,128]{2,1,0:T(8,128)S(1)}, u32[]{:S(2)}, u32[]{:S(2)}) collective-permute-start(f32[8,64,128]{2,1,0:T(8,128)S(1)} %get-tuple-element.114), channel_id=1, source_target_pairs={{0,64},{32,96},{64,0},{96,32},{1,65},{33,97},{65,1},{97,33},{2,66}... | collective-permute-start | bytes 786440 | tf_op jit(solution)/shard_map/ppermute | solution.py:682
